TPU v7x, 32 devices: a whole 2x2x4 slice. The times are simulated.
32 devices in a mesh: blk: 2 (over x), tp: 4 (over y, core), enc: 4 (over z).
Axes of the slice: x: 2, y: 2, z: 4, core: 2. Of those that a mesh axis runs over, the one named last changes fastest.
Arguments:
- self_query_columns: bfloat16 [1024, 4096], P('blk', ('tp', 'enc')), may hold values from -12 to 12
- text_key_value: bfloat16 [1024, 2, 512], P('blk', None, 'tp'), may hold values from -9 to 9
- cross_query_columns: bfloat16 [1024, 4096], P('blk', ('tp', 'enc')), may hold values from -12 to 12
- image_kv: bfloat16 [2, 2, 6404, 512], P('blk', None, 'enc', 'tp'), may hold values from -9 to 9
- block_images: int32 [8, 2], P('blk'), may hold values from 0 to 1, as said below
- image_owner: int32 [2], replicated, may hold values from 0 to 1, each once
Outputs:
- self_out: bfloat16 [1024, 4096], P('blk', ('tp', 'enc'))
- cross_out: bfloat16 [1024, 4096], P('blk', ('tp', 'enc'))
Inputs may be any that keep to these rules, and one draw needn't show every extreme that they name: `block_images`: each block of 128 text tokens sees one or two images: the image most recently placed before it and, in some blocks, the image placed before that one. Image ids rise along the text, every image is seen by some block, and some block sees two. A permutation: image i's keys and values are slot image_owner[i] of image_kv.
All inputs are finite; a program needn't handle non-finite values.
Results may differ from a plain program's by a relative error of at most 0.007.
Values may be sent and summed in bfloat16 or wider, within the bound.
No kernel may reach another device: no remote copies, remote signals or barrier semaphores. Data moves between devices by JAX's collectives and lax.ppermute only.
A program may use at most 64 MiB of HBM per device.

v0:
```python
import functools
import math

import jax
import jax.numpy as jnp
from jax import lax
from jax.experimental import pallas as pl
from jax.experimental.pallas import tpu as pltpu
from jax.sharding import PartitionSpec as P

HEAD_SIZE = 128
MASK_BLOCK_TOKENS = 128
LANES = 128
LOWEST = -1e30
MIXED_ROWS = HEAD_SIZE + 16
SHIFT_KEYS = 256
MOST_SUM = 2.0**100
LOG2_SCALE = math.log2(math.e) / math.sqrt(HEAD_SIZE)
VMEM_LIMIT = 48 * 1024 * 1024

LITTLE = pl.CostEstimate(flops=0, bytes_accessed=1024, transcendentals=0)
MUCH = pl.CostEstimate(flops=2_000_000_000, bytes_accessed=1024, transcendentals=0)

VMEM = pl.BlockSpec(memory_space=pltpu.VMEM)
SMEM = pl.BlockSpec(memory_space=pltpu.SMEM)


def padded(count):
    return -(-count // LANES) * LANES


def nt_dot(a, b):
    return lax.dot_general(a, b, (((1,), (1,)), ((), ())), preferred_element_type=jnp.float32)


def at_block(block, size=MASK_BLOCK_TOKENS):
    return pl.ds(pl.multiple_of(block * size, size), size)


def stacked_heads(rows):
    heads = rows.shape[1] // HEAD_SIZE
    return jnp.concatenate([rows[:, h * HEAD_SIZE : (h + 1) * HEAD_SIZE] for h in range(heads)], axis=0)


def with_ones(value_t):
    shape = (MIXED_ROWS - HEAD_SIZE, value_t.shape[1])
    ones = (lax.broadcasted_iota(jnp.int32, shape, 0) == 0).astype(jnp.bfloat16)
    return jnp.concatenate([value_t, ones], axis=0)


def fold(high, mixed, scores, value_t, exact):
    seen = scores if exact else scores[0 : min(SHIFT_KEYS, scores.shape[0]), :]
    new_high = jnp.maximum(high, jnp.max(seen, axis=0, keepdims=True))
    weights = jnp.exp2(scores * LOG2_SCALE - new_high * LOG2_SCALE).astype(jnp.bfloat16)
    fading = jnp.exp2((high - new_high) * LOG2_SCALE)
    mixed = mixed * fading + jnp.dot(with_ones(value_t), weights, preferred_element_type=jnp.float32)
    return new_high, mixed


def prepare_kernel(kv_ref, out_ref):
    count = kv_ref.shape[1]
    whole = count // LANES * LANES
    rest = count - whole
    out_ref[0, 0:whole, :] = kv_ref[0, 0:whole, :]
    for at in range(0, whole, LANES):
        out_ref[1, at : at + LANES, :] = kv_ref[1, at : at + LANES, :].T
    if rest:
        empty = jnp.zeros((LANES - rest, HEAD_SIZE), jnp.float32)
        tail_key = jnp.concatenate([kv_ref[0, whole:count, :].astype(jnp.float32), empty], axis=0)
        tail_value = jnp.concatenate([kv_ref[1, whole:count, :].astype(jnp.float32), empty], axis=0)
        out_ref[0, whole : whole + LANES, :] = tail_key.astype(jnp.bfloat16)
        out_ref[1, whole : whole + LANES, :] = tail_value.T.astype(jnp.bfloat16)


def prepare(kv):
    return pl.pallas_call(
        prepare_kernel,
        out_shape=jax.ShapeDtypeStruct((2, padded(kv.shape[1]), HEAD_SIZE), jnp.bfloat16),
        in_specs=[VMEM],
        out_specs=VMEM,
        compiler_params=pltpu.CompilerParams(vmem_limit_bytes=VMEM_LIMIT),
        cost_estimate=LITTLE,
        name="prepare",
    )(kv)


def lse_rows(block_count):
    return -(-3 * block_count // 16) * 16


def packed_blocks(rows):
    return next(count for count in range(1, rows) if count * HEAD_SIZE + lse_rows(count) == rows)


def table_kernel(position_ref, images_ref, owner_ref, table_ref):
    block_count, slots = images_ref.shape
    for piece in range(slots):
        slot = lax.rem(position_ref[0] + (slots - piece), slots)
        base = piece * (block_count + 1)
        count = jnp.int32(0)
        for block in range(block_count):
            table_ref[base + 1 + block] = jnp.int32(0)
        for block in range(block_count):
            seen = lax.fori_loop(
                0,
                slots,
                lambda image, sum, block=block, slot=slot: sum
                + jnp.where(owner_ref[image] == slot, images_ref[block, image], 0),
                jnp.int32(0),
            )

            @pl.when(seen > 0)
            def _(base=base, block=block, count=count):
                table_ref[base + 1 + count] = jnp.int32(block)

            count = count + jnp.where(seen > 0, 1, 0)
        table_ref[base] = count


def seen_table(position, block_images, image_owner):
    block_count, slots = block_images.shape
    return pl.pallas_call(
        table_kernel,
        out_shape=jax.ShapeDtypeStruct((slots * (block_count + 1),), jnp.int32),
        in_specs=[SMEM] * 3,
        out_specs=SMEM,
        name="seen_table",
    )(position, block_images, image_owner)


def chunks_of(width):
    half = width // LANES // 2 * LANES
    return [(0, half), (half, width)] if half else [(0, width)]


def cross_kernel(key_count, pieces, offset, last, parts, table_ref, *refs):
    q_refs, images, refs = refs[:parts], refs[parts : parts + pieces], refs[parts + pieces :]
    if offset:
        before, refs = refs[:2], refs[2:]
    if last:
        out_ref, lse_ref, high_ref, mixed_ref, peak_ref, redo_ref = refs
    else:
        high_ref, mixed_ref, peak_ref, redo_ref = refs
    block_count = q_refs[0].shape[0] // MASK_BLOCK_TOKENS
    rows = q_refs[0].shape[1] // HEAD_SIZE * MASK_BLOCK_TOKENS
    peak_ref[...] = jnp.full_like(peak_ref, LOWEST)
    redo_ref[0] = jnp.int32(0)

    def fold_pair(blocks, image, exact):
        width = image.shape[1]
        queries = [functools.reduce(jnp.add, [q[at_block(block), :] for q in q_refs]) for block in blocks]
        queries = jnp.concatenate([stacked_heads(one) for one in queries], axis=0)
        chunks = chunks_of(width)

        def scores_of(start, stop):
            scores = nt_dot(image[0, start:stop, :], queries)
            if stop > key_count:
                body = stop - start - LANES
                tail = scores[body:, :]
                key_id = start + body + lax.broadcasted_iota(jnp.int32, tail.shape, 0)
                tail = jnp.where(key_id < key_count, tail, LOWEST)
                scores = jnp.concatenate([scores[:body, :], tail], axis=0) if body else tail
            return scores

        @pl.when(exact)
        def _():
            tops = [jnp.max(scores_of(*chunk), axis=0, keepdims=True) for chunk in chunks]
            peak_ref[0:1, :] = functools.reduce(jnp.maximum, tops)

        high = jnp.concatenate([high_ref[block][0:1] for block in blocks], axis=1)
        mixed = jnp.concatenate([mixed_ref[block] for block in blocks], axis=1)
        scores = scores_of(*chunks[0])
        seen = jnp.max(scores[0 : min(SHIFT_KEYS, scores.shape[0])], axis=0, keepdims=True)
        new_high = jnp.maximum(jnp.maximum(high, seen), peak_ref[0:1, :])
        shift = new_high * LOG2_SCALE
        mixed = mixed * jnp.exp2((high - new_high) * LOG2_SCALE)
        for index, (start, stop) in enumerate(chunks):
            following = scores_of(*chunks[index + 1]) if index + 1 < len(chunks) else None
            weights = jnp.exp2(scores * LOG2_SCALE - shift).astype(jnp.bfloat16)
            value_t = jnp.concatenate([image[1, c : c + LANES, :] for c in range(start, stop, LANES)], axis=1)
            mixed = mixed + jnp.dot(with_ones(value_t), weights, preferred_element_type=jnp.float32)
            scores = following
        for index, block in enumerate(blocks):
            own = slice(index * rows, (index + 1) * rows)
            high_ref[block] = jnp.broadcast_to(new_high[:, own], high_ref.shape[1:])
            mixed_ref[block] = mixed[:, own]

    def attempt(trial, carry):
        @pl.when((trial == 0) | (redo_ref[0] > 0))
        def _():
            if offset:
                high_ref[...] = before[0][...]
                mixed_ref[...] = before[1][...]
            else:
                high_ref[...] = jnp.full_like(high_ref, LOWEST)
                mixed_ref[...] = jnp.zeros_like(mixed_ref)
            for piece in range(pieces):
                base = (offset + piece) * (block_count + 1)
                count = table_ref[base]

                def pair_step(pair, carry, piece=piece, base=base, count=count):
                    blocks = [table_ref[base + 1 + 2 * pair], table_ref[base + jnp.minimum(2 * pair + 2, count)]]
                    fold_pair(blocks, images[piece], trial > 0)
                    return carry

                lax.fori_loop(0, (count + 1) // 2, pair_step, 0)
            most = functools.reduce(
                jnp.maximum, [mixed_ref[block, HEAD_SIZE : HEAD_SIZE + 1, :] for block in range(block_count)]
            )
            redo_ref[0] = 1 - jnp.min((most <= MOST_SUM).astype(jnp.int32))

        return carry

    lax.fori_loop(0, 2, attempt, 0)

    if last:
        lse_ref[...] = jnp.zeros_like(lse_ref)
        for block in range(block_count):
            total = mixed_ref[block, HEAD_SIZE : HEAD_SIZE + 1, :]
            out_ref[block * HEAD_SIZE : (block + 1) * HEAD_SIZE, :] = (
                mixed_ref[block, 0:HEAD_SIZE, :] / total
            ).astype(jnp.bfloat16)
            lse_ref[block : block + 1, :] = high_ref[block, 0:1, :] * LOG2_SCALE + jnp.log2(total)
        out_ref[block_count * HEAD_SIZE :, :] = lse_pieces(lse_ref[0:block_count, :], block_count)


def cross_part(table, queries, images, key_count, offset, last, before=()):
    tokens, columns = queries[0].shape
    block_count = tokens // MASK_BLOCK_TOKENS
    rows = columns // HEAD_SIZE * MASK_BLOCK_TOKENS
    state = [(block_count, 8, rows), (block_count, MIXED_ROWS, rows)]
    scratch = [pltpu.VMEM((8, 2 * rows), jnp.float32), pltpu.SMEM((1,), jnp.int32)]
    if last:
        out_shape = jax.ShapeDtypeStruct((block_count * HEAD_SIZE + lse_rows(block_count), rows), jnp.bfloat16)
        scratch = [pltpu.VMEM(shape, jnp.float32) for shape in state] + scratch
        scratch = [pltpu.VMEM((-(-block_count // 8) * 8, rows), jnp.float32)] + scratch
    else:
        out_shape = tuple(jax.ShapeDtypeStruct(shape, jnp.float32) for shape in state)
    return pl.pallas_call(
        functools.partial(cross_kernel, key_count, len(images), offset, last, len(queries)),
        out_shape=out_shape,
        in_specs=[SMEM] + [VMEM] * (len(queries) + len(images) + len(before)),
        out_specs=VMEM if last else (VMEM,) * 2,
        scratch_shapes=scratch,
        compiler_params=pltpu.CompilerParams(vmem_limit_bytes=VMEM_LIMIT),
        cost_estimate=MUCH,
        name="cross_last" if last else "cross_first",
    )(table, *queries, *images, *before)


def lse_of(ref, block_count):
    tail = ref[block_count * HEAD_SIZE :, :].astype(jnp.float32)
    return tail[0:block_count] + tail[block_count : 2 * block_count] + tail[2 * block_count : 3 * block_count]


def lse_pieces(lse, block_count):
    first = lse.astype(jnp.bfloat16).astype(jnp.float32)
    second = (lse - first).astype(jnp.bfloat16).astype(jnp.float32)
    pieces = [first, second, lse - first - second]
    spare = lse_rows(block_count) - 3 * block_count
    if spare:
        pieces.append(jnp.zeros((spare, lse.shape[1]), jnp.float32))
    return jnp.concatenate(pieces, axis=0).astype(jnp.bfloat16)


def mixed_block(part_refs, weights, block):
    at = slice(block * HEAD_SIZE, (block + 1) * HEAD_SIZE)
    terms = [weight[block : block + 1, :] * ref[at, :].astype(jnp.float32) for ref, weight in zip(part_refs, weights)]
    return functools.reduce(jnp.add, terms)


def combine_kernel(held, last, *refs):
    if held:
        mixed_ref, lse_ref, part_ref, *out_refs = refs
        block_count = lse_ref.shape[0]
        lse = [lse_ref[...], lse_of(part_ref, block_count)]
    else:
        mixed_ref, part_ref, *out_refs = refs
        block_count = packed_blocks(part_ref.shape[0])
        lse = [lse_of(mixed_ref, block_count), lse_of(part_ref, block_count)]
    highest = functools.reduce(jnp.maximum, lse)
    weights = [jnp.exp2(one - highest) for one in lse]
    total = functools.reduce(jnp.add, weights)
    weights = [one / total for one in weights]
    for block in range(block_count):
        mixed = mixed_block((mixed_ref, part_ref), weights, block)
        if last:
            store_heads(out_refs[0], block, mixed)
        else:
            out_refs[0][block * HEAD_SIZE : (block + 1) * HEAD_SIZE, :] = mixed
    if not last:
        out_refs[1][...] = highest + jnp.log2(total)


def store_heads(out_ref, block, mixed):
    at = slice(block * MASK_BLOCK_TOKENS, (block + 1) * MASK_BLOCK_TOKENS)
    for head in range(out_ref.shape[1] // HEAD_SIZE):
        piece = mixed[:, head * MASK_BLOCK_TOKENS : (head + 1) * MASK_BLOCK_TOKENS]
        out_ref[at, head * HEAD_SIZE : (head + 1) * HEAD_SIZE] = piece.T.astype(jnp.bfloat16)


def combined(so_far, part, shape, last):
    tokens, columns = shape
    held = len(so_far) == 2
    block_count = tokens // MASK_BLOCK_TOKENS
    rows = columns // HEAD_SIZE * MASK_BLOCK_TOKENS
    if last:
        out_shape = jax.ShapeDtypeStruct(shape, jnp.bfloat16)
    else:
        out_shape = (
            jax.ShapeDtypeStruct((block_count * HEAD_SIZE, rows), jnp.float32),
            jax.ShapeDtypeStruct((block_count, rows), jnp.float32),
        )
    return pl.pallas_call(
        functools.partial(combine_kernel, held, last),
        out_shape=out_shape,
        in_specs=[VMEM] * (len(so_far) + 1),
        out_specs=VMEM if last else (VMEM,) * 2,
        compiler_params=pltpu.CompilerParams(vmem_limit_bytes=VMEM_LIMIT),
        cost_estimate=MUCH,
        name="combine_last" if last else "combine",
    )(*so_far, part)


def pair_queries(q_ref, first, blocks):
    return jnp.concatenate(
        [
            stacked_heads(q_ref[block * MASK_BLOCK_TOKENS : (block + 1) * MASK_BLOCK_TOKENS, :])
            for block in range(first, first + blocks)
        ],
        axis=0,
    )


def self_first_kernel(group, q_ref, text_ref, high_ref, mixed_ref, value_ref):
    tokens, columns = q_ref.shape
    rows = columns // HEAD_SIZE * MASK_BLOCK_TOKENS
    value_ref[...] = text_ref[:, HEAD_SIZE:].T
    for index in range(tokens // MASK_BLOCK_TOKENS // group):
        first = index * group
        start, stop = first * MASK_BLOCK_TOKENS, (first + group) * MASK_BLOCK_TOKENS
        scores = nt_dot(text_ref[0:stop, 0:HEAD_SIZE], pair_queries(q_ref, first, group))
        tail = scores[start:, :]
        key_id = lax.broadcasted_iota(jnp.int32, tail.shape, 0)
        column = lax.broadcasted_iota(jnp.int32, tail.shape, 1)
        query_id = column // rows * MASK_BLOCK_TOKENS + column % MASK_BLOCK_TOKENS
        tail = jnp.where(key_id <= query_id, tail, LOWEST)
        scores = jnp.concatenate([scores[:start, :], tail], axis=0) if start else tail
        high = jnp.full((1, group * rows), LOWEST, jnp.float32)
        mixed = jnp.zeros((MIXED_ROWS, group * rows), jnp.float32)
        high, mixed = fold(high, mixed, scores, value_ref[:, 0:stop], True)
        high_ref[index] = jnp.broadcast_to(high, high_ref.shape[1:])
        mixed_ref[index] = mixed


def self_last_kernel(group, pieces, position_ref, q_ref, high_ref, mixed_ref, *refs):
    texts = refs[:pieces]
    out_ref, value_ref, new_high_ref, new_mixed_ref = refs[pieces:]
    rows = q_ref.shape[1] // HEAD_SIZE * MASK_BLOCK_TOKENS
    new_high_ref[...] = high_ref[...]
    new_mixed_ref[...] = mixed_ref[...]
    for piece in range(pieces):

        @pl.when(position_ref[0] >= piece + 1)
        def _(piece=piece):
            value_ref[...] = texts[piece][:, HEAD_SIZE:].T
            for index in range(high_ref.shape[0]):
                scores = nt_dot(texts[piece][:, 0:HEAD_SIZE], pair_queries(q_ref, index * group, group))
                high, mixed = fold(new_high_ref[index, 0:1, :], new_mixed_ref[index], scores, value_ref[...], True)
                new_high_ref[index] = jnp.broadcast_to(high, high_ref.shape[1:])
                new_mixed_ref[index] = mixed

    for index in range(high_ref.shape[0]):
        total = new_mixed_ref[index, HEAD_SIZE : HEAD_SIZE + 1, :]
        mixed = new_mixed_ref[index, 0:HEAD_SIZE, :] / total
        for block in range(group):
            store_heads(out_ref, index * group + block, mixed[:, block * rows : (block + 1) * rows])


def self_first(queries, text):
    tokens, columns = queries.shape
    block_count = tokens // MASK_BLOCK_TOKENS
    group = 1 if block_count % 2 else 2
    width = group * columns // HEAD_SIZE * MASK_BLOCK_TOKENS
    return pl.pallas_call(
        functools.partial(self_first_kernel, group),
        out_shape=(
            jax.ShapeDtypeStruct((block_count // group, 8, width), jnp.float32),
            jax.ShapeDtypeStruct((block_count // group, MIXED_ROWS, width), jnp.float32),
        ),
        in_specs=[VMEM] * 2,
        out_specs=(VMEM,) * 2,
        scratch_shapes=[pltpu.VMEM((HEAD_SIZE, tokens), jnp.bfloat16)],
        compiler_params=pltpu.CompilerParams(vmem_limit_bytes=VMEM_LIMIT),
        cost_estimate=LITTLE,
        name="self_first",
    )(queries, text)


def self_last(position, queries, state, texts):
    tokens, columns = queries.shape
    group = tokens // MASK_BLOCK_TOKENS // state[0].shape[0]
    return pl.pallas_call(
        functools.partial(self_last_kernel, group, len(texts)),
        out_shape=jax.ShapeDtypeStruct((tokens, columns), jnp.bfloat16),
        in_specs=[SMEM] + [VMEM] * (3 + len(texts)),
        out_specs=VMEM,
        scratch_shapes=[pltpu.VMEM((HEAD_SIZE, tokens), jnp.bfloat16)]
        + [pltpu.VMEM(one.shape, jnp.float32) for one in state],
        compiler_params=pltpu.CompilerParams(vmem_limit_bytes=VMEM_LIMIT),
        cost_estimate=LITTLE,
        name="self_last",
    )(position, queries, *state, *texts)


def shifted(value, axis, steps):
    count = lax.axis_size(axis)
    return lax.ppermute(value, axis, [(source, (source + steps) % count) for source in range(count)])


def swapped(value, axis, bits):
    return lax.ppermute(value, axis, [(source, source ^ bits) for source in range(lax.axis_size(axis))])


def moved(value, pairs):
    return lax.ppermute(value, "enc", pairs)


def gathered_queries(queries, ring):
    if ring != 4:
        return {step: [shifted(queries, "enc", ring - step)] for step in range(1, ring)}
    next_but_one = swapped(queries, "enc", 2)
    near = swapped(queries, "enc", 1)
    middle = moved(queries, [(1, 2), (2, 1)])
    ends = moved(next_but_one, [(2, 3), (1, 0)])
    return {1: [near], 2: [next_but_one], 3: [middle, ends]}


def after(value, earlier):
    return lax.optimization_barrier((value, earlier))[0]


def per_device(
    self_queries, text_kv, cross_queries, image_kv, block_images, image_owner
):
    rows = self_queries.shape[0]
    key_count = image_kv.shape[2]
    cycle = lax.axis_size("blk")
    ring = lax.axis_size("enc")
    position = lax.axis_index("blk").astype(jnp.int32)[None]

    images = [prepare(image_kv[0])]
    for _ in range(1, cycle):
        images.append(shifted(images[-1], "blk", 1))
    queries = gathered_queries(cross_queries, ring)
    queries[0] = [cross_queries]
    table = seen_table(position, block_images, image_owner)

    text = text_kv.reshape(rows, 2 * HEAD_SIZE)
    texts = []
    onward = after(text, images[-1])
    for _ in range(1, cycle):
        onward = lax.ppermute(onward, "blk", [(source, source + 1) for source in range(cycle - 1)])
        texts.append(onward)

    latest = [None]

    def in_turn(arrays):
        return arrays if latest[0] is None else [after(one, latest[0]) for one in arrays]

    def begun(step):
        latest[0] = cross_part(table, in_turn(queries[step]), images[:1], key_count, 0, False)
        return latest[0]

    def finished(step, state=None):
        used = images if state is None else images[1:]
        before = () if state is None else state
        offset = 0 if state is None else 1
        latest[0] = cross_part(table, in_turn(queries[step]), used, key_count, offset, True, before)
        return latest[0]

    split = cycle > 1
    own = begun(0) if split else None
    self_state = latest[0] = self_first(in_turn([self_queries])[0], text)
    steps = [2, 1, 3] if ring == 4 else list(range(1, ring))
    states = {step: begun(step) for step in steps[:-1]} if split else {}
    received = []
    for step in [2, 3, 1] if ring == 4 else steps:
        part = finished(step, states.get(step))
        received.append(swapped(part, "enc", step) if ring == 4 else shifted(part, "enc", step))
    own_part = finished(0, own)
    self_out = latest[0] = self_last(position, in_turn([self_queries])[0], self_state, texts)
    so_far = in_turn([own_part])
    for index, part in enumerate(received):
        so_far = combined(so_far, part, cross_queries.shape, index + 1 == len(received))
    return (self_out, so_far)


def solution(mesh):
    placed = (
        P("blk", ("tp", "enc")),
        P("blk", None, "tp"),
        P("blk", ("tp", "enc")),
        P("blk", None, "enc", "tp"),
        P("blk", None),
        P(),
    )
    return jax.shard_map(
        per_device,
        mesh=mesh,
        in_specs=placed,
        out_specs=(P("blk", ("tp", "enc")), P("blk", ("tp", "enc"))),
        check_vma=False,
    )
```

profile of v0, /device:TPU:0, one launch (start us, length us, event | category | flops | bytes accessed | tf_op | source)
XLA Modules:
  0.0 56.9 jit_solution(15811388353979109428)
XLA Ops:
  0.6 1.3 %copy.13 = bf16[1,2,1601,128]{3,2,1,0:T(8,128)(2,1)S(1)} copy(bf16[1,2,1601,128]{3,1,2,0:T(2,128)(2,1)} %param.9) | data formatting | bytes 1639424 | tf_op args[3]
  1.9 0.0 copy-start.2
  1.9 0.2 prepare.1.refs_1_.refs_2_
  2.1 3.0 %collective-permute-start.3 = (bf16[2,1664,128]{2,1,0:T(8,128)(2,1)S(1)}, bf16[2,1664,128]{2,1,0:T(8,128)(2,1)S(1)}, u32[]{:S(2)}, u32[]{:S(2)}) collective-permute-start(bf16[2,1664,128]{2,1,0:T(8,128)(2,1)S(1)} %prepare.1.refs_1_.refs_2_), channel_id=1, source_target_pairs={{0,16},{16,0},{1,17},{17,1},{2,18},{18,2},{3,19},{19,3},{4,20},{20... | collective-permute-start | bytes 2555912 | tf_op jit(solution)/shard_map/ppermute | solution.py:418
  5.1 0.0 copy-done.2
  5.1 2.6 %collective-permute-start.2 = (bf16[512,256]{1,0:T(8,128)(2,1)S(1)}, bf16[512,256]{1,0:T(8,128)(2,1)S(1)}, u32[]{:S(2)}, u32[]{:S(2)}) collective-permute-start(bf16[512,256]{1,0:T(8,128)(2,1)S(1)} %copy-done.2), channel_id=1, source_target_pairs={{0,2},{1,3},{2,0},{3,1},{4,6},{5,7},{6,4},{7,5},{8,10},{9,11},{10,... | collective-permute-start | bytes 786440 | tf_op jit(solution)/shard_map/ppermute | solution.py:422
  7.7 1.6 %collective-permute-start = (bf16[512,256]{1,0:T(8,128)(2,1)S(1)}, bf16[512,256]{1,0:T(8,128)(2,1)S(1)}, u32[]{:S(2)}, u32[]{:S(2)}) collective-permute-start(bf16[512,256]{1,0:T(8,128)(2,1)S(1)} %copy-done.2), channel_id=1, source_target_pairs={{0,1},{1,0},{2,3},{3,2},{4,5},{5,4},{6,7},{7,6},{8,9},{9,8},{10,11... | collective-permute-start | bytes 786440 | tf_op jit(solution)/shard_map/ppermute | solution.py:422
  9.3 0.7 %collective-permute-start.1 = (bf16[512,256]{1,0:T(8,128)(2,1)S(1)}, bf16[512,256]{1,0:T(8,128)(2,1)S(1)}, u32[]{:S(2)}, u32[]{:S(2)}) collective-permute-start(bf16[512,256]{1,0:T(8,128)(2,1)S(1)} %copy-done.2), channel_id=1, source_target_pairs={{1,2},{2,1},{5,6},{6,5},{9,10},{10,9},{13,14},{14,13},{17,18},{18,... | collective-permute-start | bytes 786440 | tf_op jit(solution)/shard_map/ppermute | solution.py:426
  9.9 0.0 copy-start.4
  10.0 0.7 %copy-done.4 = s32[4,2]{0,1:T(2,128)S(1)} copy-done((s32[4,2]{0,1:T(2,128)S(1)}, s32[4,2]{0,1:T(2,128)}, u32[]{:S(2)}) %copy-start.4) | copy-done | bytes 56
  10.6 0.7 %copy.8.images_ref = s32[4,2]{1,0:T(4,128)} copy(s32[4,2]{0,1:T(2,128)S(1)} %copy-done.4) | data formatting | bytes 64 | tf_op args[4]
  11.3 1.4 %seen_table.1.table_ref = s32[10]{0:T(128)} custom-call(s32[1]{0:T(128)} %bitcast.position_ref, s32[4,2]{1,0:T(4,128)} %copy.8.images_ref, s32[2]{0:T(128)} %owner_ref.1), custom_call_target="tpu_custom_call" | custom-call | tf_op jit(solution)/shard_map/seen_table/pallas_call | solution.py:122
  12.6 0.0 copy-start.1
  12.7 0.6 %copy-done.1 = s32[10]{0:T(128)S(1)} copy-done((s32[10]{0:T(128)S(1)}, s32[10]{0:T(128)}, u32[]{:S(2)}) %copy-start.1) | copy-done | bytes 64
  13.3 0.0 copy-start.3
  13.3 2.9 %cross_first.3 = (f32[4,8,256]{2,1,0:T(8,128)S(1)}, f32[4,144,256]{2,1,0:T(8,128)S(1)}) custom-call(s32[10]{0:T(128)S(1)} %copy-done.1, bf16[512,256]{1,0:T(8,128)(2,1)S(1)} %copy-done.2, bf16[2,1664,128]{2,1,0:T(8,128)(2,1)S(1)} %prepare.1.refs_1_.refs_2_), custom_call_target="tpu_custom_call" | custom-call | flops 2000000000 | bytes 1024 | tf_op jit(solution)/shard_map/cross_first/pallas_call | solution.py:239
  16.2 0.0 copy-done.3
  16.2 0.0 copy-start
  16.3 0.9 %copy-done = bf16[512,256]{1,0:T(8,128)(2,1)S(1)} copy-done((bf16[512,256]{1,0:T(8,128)(2,1)S(1)}, bf16[512,256]{1,0:T(8,128)(2,1)}, u32[]{:S(2)}) %copy-start) | copy-done | bytes 262168
  17.2 1.1 %self_first.1 = (f32[2,8,512]{2,1,0:T(8,128)S(1)}, f32[2,144,512]{2,1,0:T(8,128)S(1)}) custom-call(bf16[512,256]{1,0:T(8,128)(2,1)S(1)} %copy-done, bf16[512,256]{1,0:T(8,128)(2,1)S(1)} %bitcast.9), custom_call_target="tpu_custom_call" | custom-call | bytes 1024 | tf_op jit(solution)/shard_map/self_first/pallas_call | solution.py:385
  18.3 2.3 %collective-permute-done.2.refs_0_ = bf16[512,256]{1,0:T(8,128)(2,1)S(1)} collective-permute-done((bf16[512,256]{1,0:T(8,128)(2,1)S(1)}, bf16[512,256]{1,0:T(8,128)(2,1)S(1)}, u32[]{:S(2)}, u32[]{:S(2)}) %collective-permute-start.2) | collective-permute-done | bytes 262176 | tf_op jit(solution)/shard_map/ppermute | solution.py:422
  20.6 2.9 %cross_first.4 = (f32[4,8,256]{2,1,0:T(8,128)S(1)}, f32[4,144,256]{2,1,0:T(8,128)S(1)}) custom-call(s32[10]{0:T(128)S(1)} %copy-done.1, bf16[512,256]{1,0:T(8,128)(2,1)S(1)} %collective-permute-done.2.refs_0_, bf16[2,1664,128]{2,1,0:T(8,128)(2,1)S(1)} %prepare.1.refs_1_.refs_2_), custom_call_target="tpu_custom_call" | custom-call | flops 2000000000 | bytes 1024 | tf_op jit(solution)/shard_map/cross_first/pallas_call | solution.py:239
  23.5 0.0 collective-permute-done.refs_0_
  23.5 1.3 %collective-permute-start.4 = (bf16[512,256]{1,0:T(8,128)(2,1)S(1)}, bf16[512,256]{1,0:T(8,128)(2,1)S(1)}, u32[]{:S(2)}, u32[]{:S(2)}) collective-permute-start(bf16[512,256]{1,0:T(8,128)(2,1)S(1)} %collective-permute-done.2.refs_0_), channel_id=1, source_target_pairs={{2,3},{1,0},{6,7},{5,4},{10,11},{9,8},{14,15},{13,12},{18,19},{17,... | collective-permute-start | bytes 786440 | tf_op jit(solution)/shard_map/ppermute | solution.py:426
  24.8 2.9 %cross_first.5 = (f32[4,8,256]{2,1,0:T(8,128)S(1)}, f32[4,144,256]{2,1,0:T(8,128)S(1)}) custom-call(s32[10]{0:T(128)S(1)} %copy-done.1, bf16[512,256]{1,0:T(8,128)(2,1)S(1)} %collective-permute-done.refs_0_, bf16[2,1664,128]{2,1,0:T(8,128)(2,1)S(1)} %prepare.1.refs_1_.refs_2_), custom_call_target="tpu_custom_call" | custom-call | flops 2000000000 | bytes 1024 | tf_op jit(solution)/shard_map/cross_first/pallas_call | solution.py:239
  27.7 0.0 collective-permute-done.3.refs_1_.refs_3_
  27.7 1.9 %cross_last.4 = bf16[528,256]{1,0:T(8,128)(2,1)S(1)} custom-call(s32[10]{0:T(128)S(1)} %copy-done.1, bf16[512,256]{1,0:T(8,128)(2,1)S(1)} %collective-permute-done.2.refs_0_, bf16[2,1664,128]{2,1,0:T(8,128)(2,1)S(1)} %collective-permute-done.3.refs_1_.refs_3_, f32[4,8,256]{2,1,0:T(8,128)S(1)} %get-tuple-element.31.refs_2_, ...), custom_call_target="tpu_custom_call" | custom-call | flops 2000000000 | bytes 1024 | tf_op jit(solution)/shard_map/cross_last/pallas_call | solution.py:239
  29.6 3.6 %collective-permute-start.6 = (bf16[528,256]{1,0:T(8,128)(2,1)S(1)}, bf16[528,256]{1,0:T(8,128)(2,1)S(1)}, u32[]{:S(2)}, u32[]{:S(2)}) collective-permute-start(bf16[528,256]{1,0:T(8,128)(2,1)S(1)} %cross_last.4), channel_id=1, source_target_pairs={{0,2},{1,3},{2,0},{3,1},{4,6},{5,7},{6,4},{7,5},{8,10},{9,11},{10,... | collective-permute-start | bytes 811016 | tf_op jit(solution)/shard_map/ppermute | solution.py:422
  33.3 0.0 collective-permute-done.4.refs_1_
  33.3 0.0 collective-permute-done.1.refs_0_
  33.3 4.0 %cross_last.5 = bf16[528,256]{1,0:T(8,128)(2,1)S(1)} custom-call(s32[10]{0:T(128)S(1)} %copy-done.1, bf16[512,256]{1,0:T(8,128)(2,1)S(1)} %collective-permute-done.1.refs_0_, bf16[512,256]{1,0:T(8,128)(2,1)S(1)} %collective-permute-done.4.refs_1_, bf16[2,1664,128]{2,1,0:T(8,128)(2,1)S(1)} %prepare.1.refs_1_.refs_2_, ...), custom_call_target="tpu_custom_call" | custom-call | flops 2000000000 | bytes 1024 | tf_op jit(solution)/shard_map/cross_last/pallas_call | solution.py:239
  37.3 4.6 %collective-permute-start.7 = (bf16[528,256]{1,0:T(8,128)(2,1)S(1)}, bf16[528,256]{1,0:T(8,128)(2,1)S(1)}, u32[]{:S(2)}, u32[]{:S(2)}) collective-permute-start(bf16[528,256]{1,0:T(8,128)(2,1)S(1)} %cross_last.5), channel_id=1, source_target_pairs={{0,3},{1,2},{2,1},{3,0},{4,7},{5,6},{6,5},{7,4},{8,11},{9,10},{10,... | collective-permute-start | bytes 811016 | tf_op jit(solution)/shard_map/ppermute | solution.py:422
  41.9 2.2 %collective-permute-start.5 = (bf16[512,256]{1,0:T(8,128)(2,1)S(1)}, bf16[512,256]{1,0:T(8,128)(2,1)S(1)}, u32[]{:S(2)}, u32[]{:S(2)}) collective-permute-start(bf16[512,256]{1,0:T(8,128)(2,1)S(1)} %bitcast.10), channel_id=1, source_target_pairs={{0,16},{1,17},{2,18},{3,19},{4,20},{5,21},{6,22},{7,23},{8,24},{9,... | collective-permute-start | bytes 786440 | tf_op jit(solution)/shard_map/ppermute | solution.py:463
  44.1 1.9 %cross_last.6 = bf16[528,256]{1,0:T(8,128)(2,1)S(1)} custom-call(s32[10]{0:T(128)S(1)} %copy-done.1, bf16[512,256]{1,0:T(8,128)(2,1)S(1)} %collective-permute-done.refs_0_, bf16[2,1664,128]{2,1,0:T(8,128)(2,1)S(1)} %collective-permute-done.3.refs_1_.refs_3_, f32[4,8,256]{2,1,0:T(8,128)S(1)} %get-tuple-element.34.refs_2_, ...), custom_call_target="tpu_custom_call" | custom-call | flops 2000000000 | bytes 1024 | tf_op jit(solution)/shard_map/cross_last/pallas_call | solution.py:239
  46.0 0.1 collective-permute-start.8
  46.1 1.9 %cross_last.7.refs_0_ = bf16[528,256]{1,0:T(8,128)(2,1)S(1)} custom-call(s32[10]{0:T(128)S(1)} %copy-done.1, bf16[512,256]{1,0:T(8,128)(2,1)S(1)} %copy-done.2, bf16[2,1664,128]{2,1,0:T(8,128)(2,1)S(1)} %collective-permute-done.3.refs_1_.refs_3_, f32[4,8,256]{2,1,0:T(8,128)S(1)} %get-tuple-element.25.refs_2_, f32[4,144,256]{2,1,0:T(8,128)S(1)} %get-tuple-element.26.refs_3_), custom_call_target="tpu_custom_call" | custom-call | flops 2000000000 | bytes 1024 | tf_op jit(solution)/shard_map/cross_last/pallas_call | solution.py:239
  48.0 0.4 collective-permute-done.5.refs_0_
  48.4 0.9 %self_last.1 = bf16[512,256]{1,0:T(8,128)(2,1)} custom-call(s32[1]{0:T(128)} %bitcast.position_ref, bf16[512,256]{1,0:T(8,128)(2,1)S(1)} %copy-done, f32[2,8,512]{2,1,0:T(8,128)S(1)} %get-tuple-element.28.high_ref, f32[2,144,512]{2,1,0:T(8,128)S(1)} %get-tuple-element.29.mixed_ref, bf16[512,256]{1,0:T(8,128)(2,1)S(1)} %collective-permute-done.5.refs_0_), custom_call_target="tpu_custom_call" | custom-call | bytes 1024 | tf_op jit(solution)/shard_map/self_last/pallas_call | solution.py:403
  49.3 1.1 %collective-permute-done.6.refs_1_ = bf16[528,256]{1,0:T(8,128)(2,1)S(1)} collective-permute-done((bf16[528,256]{1,0:T(8,128)(2,1)S(1)}, bf16[528,256]{1,0:T(8,128)(2,1)S(1)}, u32[]{:S(2)}, u32[]{:S(2)}) %collective-permute-start.6) | collective-permute-done | bytes 270368 | tf_op jit(solution)/shard_map/ppermute | solution.py:422
  50.4 0.1 combine.2
  50.5 0.0 collective-permute-done.7.refs_2_
  50.5 0.1 combine.3
  50.6 5.4 %collective-permute-done.8.refs_2_ = bf16[528,256]{1,0:T(8,128)(2,1)S(1)} collective-permute-done((bf16[528,256]{1,0:T(8,128)(2,1)S(1)}, bf16[528,256]{1,0:T(8,128)(2,1)S(1)}, u32[]{:S(2)}, u32[]{:S(2)}) %collective-permute-start.8) | collective-permute-done | bytes 270368 | tf_op jit(solution)/shard_map/ppermute | solution.py:422
  56.0 0.9 %combine_last.1 = bf16[512,256]{1,0:T(8,128)(2,1)} custom-call(f32[512,256]{1,0:T(8,128)S(1)} %get-tuple-element.46.refs_0_, f32[4,256]{1,0:T(4,128)S(1)} %get-tuple-element.47.refs_1_, bf16[528,256]{1,0:T(8,128)(2,1)S(1)} %collective-permute-done.8.refs_2_), custom_call_target="tpu_custom_call" | custom-call | flops 2000000000 | bytes 1024 | tf_op jit(solution)/shard_map/combine_last/pallas_call | solution.py:314
  (1 shorter events, 0.0 us)
Async XLA Ops:
  1.9 3.2 %copy-start.2 = (bf16[512,256]{1,0:T(8,128)(2,1)S(1)}, bf16[512,256]{1,0:T(8,128)(2,1)}, u32[]{:S(2)}) copy-start(bf16[512,256]{1,0:T(8,128)(2,1)} %refs_0_.2) | copy-start | bytes 786436
  2.1 25.6 %collective-permute-start.3 = (bf16[2,1664,128]{2,1,0:T(8,128)(2,1)S(1)}, bf16[2,1664,128]{2,1,0:T(8,128)(2,1)S(1)}, u32[]{:S(2)}, u32[]{:S(2)}) collective-permute-start(bf16[2,1664,128]{2,1,0:T(8,128)(2,1)S(1)} %prepare.1.refs_1_.refs_2_), channel_id=1, source_target_pairs={{0,16},{16,0},{1,17},{17,1},{2,18},{18,2},{3,19},{19,3},{4,20},{20... | collective-permute-start | bytes 2555912 | tf_op jit(solution)/shard_map/ppermute | solution.py:418
  5.1 15.5 %collective-permute-start.2 = (bf16[512,256]{1,0:T(8,128)(2,1)S(1)}, bf16[512,256]{1,0:T(8,128)(2,1)S(1)}, u32[]{:S(2)}, u32[]{:S(2)}) collective-permute-start(bf16[512,256]{1,0:T(8,128)(2,1)S(1)} %copy-done.2), channel_id=1, source_target_pairs={{0,2},{1,3},{2,0},{3,1},{4,6},{5,7},{6,4},{7,5},{8,10},{9,11},{10,... | collective-permute-start | bytes 786440 | tf_op jit(solution)/shard_map/ppermute | solution.py:422
  7.7 15.8 %collective-permute-start = (bf16[512,256]{1,0:T(8,128)(2,1)S(1)}, bf16[512,256]{1,0:T(8,128)(2,1)S(1)}, u32[]{:S(2)}, u32[]{:S(2)}) collective-permute-start(bf16[512,256]{1,0:T(8,128)(2,1)S(1)} %copy-done.2), channel_id=1, source_target_pairs={{0,1},{1,0},{2,3},{3,2},{4,5},{5,4},{6,7},{7,6},{8,9},{9,8},{10,11... | collective-permute-start | bytes 786440 | tf_op jit(solution)/shard_map/ppermute | solution.py:422
  9.3 24.0 %collective-permute-start.1 = (bf16[512,256]{1,0:T(8,128)(2,1)S(1)}, bf16[512,256]{1,0:T(8,128)(2,1)S(1)}, u32[]{:S(2)}, u32[]{:S(2)}) collective-permute-start(bf16[512,256]{1,0:T(8,128)(2,1)S(1)} %copy-done.2), channel_id=1, source_target_pairs={{1,2},{2,1},{5,6},{6,5},{9,10},{10,9},{13,14},{14,13},{17,18},{18,... | collective-permute-start | bytes 786440 | tf_op jit(solution)/shard_map/ppermute | solution.py:426
  9.9 0.7 %copy-start.4 = (s32[4,2]{0,1:T(2,128)S(1)}, s32[4,2]{0,1:T(2,128)}, u32[]{:S(2)}) copy-start(s32[4,2]{0,1:T(2,128)} %param.10) | copy-start | bytes 100
  12.6 0.7 %copy-start.1 = (s32[10]{0:T(128)S(1)}, s32[10]{0:T(128)}, u32[]{:S(2)}) copy-start(s32[10]{0:T(128)} %seen_table.1.table_ref) | copy-start | bytes 124
  13.3 2.9 %copy-start.3 = (bf16[512,2,128]{2,1,0:T(2,128)(2,1)S(1)}, bf16[512,2,128]{2,1,0:T(2,128)(2,1)}, u32[]{:S(2)}) copy-start(bf16[512,2,128]{2,1,0:T(2,128)(2,1)} %param.7) | copy-start | bytes 786436
  16.2 1.0 %copy-start = (bf16[512,256]{1,0:T(8,128)(2,1)S(1)}, bf16[512,256]{1,0:T(8,128)(2,1)}, u32[]{:S(2)}) copy-start(bf16[512,256]{1,0:T(8,128)(2,1)} %q_ref.1) | copy-start | bytes 786436
  23.5 9.8 %collective-permute-start.4 = (bf16[512,256]{1,0:T(8,128)(2,1)S(1)}, bf16[512,256]{1,0:T(8,128)(2,1)S(1)}, u32[]{:S(2)}, u32[]{:S(2)}) collective-permute-start(bf16[512,256]{1,0:T(8,128)(2,1)S(1)} %collective-permute-done.2.refs_0_), channel_id=1, source_target_pairs={{2,3},{1,0},{6,7},{5,4},{10,11},{9,8},{14,15},{13,12},{18,19},{17,... | collective-permute-start | bytes 786440 | tf_op jit(solution)/shard_map/ppermute | solution.py:426
  29.6 20.7 %collective-permute-start.6 = (bf16[528,256]{1,0:T(8,128)(2,1)S(1)}, bf16[528,256]{1,0:T(8,128)(2,1)S(1)}, u32[]{:S(2)}, u32[]{:S(2)}) collective-permute-start(bf16[528,256]{1,0:T(8,128)(2,1)S(1)} %cross_last.4), channel_id=1, source_target_pairs={{0,2},{1,3},{2,0},{3,1},{4,6},{5,7},{6,4},{7,5},{8,10},{9,11},{10,... | collective-permute-start | bytes 811016 | tf_op jit(solution)/shard_map/ppermute | solution.py:422
  37.3 13.2 %collective-permute-start.7 = (bf16[528,256]{1,0:T(8,128)(2,1)S(1)}, bf16[528,256]{1,0:T(8,128)(2,1)S(1)}, u32[]{:S(2)}, u32[]{:S(2)}) collective-permute-start(bf16[528,256]{1,0:T(8,128)(2,1)S(1)} %cross_last.5), channel_id=1, source_target_pairs={{0,3},{1,2},{2,1},{3,0},{4,7},{5,6},{6,5},{7,4},{8,11},{9,10},{10,... | collective-permute-start | bytes 811016 | tf_op jit(solution)/shard_map/ppermute | solution.py:422
  41.9 6.5 %collective-permute-start.5 = (bf16[512,256]{1,0:T(8,128)(2,1)S(1)}, bf16[512,256]{1,0:T(8,128)(2,1)S(1)}, u32[]{:S(2)}, u32[]{:S(2)}) collective-permute-start(bf16[512,256]{1,0:T(8,128)(2,1)S(1)} %bitcast.10), channel_id=1, source_target_pairs={{0,16},{1,17},{2,18},{3,19},{4,20},{5,21},{6,22},{7,23},{8,24},{9,... | collective-permute-start | bytes 786440 | tf_op jit(solution)/shard_map/ppermute | solution.py:463
  46.0 10.0 %collective-permute-start.8 = (bf16[528,256]{1,0:T(8,128)(2,1)S(1)}, bf16[528,256]{1,0:T(8,128)(2,1)S(1)}, u32[]{:S(2)}, u32[]{:S(2)}) collective-permute-start(bf16[528,256]{1,0:T(8,128)(2,1)S(1)} %cross_last.6), channel_id=1, source_target_pairs={{0,1},{1,0},{2,3},{3,2},{4,5},{5,4},{6,7},{7,6},{8,9},{9,8},{10,11... | collective-permute-start | bytes 811016 | tf_op jit(solution)/shard_map/ppermute | solution.py:422
where the time goes:
time: 56.8 us; the launch traced here: 56.9 us
  Pallas kernels  23.1 us (41%)
  starting transfers between devices  19.6 us (35%)
  waiting for transfers between devices  9.21 us (16%)
  local copies, waits for them, and re-layouts  4.19 us (7%)
  between operations  0.82 us (1%)
    pallas_call x7, Pallas kernels, cross_part(): pl.pallas_call(functools.partial(cross_kernel, key_count, len(images), of...  18.4 us
    ppermute x5, starting transfers between devices, swapped(): lax.ppermute(value, axis, [(source, source ^ bits) for source in range(la...  12.4 us
    ppermute x5, waiting for transfers between devices, swapped(): lax.ppermute(value, axis, [(source, source ^ bits) for source in range(la...  8.83 us
    unnamed x13, local copies, waits for them, and re-layouts  4.19 us
    ppermute x1, starting transfers between devices, shifted(): lax.ppermute(value, axis, [(source, (source + steps) % count) for source...  3 us
    ppermute x1, starting transfers between devices, per_device(): lax.ppermute(onward, 'blk', [(source, source + 1) for source in range(cyc...  2.23 us
    ppermute x2, starting transfers between devices, moved(): return lax.ppermute(value, 'enc', pairs)  1.96 us
    pallas_call x1, Pallas kernels, seen_table(): pl.pallas_call(table_kernel, out_shape=jax.ShapeDtypeStruct((slots * (blo...  1.35 us
  transfers between devices with their start and end apart: 9, of which 4 were waited for; matrix products, arithmetic and copies ran while one was open for 1% of the time, Pallas kernels for 39%

commit v1 on v0

--- a/solution.py
+++ b/solution.py
@@ -426,16 +426,6 @@
     return lax.ppermute(value, "enc", pairs)
 
 
-def gathered_queries(queries, ring):
-    if ring != 4:
-        return {step: [shifted(queries, "enc", ring - step)] for step in range(1, ring)}
-    next_but_one = swapped(queries, "enc", 2)
-    near = swapped(queries, "enc", 1)
-    middle = moved(queries, [(1, 2), (2, 1)])
-    ends = moved(next_but_one, [(2, 3), (1, 0)])
-    return {1: [near], 2: [next_but_one], 3: [middle, ends]}
-
-
 def after(value, earlier):
     return lax.optimization_barrier((value, earlier))[0]
 
@@ -452,7 +442,10 @@
     images = [prepare(image_kv[0])]
     for _ in range(1, cycle):
         images.append(shifted(images[-1], "blk", 1))
-    queries = gathered_queries(cross_queries, ring)
+    if ring == 4:
+        queries = {step: [swapped(cross_queries, "enc", step)] for step in (2, 1)}
+    else:
+        queries = {step: [shifted(cross_queries, "enc", ring - step)] for step in range(1, ring)}
     queries[0] = [cross_queries]
     table = seen_table(position, block_images, image_owner)
 
@@ -480,12 +473,16 @@
         return latest[0]
 
     split = cycle > 1
+    self_state = latest[0] = self_first(self_queries, text)
     own = begun(0) if split else None
-    self_state = latest[0] = self_first(in_turn([self_queries])[0], text)
-    steps = [2, 1, 3] if ring == 4 else list(range(1, ring))
-    states = {step: begun(step) for step in steps[:-1]} if split else {}
+    if ring == 4:
+        middle = moved(in_turn([cross_queries])[0], [(1, 2), (2, 1)])
+        ends = moved(queries[2][0], [(2, 3), (1, 0)])
+        queries[3] = [middle, ends]
+    steps = [2, 3, 1] if ring == 4 else list(range(1, ring))
+    states = {step: begun(step) for step in steps[:1]} if split else {}
     received = []
-    for step in [2, 3, 1] if ring == 4 else steps:
+    for step in steps:
         part = finished(step, states.get(step))
         received.append(swapped(part, "enc", step) if ring == 4 else shifted(part, "enc", step))
     own_part = finished(0, own)

time: 56.8 us -> 54.4 us (0.958); the launches traced: 56.9 us -> 53.9 us
  Pallas kernels: 23.1 us -> 18.9 us
  starting transfers between devices: 19.6 us -> 22.2 us
  waiting for transfers between devices: 9.21 us -> 7.84 us
    pallas_call x7 -> x6, Pallas kernels: 18.4 us -> 14.3 us  [cross_part(): pl.pallas_call(functools.partial(cross_kernel, key_count, len(images), of...]
    ppermute x5, starting transfers between devices: 12.4 us -> 14 us  [swapped(): lax.ppermute(value, axis, [(source, source ^ bits) for source in range(la...]
    ppermute x5, waiting for transfers between devices: 8.83 us -> 7.43 us  [swapped(): lax.ppermute(value, axis, [(source, source ^ bits) for source in range(la...]
    ppermute x1, starting transfers between devices: 2.23 us -> 3.25 us  [per_device(): lax.ppermute(onward, 'blk', [(source, source + 1) for source in range(cyc...]
  transfers between devices with their start and end apart: 9 -> 9, of which waited for: 4 -> 4; matrix products, arithmetic and copies ran while one was open for 1% -> 1% of each run, Pallas kernels for 39% -> 33%
where the time goes in v1:
time: 54.4 us; the launch traced here: 53.9 us
  starting transfers between devices  22.2 us (41%)
  Pallas kernels  18.9 us (35%)
  waiting for transfers between devices  7.84 us (14%)
  local copies, waits for them, and re-layouts  4.2 us (8%)
  between operations  0.8 us (1%)
    pallas_call x6, Pallas kernels, cross_part(): pl.pallas_call(functools.partial(cross_kernel, key_count, len(images), of...  14.3 us
    ppermute x5, starting transfers between devices, swapped(): lax.ppermute(value, axis, [(source, source ^ bits) for source in range(la...  14 us
    ppermute x5, waiting for transfers between devices, swapped(): lax.ppermute(value, axis, [(source, source ^ bits) for source in range(la...  7.43 us
    unnamed x13, local copies, waits for them, and re-layouts  4.2 us
    ppermute x1, starting transfers between devices, per_device(): lax.ppermute(onward, 'blk', [(source, source + 1) for source in range(cyc...  3.25 us
    ppermute x1, starting transfers between devices, shifted(): lax.ppermute(value, axis, [(source, (source + steps) % count) for source...  3 us
    ppermute x2, starting transfers between devices, moved(): return lax.ppermute(value, 'enc', pairs)  1.96 us
    pallas_call x1, Pallas kernels, seen_table(): pl.pallas_call(table_kernel, out_shape=jax.ShapeDtypeStruct((slots * (blo...  1.35 us
  transfers between devices with their start and end apart: 9, of which 4 were waited for; matrix products, arithmetic and copies ran while one was open for 1% of the time, Pallas kernels for 33%

profile of v1, /device:TPU:0, one launch (start us, length us, event | category | flops | bytes accessed | tf_op | source)
XLA Modules:
  0.0 53.9 jit_solution(11022732841760514163)
XLA Ops:
  0.6 1.3 %copy.13 = bf16[1,2,1601,128]{3,2,1,0:T(8,128)(2,1)S(1)} copy(bf16[1,2,1601,128]{3,1,2,0:T(2,128)(2,1)} %param.9) | data formatting | bytes 1639424 | tf_op args[3]
  1.9 0.0 copy-start.2
  1.9 0.0 copy-start.3
  1.9 0.2 prepare.1.refs_1_.refs_2_
  2.1 3.0 %collective-permute-start.3 = (bf16[2,1664,128]{2,1,0:T(8,128)(2,1)S(1)}, bf16[2,1664,128]{2,1,0:T(8,128)(2,1)S(1)}, u32[]{:S(2)}, u32[]{:S(2)}) collective-permute-start(bf16[2,1664,128]{2,1,0:T(8,128)(2,1)S(1)} %prepare.1.refs_1_.refs_2_), channel_id=1, source_target_pairs={{0,16},{16,0},{1,17},{17,1},{2,18},{18,2},{3,19},{19,3},{4,20},{20... | collective-permute-start | bytes 2555912 | tf_op jit(solution)/shard_map/ppermute | solution.py:418
  5.1 0.0 copy-done.2
  5.1 2.6 %collective-permute-start.2 = (bf16[512,256]{1,0:T(8,128)(2,1)S(1)}, bf16[512,256]{1,0:T(8,128)(2,1)}, u32[]{:S(2)}, u32[]{:S(2)}) collective-permute-start(bf16[512,256]{1,0:T(8,128)(2,1)S(1)} %copy-done.2), channel_id=1, source_target_pairs={{0,2},{1,3},{2,0},{3,1},{4,6},{5,7},{6,4},{7,5},{8,10},{9,11},{10,... | collective-permute-start | bytes 786440 | tf_op jit(solution)/shard_map/ppermute | solution.py:422
  7.7 1.6 %collective-permute-start = (bf16[512,256]{1,0:T(8,128)(2,1)S(1)}, bf16[512,256]{1,0:T(8,128)(2,1)S(1)}, u32[]{:S(2)}, u32[]{:S(2)}) collective-permute-start(bf16[512,256]{1,0:T(8,128)(2,1)S(1)} %copy-done.2), channel_id=1, source_target_pairs={{0,1},{1,0},{2,3},{3,2},{4,5},{5,4},{6,7},{7,6},{8,9},{9,8},{10,11... | collective-permute-start | bytes 786440 | tf_op jit(solution)/shard_map/ppermute | solution.py:422
  9.3 0.0 copy-done.3
  9.3 0.0 copy-start
  9.3 0.9 %copy-done = bf16[512,256]{1,0:T(8,128)(2,1)S(1)} copy-done((bf16[512,256]{1,0:T(8,128)(2,1)S(1)}, bf16[512,256]{1,0:T(8,128)(2,1)}, u32[]{:S(2)}) %copy-start) | copy-done | bytes 262168
  10.2 1.1 %self_first.1 = (f32[2,8,512]{2,1,0:T(8,128)S(1)}, f32[2,144,512]{2,1,0:T(8,128)S(1)}) custom-call(bf16[512,256]{1,0:T(8,128)(2,1)S(1)} %copy-done, bf16[512,256]{1,0:T(8,128)(2,1)S(1)} %bitcast.9), custom_call_target="tpu_custom_call" | custom-call | bytes 1024 | tf_op jit(solution)/shard_map/self_first/pallas_call | solution.py:385
  11.3 0.0 copy-start.4
  11.3 0.7 %copy-done.4 = s32[4,2]{0,1:T(2,128)S(1)} copy-done((s32[4,2]{0,1:T(2,128)S(1)}, s32[4,2]{0,1:T(2,128)}, u32[]{:S(2)}) %copy-start.4) | copy-done | bytes 56
  12.0 0.7 %copy.8.images_ref = s32[4,2]{1,0:T(4,128)} copy(s32[4,2]{0,1:T(2,128)S(1)} %copy-done.4) | data formatting | bytes 64 | tf_op args[4]
  12.7 1.4 %seen_table.1.table_ref = s32[10]{0:T(128)} custom-call(s32[1]{0:T(128)} %bitcast.position_ref, s32[4,2]{1,0:T(4,128)} %copy.8.images_ref, s32[2]{0:T(128)} %owner_ref.1), custom_call_target="tpu_custom_call" | custom-call | tf_op jit(solution)/shard_map/seen_table/pallas_call | solution.py:122
  14.0 0.0 copy-start.1
  14.0 0.6 %copy-done.1 = s32[10]{0:T(128)S(1)} copy-done((s32[10]{0:T(128)S(1)}, s32[10]{0:T(128)}, u32[]{:S(2)}) %copy-start.1) | copy-done | bytes 64
  14.7 2.9 %cross_first.2 = (f32[4,8,256]{2,1,0:T(8,128)S(1)}, f32[4,144,256]{2,1,0:T(8,128)S(1)}) custom-call(s32[10]{0:T(128)S(1)} %copy-done.1, bf16[512,256]{1,0:T(8,128)(2,1)S(1)} %copy-done.2, bf16[2,1664,128]{2,1,0:T(8,128)(2,1)S(1)} %prepare.1.refs_1_.refs_2_), custom_call_target="tpu_custom_call" | custom-call | flops 2000000000 | bytes 1024 | tf_op jit(solution)/shard_map/cross_first/pallas_call | solution.py:239
  17.6 0.7 %collective-permute-start.1 = (bf16[512,256]{1,0:T(8,128)(2,1)S(1)}, bf16[512,256]{1,0:T(8,128)(2,1)S(1)}, u32[]{:S(2)}, u32[]{:S(2)}) collective-permute-start(bf16[512,256]{1,0:T(8,128)(2,1)S(1)} %copy-done.2), channel_id=1, source_target_pairs={{1,2},{2,1},{5,6},{6,5},{9,10},{10,9},{13,14},{14,13},{17,18},{18,... | collective-permute-start | bytes 786440 | tf_op jit(solution)/shard_map/ppermute | solution.py:426
  18.3 1.3 %collective-permute-done.2.refs_0_ = bf16[512,256]{1,0:T(8,128)(2,1)} collective-permute-done((bf16[512,256]{1,0:T(8,128)(2,1)S(1)}, bf16[512,256]{1,0:T(8,128)(2,1)}, u32[]{:S(2)}, u32[]{:S(2)}) %collective-permute-start.2) | collective-permute-done | bytes 262176 | tf_op jit(solution)/shard_map/ppermute | solution.py:422
  19.6 1.3 %collective-permute-start.4 = (bf16[512,256]{1,0:T(8,128)(2,1)}, bf16[512,256]{1,0:T(8,128)(2,1)S(1)}, u32[]{:S(2)}, u32[]{:S(2)}) collective-permute-start(bf16[512,256]{1,0:T(8,128)(2,1)} %collective-permute-done.2.refs_0_), channel_id=1, source_target_pairs={{2,3},{1,0},{6,7},{5,4},{10,11},{9,8},{14,15},{13,12},{18,19},{17,... | collective-permute-start | bytes 786440 | tf_op jit(solution)/shard_map/ppermute | solution.py:426
  20.9 3.3 %cross_first.3 = (f32[4,8,256]{2,1,0:T(8,128)S(1)}, f32[4,144,256]{2,1,0:T(8,128)S(1)}) custom-call(s32[10]{0:T(128)S(1)} %copy-done.1, bf16[512,256]{1,0:T(8,128)(2,1)} %collective-permute-done.2.refs_0_, bf16[2,1664,128]{2,1,0:T(8,128)(2,1)S(1)} %prepare.1.refs_1_.refs_2_), custom_call_target="tpu_custom_call" | custom-call | flops 2000000000 | bytes 1024 | tf_op jit(solution)/shard_map/cross_first/pallas_call | solution.py:239
  24.2 0.0 collective-permute-done.3.refs_1_.refs_3_.refs_2_
  24.2 1.3 %cross_last.4 = bf16[528,256]{1,0:T(8,128)(2,1)S(1)} custom-call(s32[10]{0:T(128)S(1)} %copy-done.1, bf16[512,256]{1,0:T(8,128)(2,1)} %collective-permute-done.2.refs_0_, bf16[2,1664,128]{2,1,0:T(8,128)(2,1)S(1)} %collective-permute-done.3.refs_1_.refs_3_.refs_2_, f32[4,8,256]{2,1,0:T(8,128)S(1)} %get-tuple-element.30.refs_2_, ...), custom_call_target="tpu_custom_call" | custom-call | flops 2000000000 | bytes 1024 | tf_op jit(solution)/shard_map/cross_last/pallas_call | solution.py:239
  25.5 4.8 %collective-permute-start.6 = (bf16[528,256]{1,0:T(8,128)(2,1)S(1)}, bf16[528,256]{1,0:T(8,128)(2,1)S(1)}, u32[]{:S(2)}, u32[]{:S(2)}) collective-permute-start(bf16[528,256]{1,0:T(8,128)(2,1)S(1)} %cross_last.4), channel_id=1, source_target_pairs={{0,2},{1,3},{2,0},{3,1},{4,6},{5,7},{6,4},{7,5},{8,10},{9,11},{10,... | collective-permute-start | bytes 811016 | tf_op jit(solution)/shard_map/ppermute | solution.py:422
  30.3 0.0 collective-permute-done.4.refs_1_
  30.3 0.0 collective-permute-done.1.refs_0_
  30.3 3.0 %cross_last.5 = bf16[528,256]{1,0:T(8,128)(2,1)S(1)} custom-call(s32[10]{0:T(128)S(1)} %copy-done.1, bf16[512,256]{1,0:T(8,128)(2,1)S(1)} %collective-permute-done.1.refs_0_, bf16[512,256]{1,0:T(8,128)(2,1)S(1)} %collective-permute-done.4.refs_1_, bf16[2,1664,128]{2,1,0:T(8,128)(2,1)S(1)} %prepare.1.refs_1_.refs_2_, ...), custom_call_target="tpu_custom_call" | custom-call | flops 2000000000 | bytes 1024 | tf_op jit(solution)/shard_map/cross_last/pallas_call | solution.py:239
  33.3 5.0 %collective-permute-start.7 = (bf16[528,256]{1,0:T(8,128)(2,1)S(1)}, bf16[528,256]{1,0:T(8,128)(2,1)S(1)}, u32[]{:S(2)}, u32[]{:S(2)}) collective-permute-start(bf16[528,256]{1,0:T(8,128)(2,1)S(1)} %cross_last.5), channel_id=1, source_target_pairs={{0,3},{1,2},{2,1},{3,0},{4,7},{5,6},{6,5},{7,4},{8,11},{9,10},{10,... | collective-permute-start | bytes 811016 | tf_op jit(solution)/shard_map/ppermute | solution.py:422
  38.2 0.0 collective-permute-done.refs_0_
  38.2 3.2 %collective-permute-start.5 = (bf16[512,256]{1,0:T(8,128)(2,1)S(1)}, bf16[512,256]{1,0:T(8,128)(2,1)S(1)}, u32[]{:S(2)}, u32[]{:S(2)}) collective-permute-start(bf16[512,256]{1,0:T(8,128)(2,1)S(1)} %bitcast.10), channel_id=1, source_target_pairs={{0,16},{1,17},{2,18},{3,19},{4,20},{5,21},{6,22},{7,23},{8,24},{9,... | collective-permute-start | bytes 786440 | tf_op jit(solution)/shard_map/ppermute | solution.py:456
  41.5 3.0 %cross_last.6 = bf16[528,256]{1,0:T(8,128)(2,1)S(1)} custom-call(s32[10]{0:T(128)S(1)} %copy-done.1, bf16[512,256]{1,0:T(8,128)(2,1)S(1)} %collective-permute-done.refs_0_, bf16[2,1664,128]{2,1,0:T(8,128)(2,1)S(1)} %prepare.1.refs_1_.refs_2_, bf16[2,1664,128]{2,1,0:T(8,128)(2,1)S(1)} %collective-permute-done.3.refs_1_.refs_3_.refs_2_), custom_call_target="tpu_custom_call" | custom-call | flops 2000000000 | bytes 1024 | tf_op jit(solution)/shard_map/cross_last/pallas_call | solution.py:239
  44.4 0.1 collective-permute-start.8
  44.5 0.9 %cross_last.7.refs_0_ = bf16[528,256]{1,0:T(8,128)(2,1)S(1)} custom-call(s32[10]{0:T(128)S(1)} %copy-done.1, bf16[512,256]{1,0:T(8,128)(2,1)S(1)} %copy-done.2, bf16[2,1664,128]{2,1,0:T(8,128)(2,1)S(1)} %collective-permute-done.3.refs_1_.refs_3_.refs_2_, f32[4,8,256]{2,1,0:T(8,128)S(1)} %get-tuple-element.26.refs_2_, ...), custom_call_target="tpu_custom_call" | custom-call | flops 2000000000 | bytes 1024 | tf_op jit(solution)/shard_map/cross_last/pallas_call | solution.py:239
  45.4 0.4 collective-permute-done.5.refs_0_
  45.8 0.9 %self_last.1 = bf16[512,256]{1,0:T(8,128)(2,1)} custom-call(s32[1]{0:T(128)} %bitcast.position_ref, bf16[512,256]{1,0:T(8,128)(2,1)S(1)} %copy-done, f32[2,8,512]{2,1,0:T(8,128)S(1)} %get-tuple-element.23.high_ref, f32[2,144,512]{2,1,0:T(8,128)S(1)} %get-tuple-element.24.mixed_ref, bf16[512,256]{1,0:T(8,128)(2,1)S(1)} %collective-permute-done.5.refs_0_), custom_call_target="tpu_custom_call" | custom-call | bytes 1024 | tf_op jit(solution)/shard_map/self_last/pallas_call | solution.py:403
  46.7 0.7 %collective-permute-done.6.refs_1_ = bf16[528,256]{1,0:T(8,128)(2,1)S(1)} collective-permute-done((bf16[528,256]{1,0:T(8,128)(2,1)S(1)}, bf16[528,256]{1,0:T(8,128)(2,1)S(1)}, u32[]{:S(2)}, u32[]{:S(2)}) %collective-permute-start.6) | collective-permute-done | bytes 270368 | tf_op jit(solution)/shard_map/ppermute | solution.py:422
  47.3 0.1 combine.2
  47.4 0.0 collective-permute-done.7.refs_2_
  47.5 0.1 combine.3
  47.6 5.4 %collective-permute-done.8.refs_2_ = bf16[528,256]{1,0:T(8,128)(2,1)S(1)} collective-permute-done((bf16[528,256]{1,0:T(8,128)(2,1)S(1)}, bf16[528,256]{1,0:T(8,128)(2,1)S(1)}, u32[]{:S(2)}, u32[]{:S(2)}) %collective-permute-start.8) | collective-permute-done | bytes 270368 | tf_op jit(solution)/shard_map/ppermute | solution.py:422
  53.0 0.9 %combine_last.1 = bf16[512,256]{1,0:T(8,128)(2,1)} custom-call(f32[512,256]{1,0:T(8,128)S(1)} %get-tuple-element.42.refs_0_, f32[4,256]{1,0:T(4,128)S(1)} %get-tuple-element.43.refs_1_, bf16[528,256]{1,0:T(8,128)(2,1)S(1)} %collective-permute-done.8.refs_2_), custom_call_target="tpu_custom_call" | custom-call | flops 2000000000 | bytes 1024 | tf_op jit(solution)/shard_map/combine_last/pallas_call | solution.py:314
  (1 shorter events, 0.0 us)
Async XLA Ops:
  1.9 3.2 %copy-start.2 = (bf16[512,256]{1,0:T(8,128)(2,1)S(1)}, bf16[512,256]{1,0:T(8,128)(2,1)}, u32[]{:S(2)}) copy-start(bf16[512,256]{1,0:T(8,128)(2,1)} %refs_0_.1) | copy-start | bytes 786436
  1.9 7.4 %copy-start.3 = (bf16[512,2,128]{2,1,0:T(2,128)(2,1)S(1)}, bf16[512,2,128]{2,1,0:T(2,128)(2,1)}, u32[]{:S(2)}) copy-start(bf16[512,2,128]{2,1,0:T(2,128)(2,1)} %param.7) | copy-start | bytes 786436
  2.1 22.1 %collective-permute-start.3 = (bf16[2,1664,128]{2,1,0:T(8,128)(2,1)S(1)}, bf16[2,1664,128]{2,1,0:T(8,128)(2,1)S(1)}, u32[]{:S(2)}, u32[]{:S(2)}) collective-permute-start(bf16[2,1664,128]{2,1,0:T(8,128)(2,1)S(1)} %prepare.1.refs_1_.refs_2_), channel_id=1, source_target_pairs={{0,16},{16,0},{1,17},{17,1},{2,18},{18,2},{3,19},{19,3},{4,20},{20... | collective-permute-start | bytes 2555912 | tf_op jit(solution)/shard_map/ppermute | solution.py:418
  5.1 14.5 %collective-permute-start.2 = (bf16[512,256]{1,0:T(8,128)(2,1)S(1)}, bf16[512,256]{1,0:T(8,128)(2,1)}, u32[]{:S(2)}, u32[]{:S(2)}) collective-permute-start(bf16[512,256]{1,0:T(8,128)(2,1)S(1)} %copy-done.2), channel_id=1, source_target_pairs={{0,2},{1,3},{2,0},{3,1},{4,6},{5,7},{6,4},{7,5},{8,10},{9,11},{10,... | collective-permute-start | bytes 786440 | tf_op jit(solution)/shard_map/ppermute | solution.py:422
  7.7 30.5 %collective-permute-start = (bf16[512,256]{1,0:T(8,128)(2,1)S(1)}, bf16[512,256]{1,0:T(8,128)(2,1)S(1)}, u32[]{:S(2)}, u32[]{:S(2)}) collective-permute-start(bf16[512,256]{1,0:T(8,128)(2,1)S(1)} %copy-done.2), channel_id=1, source_target_pairs={{0,1},{1,0},{2,3},{3,2},{4,5},{5,4},{6,7},{7,6},{8,9},{9,8},{10,11... | collective-permute-start | bytes 786440 | tf_op jit(solution)/shard_map/ppermute | solution.py:422
  9.3 1.0 %copy-start = (bf16[512,256]{1,0:T(8,128)(2,1)S(1)}, bf16[512,256]{1,0:T(8,128)(2,1)}, u32[]{:S(2)}) copy-start(bf16[512,256]{1,0:T(8,128)(2,1)} %q_ref.2) | copy-start | bytes 786436
  11.3 0.7 %copy-start.4 = (s32[4,2]{0,1:T(2,128)S(1)}, s32[4,2]{0,1:T(2,128)}, u32[]{:S(2)}) copy-start(s32[4,2]{0,1:T(2,128)} %param.10) | copy-start | bytes 100
  14.0 0.7 %copy-start.1 = (s32[10]{0:T(128)S(1)}, s32[10]{0:T(128)}, u32[]{:S(2)}) copy-start(s32[10]{0:T(128)} %seen_table.1.table_ref) | copy-start | bytes 124
  17.6 12.7 %collective-permute-start.1 = (bf16[512,256]{1,0:T(8,128)(2,1)S(1)}, bf16[512,256]{1,0:T(8,128)(2,1)S(1)}, u32[]{:S(2)}, u32[]{:S(2)}) collective-permute-start(bf16[512,256]{1,0:T(8,128)(2,1)S(1)} %copy-done.2), channel_id=1, source_target_pairs={{1,2},{2,1},{5,6},{6,5},{9,10},{10,9},{13,14},{14,13},{17,18},{18,... | collective-permute-start | bytes 786440 | tf_op jit(solution)/shard_map/ppermute | solution.py:426
  19.6 10.7 %collective-permute-start.4 = (bf16[512,256]{1,0:T(8,128)(2,1)}, bf16[512,256]{1,0:T(8,128)(2,1)S(1)}, u32[]{:S(2)}, u32[]{:S(2)}) collective-permute-start(bf16[512,256]{1,0:T(8,128)(2,1)} %collective-permute-done.2.refs_0_), channel_id=1, source_target_pairs={{2,3},{1,0},{6,7},{5,4},{10,11},{9,8},{14,15},{13,12},{18,19},{17,... | collective-permute-start | bytes 786440 | tf_op jit(solution)/shard_map/ppermute | solution.py:426
  25.5 21.8 %collective-permute-start.6 = (bf16[528,256]{1,0:T(8,128)(2,1)S(1)}, bf16[528,256]{1,0:T(8,128)(2,1)S(1)}, u32[]{:S(2)}, u32[]{:S(2)}) collective-permute-start(bf16[528,256]{1,0:T(8,128)(2,1)S(1)} %cross_last.4), channel_id=1, source_target_pairs={{0,2},{1,3},{2,0},{3,1},{4,6},{5,7},{6,4},{7,5},{8,10},{9,11},{10,... | collective-permute-start | bytes 811016 | tf_op jit(solution)/shard_map/ppermute | solution.py:422
  33.3 14.2 %collective-permute-start.7 = (bf16[528,256]{1,0:T(8,128)(2,1)S(1)}, bf16[528,256]{1,0:T(8,128)(2,1)S(1)}, u32[]{:S(2)}, u32[]{:S(2)}) collective-permute-start(bf16[528,256]{1,0:T(8,128)(2,1)S(1)} %cross_last.5), channel_id=1, source_target_pairs={{0,3},{1,2},{2,1},{3,0},{4,7},{5,6},{6,5},{7,4},{8,11},{9,10},{10,... | collective-permute-start | bytes 811016 | tf_op jit(solution)/shard_map/ppermute | solution.py:422
  38.2 7.6 %collective-permute-start.5 = (bf16[512,256]{1,0:T(8,128)(2,1)S(1)}, bf16[512,256]{1,0:T(8,128)(2,1)S(1)}, u32[]{:S(2)}, u32[]{:S(2)}) collective-permute-start(bf16[512,256]{1,0:T(8,128)(2,1)S(1)} %bitcast.10), channel_id=1, source_target_pairs={{0,16},{1,17},{2,18},{3,19},{4,20},{5,21},{6,22},{7,23},{8,24},{9,... | collective-permute-start | bytes 786440 | tf_op jit(solution)/shard_map/ppermute | solution.py:456
  44.4 8.6 %collective-permute-start.8 = (bf16[528,256]{1,0:T(8,128)(2,1)S(1)}, bf16[528,256]{1,0:T(8,128)(2,1)S(1)}, u32[]{:S(2)}, u32[]{:S(2)}) collective-permute-start(bf16[528,256]{1,0:T(8,128)(2,1)S(1)} %cross_last.6), channel_id=1, source_target_pairs={{0,1},{1,0},{2,3},{3,2},{4,5},{5,4},{6,7},{7,6},{8,9},{9,8},{10,11... | collective-permute-start | bytes 811016 | tf_op jit(solution)/shard_map/ppermute | solution.py:422

commit v2 on v1

--- a/solution.py
+++ b/solution.py
@@ -115,13 +115,14 @@
 
             count = count + jnp.where(seen > 0, 1, 0)
         table_ref[base] = count
+    table_ref[slots * (block_count + 1)] = position_ref[1]
 
 
 def seen_table(position, block_images, image_owner):
     block_count, slots = block_images.shape
     return pl.pallas_call(
         table_kernel,
-        out_shape=jax.ShapeDtypeStruct((slots * (block_count + 1),), jnp.int32),
+        out_shape=jax.ShapeDtypeStruct((slots * (block_count + 1) + 1,), jnp.int32),
         in_specs=[SMEM] * 3,
         out_specs=SMEM,
         name="seen_table",
@@ -148,7 +149,10 @@
 
     def fold_pair(blocks, image, exact):
         width = image.shape[1]
-        queries = [functools.reduce(jnp.add, [q[at_block(block), :] for q in q_refs]) for block in blocks]
+        queries = [q_refs[0][at_block(block), :] for block in blocks]
+        if parts > 1:
+            first = table_ref[table_ref.shape[0] - 1] > 0
+            queries = [jnp.where(first, one, q_refs[1][at_block(block), :]) for one, block in zip(queries, blocks)]
         queries = jnp.concatenate([stacked_heads(one) for one in queries], axis=0)
         chunks = chunks_of(width)
 
@@ -422,10 +426,6 @@
     return lax.ppermute(value, axis, [(source, source ^ bits) for source in range(lax.axis_size(axis))])
 
 
-def moved(value, pairs):
-    return lax.ppermute(value, "enc", pairs)
-
-
 def after(value, earlier):
     return lax.optimization_barrier((value, earlier))[0]
 
@@ -437,13 +437,17 @@
     key_count = image_kv.shape[2]
     cycle = lax.axis_size("blk")
     ring = lax.axis_size("enc")
-    position = lax.axis_index("blk").astype(jnp.int32)[None]
+    place = lax.axis_index("enc")
+    inside = (place > 0) & (place < ring - 1)
+    position = jnp.stack([lax.axis_index("blk"), inside]).astype(jnp.int32)
 
     images = [prepare(image_kv[0])]
     for _ in range(1, cycle):
         images.append(shifted(images[-1], "blk", 1))
     if ring == 4:
         queries = {step: [swapped(cross_queries, "enc", step)] for step in (2, 1)}
+        middle = lax.ppermute(cross_queries, "enc", [(0, 0), (1, 2), (2, 1), (3, 3)])
+        queries[3] = [middle, swapped(queries[2][0], "enc", 1)]
     else:
         queries = {step: [shifted(cross_queries, "enc", ring - step)] for step in range(1, ring)}
     queries[0] = [cross_queries]
@@ -453,7 +457,7 @@
     texts = []
     onward = after(text, images[-1])
     for _ in range(1, cycle):
-        onward = lax.ppermute(onward, "blk", [(source, source + 1) for source in range(cycle - 1)])
+        onward = shifted(onward, "blk", 1)
         texts.append(onward)
 
     latest = [None]
@@ -475,10 +479,6 @@
     split = cycle > 1
     self_state = latest[0] = self_first(self_queries, text)
     own = begun(0) if split else None
-    if ring == 4:
-        middle = moved(in_turn([cross_queries])[0], [(1, 2), (2, 1)])
-        ends = moved(queries[2][0], [(2, 3), (1, 0)])
-        queries[3] = [middle, ends]
     steps = [2, 3, 1] if ring == 4 else list(range(1, ring))
     states = {step: begun(step) for step in steps[:1]} if split else {}
     received = []

time: 54.4 us -> 54.5 us (level)
  Pallas kernels: 18.9 us -> 24.1 us
  starting transfers between devices: 22.2 us -> 17.4 us
  waiting for transfers between devices: 7.84 us -> 6.95 us
  other arithmetic: 0 us -> 0.61 us
    pallas_call x6, Pallas kernels: 14.3 us -> 18.9 us  [cross_part(): pl.pallas_call(functools.partial(cross_kernel, key_count, len(images), of...]
    ppermute x3 -> x1, starting transfers between devices: 5.21 us -> 1.34 us  [per_device(): lax.ppermute(cross_queries, 'enc', [(0, 0), (1, 2), (2, 1), (3, 3)])]
    ppermute x5 -> x6, starting transfers between devices: 14 us -> 10.3 us  [swapped(): lax.ppermute(value, axis, [(source, source ^ bits) for source in range(la...]
    ppermute x1 -> x2, starting transfers between devices: 3 us -> 5.74 us  [shifted(): lax.ppermute(value, axis, [(source, (source + steps) % count) for source...]
    another operation x0 -> x1, other arithmetic: none -> 0.61 us  [per_device(): position = jnp.stack([lax.axis_index('blk'), inside]).astype(jnp.int32)]
    ppermute x5 -> x6, waiting for transfers between devices: 7.43 us -> 6.94 us  [swapped(): lax.ppermute(value, axis, [(source, source ^ bits) for source in range(la...]
    unnamed x13 -> x15, local copies, waits for them, and re-layouts: 4.2 us -> 4.21 us
  transfers between devices with their start and end apart: 9 -> 9, of which waited for: 4 -> 3; matrix products, arithmetic and copies ran while one was open for 1% -> 2% of each run, Pallas kernels for 33% -> 43%
where the time goes in v2:
time: 54.5 us; the launch traced here: 54 us
  Pallas kernels  24.1 us (44%)
  starting transfers between devices  17.4 us (32%)
  waiting for transfers between devices  6.95 us (13%)
  local copies, waits for them, and re-layouts  4.21 us (8%)
  between operations  0.78 us (1%)
  other arithmetic  0.61 us (1%)
    pallas_call x6, Pallas kernels, cross_part(): pl.pallas_call(functools.partial(cross_kernel, key_count, len(images), of...  18.9 us
    ppermute x6, starting transfers between devices, swapped(): lax.ppermute(value, axis, [(source, source ^ bits) for source in range(la...  10.3 us
    ppermute x6, waiting for transfers between devices, swapped(): lax.ppermute(value, axis, [(source, source ^ bits) for source in range(la...  6.94 us
    ppermute x2, starting transfers between devices, shifted(): lax.ppermute(value, axis, [(source, (source + steps) % count) for source...  5.74 us
    unnamed x15, local copies, waits for them, and re-layouts  4.21 us
    pallas_call x1, Pallas kernels, self_last(): pl.pallas_call(functools.partial(self_last_kernel, group, len(texts)), ou...  1.43 us
    pallas_call x1, Pallas kernels, seen_table(): pl.pallas_call(table_kernel, out_shape=jax.ShapeDtypeStruct((slots * (blo...  1.36 us
    ppermute x1, starting transfers between devices, per_device(): lax.ppermute(cross_queries, 'enc', [(0, 0), (1, 2), (2, 1), (3, 3)])  1.34 us
  transfers between devices with their start and end apart: 9, of which 3 were waited for; matrix products, arithmetic and copies ran while one was open for 2% of the time, Pallas kernels for 43%

profile of v2, /device:TPU:0, one launch (start us, length us, event | category | flops | bytes accessed | tf_op | source)
XLA Modules:
  0.0 54.0 jit_solution(7616640163855267158)
XLA Ops:
  0.6 1.3 %copy.13 = bf16[1,2,1601,128]{3,2,1,0:T(8,128)(2,1)S(1)} copy(bf16[1,2,1601,128]{3,1,2,0:T(2,128)(2,1)} %param.9) | data formatting | bytes 1639424 | tf_op args[3]
  1.9 0.0 copy-start.3
  1.9 0.0 copy-start.4
  1.9 0.2 prepare.1.refs_1_.refs_2_
  2.1 3.0 %collective-permute-start.3 = (bf16[2,1664,128]{2,1,0:T(8,128)(2,1)S(1)}, bf16[2,1664,128]{2,1,0:T(8,128)(2,1)S(1)}, u32[]{:S(2)}, u32[]{:S(2)}) collective-permute-start(bf16[2,1664,128]{2,1,0:T(8,128)(2,1)S(1)} %prepare.1.refs_1_.refs_2_), channel_id=1, source_target_pairs={{0,16},{16,0},{1,17},{17,1},{2,18},{18,2},{3,19},{19,3},{4,20},{20... | collective-permute-start | bytes 2555912 | tf_op jit(solution)/shard_map/ppermute | solution.py:422
  5.1 0.0 copy-done.3
  5.1 2.6 %collective-permute-start.2 = (bf16[512,256]{1,0:T(8,128)(2,1)S(1)}, bf16[512,256]{1,0:T(8,128)(2,1)}, u32[]{:S(2)}, u32[]{:S(2)}) collective-permute-start(bf16[512,256]{1,0:T(8,128)(2,1)S(1)} %copy-done.3), channel_id=1, source_target_pairs={{0,2},{1,3},{2,0},{3,1},{4,6},{5,7},{6,4},{7,5},{8,10},{9,11},{10,... | collective-permute-start | bytes 786440 | tf_op jit(solution)/shard_map/ppermute | solution.py:426
  7.7 1.3 %collective-permute-start.1 = (bf16[512,256]{1,0:T(8,128)(2,1)S(1)}, bf16[512,256]{1,0:T(8,128)(2,1)}, u32[]{:S(2)}, u32[]{:S(2)}) collective-permute-start(bf16[512,256]{1,0:T(8,128)(2,1)S(1)} %copy-done.3), channel_id=1, source_target_pairs={{0,0},{1,2},{2,1},{3,3},{4,4},{5,6},{6,5},{7,7},{8,8},{9,10},{10,9... | collective-permute-start | bytes 786440 | tf_op jit(solution)/shard_map/ppermute | solution.py:449
  9.0 2.2 %collective-permute-start = (bf16[512,256]{1,0:T(8,128)(2,1)S(1)}, bf16[512,256]{1,0:T(8,128)(2,1)S(1)}, u32[]{:S(2)}, u32[]{:S(2)}) collective-permute-start(bf16[512,256]{1,0:T(8,128)(2,1)S(1)} %copy-done.3), channel_id=1, source_target_pairs={{0,1},{1,0},{2,3},{3,2},{4,5},{5,4},{6,7},{7,6},{8,9},{9,8},{10,11... | collective-permute-start | bytes 786440 | tf_op jit(solution)/shard_map/ppermute | solution.py:426
  11.3 0.0 copy-start.5
  11.3 0.7 %copy-done.5 = s32[4,2]{0,1:T(2,128)S(1)} copy-done((s32[4,2]{0,1:T(2,128)S(1)}, s32[4,2]{0,1:T(2,128)}, u32[]{:S(2)}) %copy-start.5) | copy-done | bytes 56
  11.9 0.7 %copy.8.images_ref = s32[4,2]{1,0:T(4,128)} copy(s32[4,2]{0,1:T(2,128)S(1)} %copy-done.5) | data formatting | bytes 64 | tf_op args[4]
  12.6 0.0 copy-done.4
  12.6 0.0 copy-start
  12.6 0.9 %copy-done = bf16[512,256]{1,0:T(8,128)(2,1)S(1)} copy-done((bf16[512,256]{1,0:T(8,128)(2,1)S(1)}, bf16[512,256]{1,0:T(8,128)(2,1)}, u32[]{:S(2)}) %copy-start) | copy-done | bytes 262168
  13.6 1.1 %self_first.1 = (f32[2,8,512]{2,1,0:T(8,128)S(1)}, f32[2,144,512]{2,1,0:T(8,128)S(1)}) custom-call(bf16[512,256]{1,0:T(8,128)(2,1)S(1)} %copy-done, bf16[512,256]{1,0:T(8,128)(2,1)S(1)} %bitcast.10), custom_call_target="tpu_custom_call" | custom-call | bytes 1024 | tf_op jit(solution)/shard_map/self_first/pallas_call | solution.py:389
  14.6 0.6 %pad_add_fusion.position_ref = s32[2]{0:T(128)} fusion(s32[1]{0:T(128)} %bitcast.1, s32[1]{0:T(128)} %bitcast), kind=kLoop, calls=%fused_computation.2 | loop fusion | flops 2 | bytes 16 | tf_op jit(solution)/shard_map/stack | solution.py:442
  15.3 1.4 %seen_table.1.table_ref = s32[11]{0:T(128)} custom-call(s32[2]{0:T(128)} %pad_add_fusion.position_ref, s32[4,2]{1,0:T(4,128)} %copy.8.images_ref, s32[2]{0:T(128)} %owner_ref.1), custom_call_target="tpu_custom_call" | custom-call | tf_op jit(solution)/shard_map/seen_table/pallas_call | solution.py:123
  16.6 0.0 copy-start.2
  16.6 0.6 %copy-done.2 = s32[11]{0:T(128)S(1)} copy-done((s32[11]{0:T(128)S(1)}, s32[11]{0:T(128)}, u32[]{:S(2)}) %copy-start.2) | copy-done | bytes 68
  17.3 2.9 %cross_first.2 = (f32[4,8,256]{2,1,0:T(8,128)S(1)}, f32[4,144,256]{2,1,0:T(8,128)S(1)}) custom-call(s32[11]{0:T(128)S(1)} %copy-done.2, bf16[512,256]{1,0:T(8,128)(2,1)S(1)} %copy-done.3, bf16[2,1664,128]{2,1,0:T(8,128)(2,1)S(1)} %prepare.1.refs_1_.refs_2_), custom_call_target="tpu_custom_call" | custom-call | flops 2000000000 | bytes 1024 | tf_op jit(solution)/shard_map/cross_first/pallas_call | solution.py:243
  20.2 0.5 collective-permute-done.2.refs_0_
  20.7 0.0 collective-permute-start.4
  20.7 3.4 %cross_first.3 = (f32[4,8,256]{2,1,0:T(8,128)S(1)}, f32[4,144,256]{2,1,0:T(8,128)S(1)}) custom-call(s32[11]{0:T(128)S(1)} %copy-done.2, bf16[512,256]{1,0:T(8,128)(2,1)} %collective-permute-done.2.refs_0_, bf16[2,1664,128]{2,1,0:T(8,128)(2,1)S(1)} %prepare.1.refs_1_.refs_2_), custom_call_target="tpu_custom_call" | custom-call | flops 2000000000 | bytes 1024 | tf_op jit(solution)/shard_map/cross_first/pallas_call | solution.py:243
  24.1 0.0 collective-permute-done.3.refs_1_.refs_3_.refs_2_
  24.1 2.3 %cross_last.4 = bf16[528,256]{1,0:T(8,128)(2,1)S(1)} custom-call(s32[11]{0:T(128)S(1)} %copy-done.2, bf16[512,256]{1,0:T(8,128)(2,1)} %collective-permute-done.2.refs_0_, bf16[2,1664,128]{2,1,0:T(8,128)(2,1)S(1)} %collective-permute-done.3.refs_1_.refs_3_.refs_2_, f32[4,8,256]{2,1,0:T(8,128)S(1)} %get-tuple-element.28.refs_2_, ...), custom_call_target="tpu_custom_call" | custom-call | flops 2000000000 | bytes 1024 | tf_op jit(solution)/shard_map/cross_last/pallas_call | solution.py:243
  26.4 3.1 %collective-permute-start.6 = (bf16[528,256]{1,0:T(8,128)(2,1)S(1)}, bf16[528,256]{1,0:T(8,128)(2,1)S(1)}, u32[]{:S(2)}, u32[]{:S(2)}) collective-permute-start(bf16[528,256]{1,0:T(8,128)(2,1)S(1)} %cross_last.4), channel_id=1, source_target_pairs={{0,2},{1,3},{2,0},{3,1},{4,6},{5,7},{6,4},{7,5},{8,10},{9,11},{10,... | collective-permute-start | bytes 811016 | tf_op jit(solution)/shard_map/ppermute | solution.py:426
  29.5 0.0 collective-permute-done.4.refs_1_
  29.5 0.0 collective-permute-done.1.refs_0_
  29.5 4.4 %cross_last.5 = bf16[528,256]{1,0:T(8,128)(2,1)S(1)} custom-call(s32[11]{0:T(128)S(1)} %copy-done.2, bf16[512,256]{1,0:T(8,128)(2,1)} %collective-permute-done.1.refs_0_, bf16[512,256]{1,0:T(8,128)(2,1)S(1)} %collective-permute-done.4.refs_1_, bf16[2,1664,128]{2,1,0:T(8,128)(2,1)S(1)} %prepare.1.refs_1_.refs_2_, ...), custom_call_target="tpu_custom_call" | custom-call | flops 2000000000 | bytes 1024 | tf_op jit(solution)/shard_map/cross_last/pallas_call | solution.py:243
  34.0 2.0 %collective-permute-start.7 = (bf16[528,256]{1,0:T(8,128)(2,1)S(1)}, bf16[528,256]{1,0:T(8,128)(2,1)S(1)}, u32[]{:S(2)}, u32[]{:S(2)}) collective-permute-start(bf16[528,256]{1,0:T(8,128)(2,1)S(1)} %cross_last.5), channel_id=1, source_target_pairs={{0,3},{1,2},{2,1},{3,0},{4,7},{5,6},{6,5},{7,4},{8,11},{9,10},{10,... | collective-permute-start | bytes 811016 | tf_op jit(solution)/shard_map/ppermute | solution.py:426
  36.0 0.0 collective-permute-done.refs_0_
  36.0 2.7 %collective-permute-start.5 = (bf16[512,256]{1,0:T(8,128)(2,1)S(1)}, bf16[512,256]{1,0:T(8,128)(2,1)S(1)}, u32[]{:S(2)}, u32[]{:S(2)}) collective-permute-start(bf16[512,256]{1,0:T(8,128)(2,1)S(1)} %bitcast.11), channel_id=1, source_target_pairs={{0,16},{16,0},{1,17},{17,1},{2,18},{18,2},{3,19},{19,3},{4,20},{20... | collective-permute-start | bytes 786440 | tf_op jit(solution)/shard_map/ppermute | solution.py:422
  38.7 4.0 %cross_last.6 = bf16[528,256]{1,0:T(8,128)(2,1)S(1)} custom-call(s32[11]{0:T(128)S(1)} %copy-done.2, bf16[512,256]{1,0:T(8,128)(2,1)S(1)} %collective-permute-done.refs_0_, bf16[2,1664,128]{2,1,0:T(8,128)(2,1)S(1)} %prepare.1.refs_1_.refs_2_, bf16[2,1664,128]{2,1,0:T(8,128)(2,1)S(1)} %collective-permute-done.3.refs_1_.refs_3_.refs_2_), custom_call_target="tpu_custom_call" | custom-call | flops 2000000000 | bytes 1024 | tf_op jit(solution)/shard_map/cross_last/pallas_call | solution.py:243
  42.7 0.0 copy-start.1
  42.7 0.4 collective-permute-start.8
  43.1 1.9 %cross_last.7.refs_0_ = bf16[528,256]{1,0:T(8,128)(2,1)S(1)} custom-call(s32[11]{0:T(128)S(1)} %copy-done.2, bf16[512,256]{1,0:T(8,128)(2,1)S(1)} %copy-done.3, bf16[2,1664,128]{2,1,0:T(8,128)(2,1)S(1)} %collective-permute-done.3.refs_1_.refs_3_.refs_2_, f32[4,8,256]{2,1,0:T(8,128)S(1)} %get-tuple-element.25.refs_2_, ...), custom_call_target="tpu_custom_call" | custom-call | flops 2000000000 | bytes 1024 | tf_op jit(solution)/shard_map/cross_last/pallas_call | solution.py:243
  45.0 0.0 collective-permute-done.5.refs_0_
  45.0 0.0 copy-done.1
  45.0 1.4 %self_last.1 = bf16[512,256]{1,0:T(8,128)(2,1)} custom-call(s32[2]{0:T(128)S(1)} %copy-done.1, bf16[512,256]{1,0:T(8,128)(2,1)S(1)} %copy-done, f32[2,8,512]{2,1,0:T(8,128)S(1)} %get-tuple-element.22.high_ref, f32[2,144,512]{2,1,0:T(8,128)S(1)} %get-tuple-element.23.mixed_ref, bf16[512,256]{1,0:T(8,128)(2,1)S(1)} %collective-permute-done.5.refs_0_), custom_call_target="tpu_custom_call" | custom-call | bytes 1024 | tf_op jit(solution)/shard_map/self_last/pallas_call | solution.py:407
  46.5 1.3 %collective-permute-done.6.refs_1_ = bf16[528,256]{1,0:T(8,128)(2,1)S(1)} collective-permute-done((bf16[528,256]{1,0:T(8,128)(2,1)S(1)}, bf16[528,256]{1,0:T(8,128)(2,1)S(1)}, u32[]{:S(2)}, u32[]{:S(2)}) %collective-permute-start.6) | collective-permute-done | bytes 270368 | tf_op jit(solution)/shard_map/ppermute | solution.py:426
  47.8 0.1 combine.2
  47.9 0.0 collective-permute-done.7.refs_2_
  47.9 0.1 combine.3
  48.0 5.1 %collective-permute-done.8.refs_2_ = bf16[528,256]{1,0:T(8,128)(2,1)S(1)} collective-permute-done((bf16[528,256]{1,0:T(8,128)(2,1)S(1)}, bf16[528,256]{1,0:T(8,128)(2,1)S(1)}, u32[]{:S(2)}, u32[]{:S(2)}) %collective-permute-start.8) | collective-permute-done | bytes 270368 | tf_op jit(solution)/shard_map/ppermute | solution.py:426
  53.1 0.9 %combine_last.1 = bf16[512,256]{1,0:T(8,128)(2,1)} custom-call(f32[512,256]{1,0:T(8,128)S(1)} %get-tuple-element.40.refs_0_, f32[4,256]{1,0:T(4,128)S(1)} %get-tuple-element.41.refs_1_, bf16[528,256]{1,0:T(8,128)(2,1)S(1)} %collective-permute-done.8.refs_2_), custom_call_target="tpu_custom_call" | custom-call | flops 2000000000 | bytes 1024 | tf_op jit(solution)/shard_map/combine_last/pallas_call | solution.py:318
  (1 shorter events, 0.0 us)
Async XLA Ops:
  1.9 3.2 %copy-start.3 = (bf16[512,256]{1,0:T(8,128)(2,1)S(1)}, bf16[512,256]{1,0:T(8,128)(2,1)}, u32[]{:S(2)}) copy-start(bf16[512,256]{1,0:T(8,128)(2,1)} %refs_0_.1) | copy-start | bytes 786436
  1.9 10.7 %copy-start.4 = (bf16[512,2,128]{2,1,0:T(2,128)(2,1)S(1)}, bf16[512,2,128]{2,1,0:T(2,128)(2,1)}, u32[]{:S(2)}) copy-start(bf16[512,2,128]{2,1,0:T(2,128)(2,1)} %param.7) | copy-start | bytes 786436
  2.1 22.0 %collective-permute-start.3 = (bf16[2,1664,128]{2,1,0:T(8,128)(2,1)S(1)}, bf16[2,1664,128]{2,1,0:T(8,128)(2,1)S(1)}, u32[]{:S(2)}, u32[]{:S(2)}) collective-permute-start(bf16[2,1664,128]{2,1,0:T(8,128)(2,1)S(1)} %prepare.1.refs_1_.refs_2_), channel_id=1, source_target_pairs={{0,16},{16,0},{1,17},{17,1},{2,18},{18,2},{3,19},{19,3},{4,20},{20... | collective-permute-start | bytes 2555912 | tf_op jit(solution)/shard_map/ppermute | solution.py:422
  5.1 15.6 %collective-permute-start.2 = (bf16[512,256]{1,0:T(8,128)(2,1)S(1)}, bf16[512,256]{1,0:T(8,128)(2,1)}, u32[]{:S(2)}, u32[]{:S(2)}) collective-permute-start(bf16[512,256]{1,0:T(8,128)(2,1)S(1)} %copy-done.3), channel_id=1, source_target_pairs={{0,2},{1,3},{2,0},{3,1},{4,6},{5,7},{6,4},{7,5},{8,10},{9,11},{10,... | collective-permute-start | bytes 786440 | tf_op jit(solution)/shard_map/ppermute | solution.py:426
  7.7 21.8 %collective-permute-start.1 = (bf16[512,256]{1,0:T(8,128)(2,1)S(1)}, bf16[512,256]{1,0:T(8,128)(2,1)}, u32[]{:S(2)}, u32[]{:S(2)}) collective-permute-start(bf16[512,256]{1,0:T(8,128)(2,1)S(1)} %copy-done.3), channel_id=1, source_target_pairs={{0,0},{1,2},{2,1},{3,3},{4,4},{5,6},{6,5},{7,7},{8,8},{9,10},{10,9... | collective-permute-start | bytes 786440 | tf_op jit(solution)/shard_map/ppermute | solution.py:449
  9.0 27.0 %collective-permute-start = (bf16[512,256]{1,0:T(8,128)(2,1)S(1)}, bf16[512,256]{1,0:T(8,128)(2,1)S(1)}, u32[]{:S(2)}, u32[]{:S(2)}) collective-permute-start(bf16[512,256]{1,0:T(8,128)(2,1)S(1)} %copy-done.3), channel_id=1, source_target_pairs={{0,1},{1,0},{2,3},{3,2},{4,5},{5,4},{6,7},{7,6},{8,9},{9,8},{10,11... | collective-permute-start | bytes 786440 | tf_op jit(solution)/shard_map/ppermute | solution.py:426
  11.3 0.7 %copy-start.5 = (s32[4,2]{0,1:T(2,128)S(1)}, s32[4,2]{0,1:T(2,128)}, u32[]{:S(2)}) copy-start(s32[4,2]{0,1:T(2,128)} %param.10) | copy-start | bytes 100
  12.6 1.0 %copy-start = (bf16[512,256]{1,0:T(8,128)(2,1)S(1)}, bf16[512,256]{1,0:T(8,128)(2,1)}, u32[]{:S(2)}) copy-start(bf16[512,256]{1,0:T(8,128)(2,1)} %q_ref.2) | copy-start | bytes 786436
  16.6 0.7 %copy-start.2 = (s32[11]{0:T(128)S(1)}, s32[11]{0:T(128)}, u32[]{:S(2)}) copy-start(s32[11]{0:T(128)} %seen_table.1.table_ref) | copy-start | bytes 136
  20.7 8.8 %collective-permute-start.4 = (bf16[512,256]{1,0:T(8,128)(2,1)}, bf16[512,256]{1,0:T(8,128)(2,1)S(1)}, u32[]{:S(2)}, u32[]{:S(2)}) collective-permute-start(bf16[512,256]{1,0:T(8,128)(2,1)} %collective-permute-done.2.refs_0_), channel_id=1, source_target_pairs={{0,1},{1,0},{2,3},{3,2},{4,5},{5,4},{6,7},{7,6},{8,9},{9,8},{10,11... | collective-permute-start | bytes 786440 | tf_op jit(solution)/shard_map/ppermute | solution.py:426
  26.4 21.4 %collective-permute-start.6 = (bf16[528,256]{1,0:T(8,128)(2,1)S(1)}, bf16[528,256]{1,0:T(8,128)(2,1)S(1)}, u32[]{:S(2)}, u32[]{:S(2)}) collective-permute-start(bf16[528,256]{1,0:T(8,128)(2,1)S(1)} %cross_last.4), channel_id=1, source_target_pairs={{0,2},{1,3},{2,0},{3,1},{4,6},{5,7},{6,4},{7,5},{8,10},{9,11},{10,... | collective-permute-start | bytes 811016 | tf_op jit(solution)/shard_map/ppermute | solution.py:426
  34.0 14.0 %collective-permute-start.7 = (bf16[528,256]{1,0:T(8,128)(2,1)S(1)}, bf16[528,256]{1,0:T(8,128)(2,1)S(1)}, u32[]{:S(2)}, u32[]{:S(2)}) collective-permute-start(bf16[528,256]{1,0:T(8,128)(2,1)S(1)} %cross_last.5), channel_id=1, source_target_pairs={{0,3},{1,2},{2,1},{3,0},{4,7},{5,6},{6,5},{7,4},{8,11},{9,10},{10,... | collective-permute-start | bytes 811016 | tf_op jit(solution)/shard_map/ppermute | solution.py:426
  36.0 9.0 %collective-permute-start.5 = (bf16[512,256]{1,0:T(8,128)(2,1)S(1)}, bf16[512,256]{1,0:T(8,128)(2,1)S(1)}, u32[]{:S(2)}, u32[]{:S(2)}) collective-permute-start(bf16[512,256]{1,0:T(8,128)(2,1)S(1)} %bitcast.11), channel_id=1, source_target_pairs={{0,16},{16,0},{1,17},{17,1},{2,18},{18,2},{3,19},{19,3},{4,20},{20... | collective-permute-start | bytes 786440 | tf_op jit(solution)/shard_map/ppermute | solution.py:422
  42.7 2.3 %copy-start.1 = (s32[2]{0:T(128)S(1)}, s32[2]{0:T(128)}, u32[]{:S(2)}) copy-start(s32[2]{0:T(128)} %pad_add_fusion.position_ref) | copy-start | bytes 28
  42.7 10.4 %collective-permute-start.8 = (bf16[528,256]{1,0:T(8,128)(2,1)S(1)}, bf16[528,256]{1,0:T(8,128)(2,1)S(1)}, u32[]{:S(2)}, u32[]{:S(2)}) collective-permute-start(bf16[528,256]{1,0:T(8,128)(2,1)S(1)} %cross_last.6), channel_id=1, source_target_pairs={{0,1},{1,0},{2,3},{3,2},{4,5},{5,4},{6,7},{7,6},{8,9},{9,8},{10,11... | collective-permute-start | bytes 811016 | tf_op jit(solution)/shard_map/ppermute | solution.py:426

commit v3 on v2

--- a/solution.py
+++ b/solution.py
@@ -147,7 +147,7 @@
     peak_ref[...] = jnp.full_like(peak_ref, LOWEST)
     redo_ref[0] = jnp.int32(0)
 
-    def fold_pair(blocks, image, exact):
+    def fold_pair(blocks, image, exact, held):
         width = image.shape[1]
         queries = [q_refs[0][at_block(block), :] for block in blocks]
         if parts > 1:
@@ -171,8 +171,12 @@
             tops = [jnp.max(scores_of(*chunk), axis=0, keepdims=True) for chunk in chunks]
             peak_ref[0:1, :] = functools.reduce(jnp.maximum, tops)
 
-        high = jnp.concatenate([high_ref[block][0:1] for block in blocks], axis=1)
-        mixed = jnp.concatenate([mixed_ref[block] for block in blocks], axis=1)
+        if held is None:
+            high = jnp.full((1, 2 * rows), LOWEST, jnp.float32)
+            mixed = jnp.zeros((MIXED_ROWS, 2 * rows), jnp.float32)
+        else:
+            high = jnp.concatenate([held[0][block][0:1] for block in blocks], axis=1)
+            mixed = jnp.concatenate([held[1][block] for block in blocks], axis=1)
         scores = scores_of(*chunks[0])
         seen = jnp.max(scores[0 : min(SHIFT_KEYS, scores.shape[0])], axis=0, keepdims=True)
         new_high = jnp.maximum(jnp.maximum(high, seen), peak_ref[0:1, :])
@@ -189,43 +193,57 @@
             high_ref[block] = jnp.broadcast_to(new_high[:, own], high_ref.shape[1:])
             mixed_ref[block] = mixed[:, own]
 
+    def finish():
+        for block in range(block_count):
+            total = mixed_ref[block, HEAD_SIZE : HEAD_SIZE + 1, :]
+            out_ref[block * HEAD_SIZE : (block + 1) * HEAD_SIZE, :] = (
+                mixed_ref[block, 0:HEAD_SIZE, :] * (1.0 / total)
+            ).astype(jnp.bfloat16)
+            lse_ref[block : block + 1, :] = high_ref[block, 0:1, :] * LOG2_SCALE + jnp.log2(total)
+        out_ref[block_count * HEAD_SIZE :, :] = lse_pieces(lse_ref[0:block_count, :], block_count)
+
     def attempt(trial, carry):
         @pl.when((trial == 0) | (redo_ref[0] > 0))
         def _():
-            if offset:
-                high_ref[...] = before[0][...]
-                mixed_ref[...] = before[1][...]
-            else:
-                high_ref[...] = jnp.full_like(high_ref, LOWEST)
-                mixed_ref[...] = jnp.zeros_like(mixed_ref)
             for piece in range(pieces):
                 base = (offset + piece) * (block_count + 1)
                 count = table_ref[base]
-
-                def pair_step(pair, carry, piece=piece, base=base, count=count):
+                if piece == 0:
+                    held = before if offset else None
+                    for block in range(block_count):
+                        seen = functools.reduce(
+                            jnp.logical_or,
+                            [(count > index) & (table_ref[base + 1 + index] == block) for index in range(block_count)],
+                        )
+
+                        @pl.when(jnp.logical_not(seen))
+                        def _(block=block):
+                            if held is None:
+                                high_ref[block] = jnp.full(high_ref.shape[1:], LOWEST, jnp.float32)
+                                mixed_ref[block] = jnp.zeros(mixed_ref.shape[1:], jnp.float32)
+                            else:
+                                high_ref[block] = held[0][block]
+                                mixed_ref[block] = held[1][block]
+
+                else:
+                    held = (high_ref, mixed_ref)
+
+                def pair_step(pair, carry, piece=piece, base=base, count=count, held=held):
                     blocks = [table_ref[base + 1 + 2 * pair], table_ref[base + jnp.minimum(2 * pair + 2, count)]]
-                    fold_pair(blocks, images[piece], trial > 0)
+                    fold_pair(blocks, images[piece], trial > 0, held)
                     return carry
 
                 lax.fori_loop(0, (count + 1) // 2, pair_step, 0)
             most = functools.reduce(
                 jnp.maximum, [mixed_ref[block, HEAD_SIZE : HEAD_SIZE + 1, :] for block in range(block_count)]
             )
+            if last:
+                finish()
             redo_ref[0] = 1 - jnp.min((most <= MOST_SUM).astype(jnp.int32))
 
         return carry
 
     lax.fori_loop(0, 2, attempt, 0)
-
-    if last:
-        lse_ref[...] = jnp.zeros_like(lse_ref)
-        for block in range(block_count):
-            total = mixed_ref[block, HEAD_SIZE : HEAD_SIZE + 1, :]
-            out_ref[block * HEAD_SIZE : (block + 1) * HEAD_SIZE, :] = (
-                mixed_ref[block, 0:HEAD_SIZE, :] / total
-            ).astype(jnp.bfloat16)
-            lse_ref[block : block + 1, :] = high_ref[block, 0:1, :] * LOG2_SCALE + jnp.log2(total)
-        out_ref[block_count * HEAD_SIZE :, :] = lse_pieces(lse_ref[0:block_count, :], block_count)
 
 
 def cross_part(table, queries, images, key_count, offset, last, before=()):

time: 54.5 us -> 54.1 us (level); the launches traced: 54 us -> 54.3 us
  waiting for transfers between devices: 6.95 us -> 13.4 us
  Pallas kernels: 24.1 us -> 19.9 us
  starting transfers between devices: 17.4 us -> 15.3 us
    ppermute x6, waiting for transfers between devices: 6.94 us -> 11.4 us  [swapped(): lax.ppermute(value, axis, [(source, source ^ bits) for source in range(la...]
    pallas_call x6, Pallas kernels: 18.9 us -> 14.8 us  [cross_part(): pl.pallas_call(functools.partial(cross_kernel, key_count, len(images), of...]
    ppermute x2, waiting for transfers between devices: 0.01 us -> 2.03 us  [shifted(): lax.ppermute(value, axis, [(source, (source + steps) % count) for source...]
    ppermute x6, starting transfers between devices: 10.3 us -> 9.19 us  [swapped(): lax.ppermute(value, axis, [(source, source ^ bits) for source in range(la...]
    ppermute x2, starting transfers between devices: 5.74 us -> 4.81 us  [shifted(): lax.ppermute(value, axis, [(source, (source + steps) % count) for source...]
  transfers between devices with their start and end apart: 9 -> 9, of which waited for: 3 -> 4; matrix products, arithmetic and copies ran while one was open for 2% -> 2% of each run, Pallas kernels for 43% -> 35%
where the time goes in v3:
time: 54.1 us; the launch traced here: 54.3 us
  Pallas kernels  19.9 us (37%)
  starting transfers between devices  15.3 us (28%)
  waiting for transfers between devices  13.4 us (25%)
  local copies, waits for them, and re-layouts  4.21 us (8%)
  between operations  0.79 us (1%)
  other arithmetic  0.61 us (1%)
    pallas_call x6, Pallas kernels, cross_part(): pl.pallas_call(functools.partial(cross_kernel, key_count, len(images), of...  14.8 us
    ppermute x6, waiting for transfers between devices, swapped(): lax.ppermute(value, axis, [(source, source ^ bits) for source in range(la...  11.4 us
    ppermute x6, starting transfers between devices, swapped(): lax.ppermute(value, axis, [(source, source ^ bits) for source in range(la...  9.19 us
    ppermute x2, starting transfers between devices, shifted(): lax.ppermute(value, axis, [(source, (source + steps) % count) for source...  4.81 us
    unnamed x15, local copies, waits for them, and re-layouts  4.21 us
    ppermute x2, waiting for transfers between devices, shifted(): lax.ppermute(value, axis, [(source, (source + steps) % count) for source...  2.03 us
    pallas_call x1, Pallas kernels, self_last(): pl.pallas_call(functools.partial(self_last_kernel, group, len(texts)), ou...  1.43 us
    pallas_call x1, Pallas kernels, seen_table(): pl.pallas_call(table_kernel, out_shape=jax.ShapeDtypeStruct((slots * (blo...  1.36 us
  transfers between devices with their start and end apart: 9, of which 4 were waited for; matrix products, arithmetic and copies ran while one was open for 2% of the time, Pallas kernels for 35%

profile of v3, /device:TPU:0, one launch (start us, length us, event | category | flops | bytes accessed | tf_op | source)
XLA Modules:
  0.0 54.3 jit_solution(313839426001035399)
XLA Ops:
  0.6 1.3 %copy.13 = bf16[1,2,1601,128]{3,2,1,0:T(8,128)(2,1)S(1)} copy(bf16[1,2,1601,128]{3,1,2,0:T(2,128)(2,1)} %param.9) | data formatting | bytes 1639424 | tf_op args[3]
  1.9 0.0 copy-start.3
  1.9 0.0 copy-start.4
  1.9 0.2 prepare.1.refs_1_.refs_2_
  2.1 3.0 %collective-permute-start.3 = (bf16[2,1664,128]{2,1,0:T(8,128)(2,1)S(1)}, bf16[2,1664,128]{2,1,0:T(8,128)(2,1)S(1)}, u32[]{:S(2)}, u32[]{:S(2)}) collective-permute-start(bf16[2,1664,128]{2,1,0:T(8,128)(2,1)S(1)} %prepare.1.refs_1_.refs_2_), channel_id=1, source_target_pairs={{0,16},{16,0},{1,17},{17,1},{2,18},{18,2},{3,19},{19,3},{4,20},{20... | collective-permute-start | bytes 2555912 | tf_op jit(solution)/shard_map/ppermute | solution.py:440
  5.1 0.0 copy-done.3
  5.1 2.6 %collective-permute-start.2 = (bf16[512,256]{1,0:T(8,128)(2,1)S(1)}, bf16[512,256]{1,0:T(8,128)(2,1)}, u32[]{:S(2)}, u32[]{:S(2)}) collective-permute-start(bf16[512,256]{1,0:T(8,128)(2,1)S(1)} %copy-done.3), channel_id=1, source_target_pairs={{0,2},{1,3},{2,0},{3,1},{4,6},{5,7},{6,4},{7,5},{8,10},{9,11},{10,... | collective-permute-start | bytes 786440 | tf_op jit(solution)/shard_map/ppermute | solution.py:444
  7.7 1.3 %collective-permute-start.1 = (bf16[512,256]{1,0:T(8,128)(2,1)S(1)}, bf16[512,256]{1,0:T(8,128)(2,1)}, u32[]{:S(2)}, u32[]{:S(2)}) collective-permute-start(bf16[512,256]{1,0:T(8,128)(2,1)S(1)} %copy-done.3), channel_id=1, source_target_pairs={{0,0},{1,2},{2,1},{3,3},{4,4},{5,6},{6,5},{7,7},{8,8},{9,10},{10,9... | collective-permute-start | bytes 786440 | tf_op jit(solution)/shard_map/ppermute | solution.py:467
  9.0 2.2 %collective-permute-start = (bf16[512,256]{1,0:T(8,128)(2,1)S(1)}, bf16[512,256]{1,0:T(8,128)(2,1)S(1)}, u32[]{:S(2)}, u32[]{:S(2)}) collective-permute-start(bf16[512,256]{1,0:T(8,128)(2,1)S(1)} %copy-done.3), channel_id=1, source_target_pairs={{0,1},{1,0},{2,3},{3,2},{4,5},{5,4},{6,7},{7,6},{8,9},{9,8},{10,11... | collective-permute-start | bytes 786440 | tf_op jit(solution)/shard_map/ppermute | solution.py:444
  11.3 0.0 copy-start.5
  11.3 0.7 %copy-done.5 = s32[4,2]{0,1:T(2,128)S(1)} copy-done((s32[4,2]{0,1:T(2,128)S(1)}, s32[4,2]{0,1:T(2,128)}, u32[]{:S(2)}) %copy-start.5) | copy-done | bytes 56
  11.9 0.7 %copy.8.images_ref = s32[4,2]{1,0:T(4,128)} copy(s32[4,2]{0,1:T(2,128)S(1)} %copy-done.5) | data formatting | bytes 64 | tf_op args[4]
  12.6 0.0 copy-done.4
  12.6 0.0 copy-start
  12.6 0.9 %copy-done = bf16[512,256]{1,0:T(8,128)(2,1)S(1)} copy-done((bf16[512,256]{1,0:T(8,128)(2,1)S(1)}, bf16[512,256]{1,0:T(8,128)(2,1)}, u32[]{:S(2)}) %copy-start) | copy-done | bytes 262168
  13.6 1.1 %self_first.1 = (f32[2,8,512]{2,1,0:T(8,128)S(1)}, f32[2,144,512]{2,1,0:T(8,128)S(1)}) custom-call(bf16[512,256]{1,0:T(8,128)(2,1)S(1)} %copy-done, bf16[512,256]{1,0:T(8,128)(2,1)S(1)} %bitcast.10), custom_call_target="tpu_custom_call" | custom-call | bytes 1024 | tf_op jit(solution)/shard_map/self_first/pallas_call | solution.py:407
  14.6 0.6 %pad_add_fusion.position_ref = s32[2]{0:T(128)} fusion(s32[1]{0:T(128)} %bitcast.1, s32[1]{0:T(128)} %bitcast), kind=kLoop, calls=%fused_computation.2 | loop fusion | flops 2 | bytes 16 | tf_op jit(solution)/shard_map/stack | solution.py:460
  15.3 1.4 %seen_table.1.table_ref = s32[11]{0:T(128)} custom-call(s32[2]{0:T(128)} %pad_add_fusion.position_ref, s32[4,2]{1,0:T(4,128)} %copy.8.images_ref, s32[2]{0:T(128)} %owner_ref.1), custom_call_target="tpu_custom_call" | custom-call | tf_op jit(solution)/shard_map/seen_table/pallas_call | solution.py:123
  16.6 0.0 copy-start.2
  16.6 0.6 %copy-done.2 = s32[11]{0:T(128)S(1)} copy-done((s32[11]{0:T(128)S(1)}, s32[11]{0:T(128)}, u32[]{:S(2)}) %copy-start.2) | copy-done | bytes 68
  17.3 0.9 %cross_first.2 = (f32[4,8,256]{2,1,0:T(8,128)S(1)}, f32[4,144,256]{2,1,0:T(8,128)S(1)}) custom-call(s32[11]{0:T(128)S(1)} %copy-done.2, bf16[512,256]{1,0:T(8,128)(2,1)S(1)} %copy-done.3, bf16[2,1664,128]{2,1,0:T(8,128)(2,1)S(1)} %prepare.1.refs_1_.refs_2_), custom_call_target="tpu_custom_call" | custom-call | flops 2000000000 | bytes 1024 | tf_op jit(solution)/shard_map/cross_first/pallas_call | solution.py:261
  18.1 2.6 %collective-permute-done.2.refs_0_ = bf16[512,256]{1,0:T(8,128)(2,1)} collective-permute-done((bf16[512,256]{1,0:T(8,128)(2,1)S(1)}, bf16[512,256]{1,0:T(8,128)(2,1)}, u32[]{:S(2)}, u32[]{:S(2)}) %collective-permute-start.2) | collective-permute-done | bytes 262176 | tf_op jit(solution)/shard_map/ppermute | solution.py:444
  20.7 0.0 collective-permute-start.4
  20.7 1.3 %cross_first.3 = (f32[4,8,256]{2,1,0:T(8,128)S(1)}, f32[4,144,256]{2,1,0:T(8,128)S(1)}) custom-call(s32[11]{0:T(128)S(1)} %copy-done.2, bf16[512,256]{1,0:T(8,128)(2,1)} %collective-permute-done.2.refs_0_, bf16[2,1664,128]{2,1,0:T(8,128)(2,1)S(1)} %prepare.1.refs_1_.refs_2_), custom_call_target="tpu_custom_call" | custom-call | flops 2000000000 | bytes 1024 | tf_op jit(solution)/shard_map/cross_first/pallas_call | solution.py:261
  22.0 2.0 %collective-permute-done.3.refs_1_.refs_3_.refs_2_ = bf16[2,1664,128]{2,1,0:T(8,128)(2,1)S(1)} collective-permute-done((bf16[2,1664,128]{2,1,0:T(8,128)(2,1)S(1)}, bf16[2,1664,128]{2,1,0:T(8,128)(2,1)S(1)}, u32[]{:S(2)}, u32[]{:S(2)}) %collective-permute-start.3) | collective-permute-done | bytes 852000 | tf_op jit(solution)/shard_map/ppermute | solution.py:440
  24.1 3.3 %cross_last.4 = bf16[528,256]{1,0:T(8,128)(2,1)S(1)} custom-call(s32[11]{0:T(128)S(1)} %copy-done.2, bf16[512,256]{1,0:T(8,128)(2,1)} %collective-permute-done.2.refs_0_, bf16[2,1664,128]{2,1,0:T(8,128)(2,1)S(1)} %collective-permute-done.3.refs_1_.refs_3_.refs_2_, f32[4,8,256]{2,1,0:T(8,128)S(1)} %get-tuple-element.28.refs_2_, ...), custom_call_target="tpu_custom_call" | custom-call | flops 2000000000 | bytes 1024 | tf_op jit(solution)/shard_map/cross_last/pallas_call | solution.py:261
  27.4 2.9 %collective-permute-start.6 = (bf16[528,256]{1,0:T(8,128)(2,1)S(1)}, bf16[528,256]{1,0:T(8,128)(2,1)S(1)}, u32[]{:S(2)}, u32[]{:S(2)}) collective-permute-start(bf16[528,256]{1,0:T(8,128)(2,1)S(1)} %cross_last.4), channel_id=1, source_target_pairs={{0,2},{1,3},{2,0},{3,1},{4,6},{5,7},{6,4},{7,5},{8,10},{9,11},{10,... | collective-permute-start | bytes 811016 | tf_op jit(solution)/shard_map/ppermute | solution.py:444
  30.3 0.0 collective-permute-done.4.refs_1_
  30.3 0.0 collective-permute-done.1.refs_0_
  30.3 3.4 %cross_last.5 = bf16[528,256]{1,0:T(8,128)(2,1)S(1)} custom-call(s32[11]{0:T(128)S(1)} %copy-done.2, bf16[512,256]{1,0:T(8,128)(2,1)} %collective-permute-done.1.refs_0_, bf16[512,256]{1,0:T(8,128)(2,1)S(1)} %collective-permute-done.4.refs_1_, bf16[2,1664,128]{2,1,0:T(8,128)(2,1)S(1)} %prepare.1.refs_1_.refs_2_, ...), custom_call_target="tpu_custom_call" | custom-call | flops 2000000000 | bytes 1024 | tf_op jit(solution)/shard_map/cross_last/pallas_call | solution.py:261
  33.7 1.4 %collective-permute-start.7 = (bf16[528,256]{1,0:T(8,128)(2,1)S(1)}, bf16[528,256]{1,0:T(8,128)(2,1)S(1)}, u32[]{:S(2)}, u32[]{:S(2)}) collective-permute-start(bf16[528,256]{1,0:T(8,128)(2,1)S(1)} %cross_last.5), channel_id=1, source_target_pairs={{0,3},{1,2},{2,1},{3,0},{4,7},{5,6},{6,5},{7,4},{8,11},{9,10},{10,... | collective-permute-start | bytes 811016 | tf_op jit(solution)/shard_map/ppermute | solution.py:444
  35.1 0.0 collective-permute-done.refs_0_
  35.1 1.8 %collective-permute-start.5 = (bf16[512,256]{1,0:T(8,128)(2,1)S(1)}, bf16[512,256]{1,0:T(8,128)(2,1)S(1)}, u32[]{:S(2)}, u32[]{:S(2)}) collective-permute-start(bf16[512,256]{1,0:T(8,128)(2,1)S(1)} %bitcast.11), channel_id=1, source_target_pairs={{0,16},{16,0},{1,17},{17,1},{2,18},{18,2},{3,19},{19,3},{4,20},{20... | collective-permute-start | bytes 786440 | tf_op jit(solution)/shard_map/ppermute | solution.py:440
  36.9 3.0 %cross_last.6 = bf16[528,256]{1,0:T(8,128)(2,1)S(1)} custom-call(s32[11]{0:T(128)S(1)} %copy-done.2, bf16[512,256]{1,0:T(8,128)(2,1)S(1)} %collective-permute-done.refs_0_, bf16[2,1664,128]{2,1,0:T(8,128)(2,1)S(1)} %prepare.1.refs_1_.refs_2_, bf16[2,1664,128]{2,1,0:T(8,128)(2,1)S(1)} %collective-permute-done.3.refs_1_.refs_3_.refs_2_), custom_call_target="tpu_custom_call" | custom-call | flops 2000000000 | bytes 1024 | tf_op jit(solution)/shard_map/cross_last/pallas_call | solution.py:261
  39.9 0.0 copy-start.1
  39.9 0.1 collective-permute-start.8
  40.0 2.9 %cross_last.7.refs_0_ = bf16[528,256]{1,0:T(8,128)(2,1)S(1)} custom-call(s32[11]{0:T(128)S(1)} %copy-done.2, bf16[512,256]{1,0:T(8,128)(2,1)S(1)} %copy-done.3, bf16[2,1664,128]{2,1,0:T(8,128)(2,1)S(1)} %collective-permute-done.3.refs_1_.refs_3_.refs_2_, f32[4,8,256]{2,1,0:T(8,128)S(1)} %get-tuple-element.25.refs_2_, ...), custom_call_target="tpu_custom_call" | custom-call | flops 2000000000 | bytes 1024 | tf_op jit(solution)/shard_map/cross_last/pallas_call | solution.py:261
  42.9 0.0 collective-permute-done.5.refs_0_
  42.9 0.0 copy-done.1
  42.9 1.4 %self_last.1 = bf16[512,256]{1,0:T(8,128)(2,1)} custom-call(s32[2]{0:T(128)S(1)} %copy-done.1, bf16[512,256]{1,0:T(8,128)(2,1)S(1)} %copy-done, f32[2,8,512]{2,1,0:T(8,128)S(1)} %get-tuple-element.22.high_ref, f32[2,144,512]{2,1,0:T(8,128)S(1)} %get-tuple-element.23.mixed_ref, bf16[512,256]{1,0:T(8,128)(2,1)S(1)} %collective-permute-done.5.refs_0_), custom_call_target="tpu_custom_call" | custom-call | bytes 1024 | tf_op jit(solution)/shard_map/self_last/pallas_call | solution.py:425
  44.3 4.5 %collective-permute-done.6.refs_1_ = bf16[528,256]{1,0:T(8,128)(2,1)S(1)} collective-permute-done((bf16[528,256]{1,0:T(8,128)(2,1)S(1)}, bf16[528,256]{1,0:T(8,128)(2,1)S(1)}, u32[]{:S(2)}, u32[]{:S(2)}) %collective-permute-start.6) | collective-permute-done | bytes 270368 | tf_op jit(solution)/shard_map/ppermute | solution.py:444
  48.9 0.1 combine.2
  49.0 0.0 collective-permute-done.7.refs_2_
  49.0 0.1 combine.3
  49.1 4.3 %collective-permute-done.8.refs_2_ = bf16[528,256]{1,0:T(8,128)(2,1)S(1)} collective-permute-done((bf16[528,256]{1,0:T(8,128)(2,1)S(1)}, bf16[528,256]{1,0:T(8,128)(2,1)S(1)}, u32[]{:S(2)}, u32[]{:S(2)}) %collective-permute-start.8) | collective-permute-done | bytes 270368 | tf_op jit(solution)/shard_map/ppermute | solution.py:444
  53.4 0.9 %combine_last.1 = bf16[512,256]{1,0:T(8,128)(2,1)} custom-call(f32[512,256]{1,0:T(8,128)S(1)} %get-tuple-element.40.refs_0_, f32[4,256]{1,0:T(4,128)S(1)} %get-tuple-element.41.refs_1_, bf16[528,256]{1,0:T(8,128)(2,1)S(1)} %collective-permute-done.8.refs_2_), custom_call_target="tpu_custom_call" | custom-call | flops 2000000000 | bytes 1024 | tf_op jit(solution)/shard_map/combine_last/pallas_call | solution.py:336
  (1 shorter events, 0.0 us)
Async XLA Ops:
  1.9 3.2 %copy-start.3 = (bf16[512,256]{1,0:T(8,128)(2,1)S(1)}, bf16[512,256]{1,0:T(8,128)(2,1)}, u32[]{:S(2)}) copy-start(bf16[512,256]{1,0:T(8,128)(2,1)} %refs_0_.1) | copy-start | bytes 786436
  1.9 10.7 %copy-start.4 = (bf16[512,2,128]{2,1,0:T(2,128)(2,1)S(1)}, bf16[512,2,128]{2,1,0:T(2,128)(2,1)}, u32[]{:S(2)}) copy-start(bf16[512,2,128]{2,1,0:T(2,128)(2,1)} %param.7) | copy-start | bytes 786436
  2.1 21.9 %collective-permute-start.3 = (bf16[2,1664,128]{2,1,0:T(8,128)(2,1)S(1)}, bf16[2,1664,128]{2,1,0:T(8,128)(2,1)S(1)}, u32[]{:S(2)}, u32[]{:S(2)}) collective-permute-start(bf16[2,1664,128]{2,1,0:T(8,128)(2,1)S(1)} %prepare.1.refs_1_.refs_2_), channel_id=1, source_target_pairs={{0,16},{16,0},{1,17},{17,1},{2,18},{18,2},{3,19},{19,3},{4,20},{20... | collective-permute-start | bytes 2555912 | tf_op jit(solution)/shard_map/ppermute | solution.py:440
  5.1 15.6 %collective-permute-start.2 = (bf16[512,256]{1,0:T(8,128)(2,1)S(1)}, bf16[512,256]{1,0:T(8,128)(2,1)}, u32[]{:S(2)}, u32[]{:S(2)}) collective-permute-start(bf16[512,256]{1,0:T(8,128)(2,1)S(1)} %copy-done.3), channel_id=1, source_target_pairs={{0,2},{1,3},{2,0},{3,1},{4,6},{5,7},{6,4},{7,5},{8,10},{9,11},{10,... | collective-permute-start | bytes 786440 | tf_op jit(solution)/shard_map/ppermute | solution.py:444
  7.7 22.6 %collective-permute-start.1 = (bf16[512,256]{1,0:T(8,128)(2,1)S(1)}, bf16[512,256]{1,0:T(8,128)(2,1)}, u32[]{:S(2)}, u32[]{:S(2)}) collective-permute-start(bf16[512,256]{1,0:T(8,128)(2,1)S(1)} %copy-done.3), channel_id=1, source_target_pairs={{0,0},{1,2},{2,1},{3,3},{4,4},{5,6},{6,5},{7,7},{8,8},{9,10},{10,9... | collective-permute-start | bytes 786440 | tf_op jit(solution)/shard_map/ppermute | solution.py:467
  9.0 26.1 %collective-permute-start = (bf16[512,256]{1,0:T(8,128)(2,1)S(1)}, bf16[512,256]{1,0:T(8,128)(2,1)S(1)}, u32[]{:S(2)}, u32[]{:S(2)}) collective-permute-start(bf16[512,256]{1,0:T(8,128)(2,1)S(1)} %copy-done.3), channel_id=1, source_target_pairs={{0,1},{1,0},{2,3},{3,2},{4,5},{5,4},{6,7},{7,6},{8,9},{9,8},{10,11... | collective-permute-start | bytes 786440 | tf_op jit(solution)/shard_map/ppermute | solution.py:444
  11.3 0.7 %copy-start.5 = (s32[4,2]{0,1:T(2,128)S(1)}, s32[4,2]{0,1:T(2,128)}, u32[]{:S(2)}) copy-start(s32[4,2]{0,1:T(2,128)} %param.10) | copy-start | bytes 100
  12.6 1.0 %copy-start = (bf16[512,256]{1,0:T(8,128)(2,1)S(1)}, bf16[512,256]{1,0:T(8,128)(2,1)}, u32[]{:S(2)}) copy-start(bf16[512,256]{1,0:T(8,128)(2,1)} %q_ref.2) | copy-start | bytes 786436
  16.6 0.7 %copy-start.2 = (s32[11]{0:T(128)S(1)}, s32[11]{0:T(128)}, u32[]{:S(2)}) copy-start(s32[11]{0:T(128)} %seen_table.1.table_ref) | copy-start | bytes 136
  20.7 9.6 %collective-permute-start.4 = (bf16[512,256]{1,0:T(8,128)(2,1)}, bf16[512,256]{1,0:T(8,128)(2,1)S(1)}, u32[]{:S(2)}, u32[]{:S(2)}) collective-permute-start(bf16[512,256]{1,0:T(8,128)(2,1)} %collective-permute-done.2.refs_0_), channel_id=1, source_target_pairs={{0,1},{1,0},{2,3},{3,2},{4,5},{5,4},{6,7},{7,6},{8,9},{9,8},{10,11... | collective-permute-start | bytes 786440 | tf_op jit(solution)/shard_map/ppermute | solution.py:444
  27.4 21.5 %collective-permute-start.6 = (bf16[528,256]{1,0:T(8,128)(2,1)S(1)}, bf16[528,256]{1,0:T(8,128)(2,1)S(1)}, u32[]{:S(2)}, u32[]{:S(2)}) collective-permute-start(bf16[528,256]{1,0:T(8,128)(2,1)S(1)} %cross_last.4), channel_id=1, source_target_pairs={{0,2},{1,3},{2,0},{3,1},{4,6},{5,7},{6,4},{7,5},{8,10},{9,11},{10,... | collective-permute-start | bytes 811016 | tf_op jit(solution)/shard_map/ppermute | solution.py:444
  33.7 15.3 %collective-permute-start.7 = (bf16[528,256]{1,0:T(8,128)(2,1)S(1)}, bf16[528,256]{1,0:T(8,128)(2,1)S(1)}, u32[]{:S(2)}, u32[]{:S(2)}) collective-permute-start(bf16[528,256]{1,0:T(8,128)(2,1)S(1)} %cross_last.5), channel_id=1, source_target_pairs={{0,3},{1,2},{2,1},{3,0},{4,7},{5,6},{6,5},{7,4},{8,11},{9,10},{10,... | collective-permute-start | bytes 811016 | tf_op jit(solution)/shard_map/ppermute | solution.py:444
  35.1 7.8 %collective-permute-start.5 = (bf16[512,256]{1,0:T(8,128)(2,1)S(1)}, bf16[512,256]{1,0:T(8,128)(2,1)S(1)}, u32[]{:S(2)}, u32[]{:S(2)}) collective-permute-start(bf16[512,256]{1,0:T(8,128)(2,1)S(1)} %bitcast.11), channel_id=1, source_target_pairs={{0,16},{16,0},{1,17},{17,1},{2,18},{18,2},{3,19},{19,3},{4,20},{20... | collective-permute-start | bytes 786440 | tf_op jit(solution)/shard_map/ppermute | solution.py:440
  39.9 3.0 %copy-start.1 = (s32[2]{0:T(128)S(1)}, s32[2]{0:T(128)}, u32[]{:S(2)}) copy-start(s32[2]{0:T(128)} %pad_add_fusion.position_ref) | copy-start | bytes 28
  39.9 13.5 %collective-permute-start.8 = (bf16[528,256]{1,0:T(8,128)(2,1)S(1)}, bf16[528,256]{1,0:T(8,128)(2,1)S(1)}, u32[]{:S(2)}, u32[]{:S(2)}) collective-permute-start(bf16[528,256]{1,0:T(8,128)(2,1)S(1)} %cross_last.6), channel_id=1, source_target_pairs={{0,1},{1,0},{2,3},{3,2},{4,5},{5,4},{6,7},{7,6},{8,9},{9,8},{10,11... | collective-permute-start | bytes 811016 | tf_op jit(solution)/shard_map/ppermute | solution.py:444

commit v4 on v3

--- a/solution.py
+++ b/solution.py
@@ -92,8 +92,8 @@
     return next(count for count in range(1, rows) if count * HEAD_SIZE + lse_rows(count) == rows)
 
 
-def table_kernel(position_ref, images_ref, owner_ref, table_ref):
-    block_count, slots = images_ref.shape
+def table_kernel(position_ref, inside_ref, images_ref, owner_ref, table_ref):
+    slots, block_count = images_ref.shape
     for piece in range(slots):
         slot = lax.rem(position_ref[0] + (slots - piece), slots)
         base = piece * (block_count + 1)
@@ -105,7 +105,7 @@
                 0,
                 slots,
                 lambda image, sum, block=block, slot=slot: sum
-                + jnp.where(owner_ref[image] == slot, images_ref[block, image], 0),
+                + jnp.where(owner_ref[image] == slot, images_ref[image, block], 0),
                 jnp.int32(0),
             )
 
@@ -115,18 +115,18 @@
 
             count = count + jnp.where(seen > 0, 1, 0)
         table_ref[base] = count
-    table_ref[slots * (block_count + 1)] = position_ref[1]
-
-
-def seen_table(position, block_images, image_owner):
+    table_ref[slots * (block_count + 1)] = inside_ref[0]
+
+
+def seen_table(position, inside, block_images, image_owner):
     block_count, slots = block_images.shape
     return pl.pallas_call(
         table_kernel,
         out_shape=jax.ShapeDtypeStruct((slots * (block_count + 1) + 1,), jnp.int32),
-        in_specs=[SMEM] * 3,
+        in_specs=[SMEM] * 4,
         out_specs=SMEM,
         name="seen_table",
-    )(position, block_images, image_owner)
+    )(position, inside, block_images.T, image_owner)
 
 
 def chunks_of(width):
@@ -456,8 +456,8 @@
     cycle = lax.axis_size("blk")
     ring = lax.axis_size("enc")
     place = lax.axis_index("enc")
-    inside = (place > 0) & (place < ring - 1)
-    position = jnp.stack([lax.axis_index("blk"), inside]).astype(jnp.int32)
+    inside = ((place > 0) & (place < ring - 1)).astype(jnp.int32)[None]
+    position = lax.axis_index("blk").astype(jnp.int32)[None]
 
     images = [prepare(image_kv[0])]
     for _ in range(1, cycle):
@@ -469,14 +469,7 @@
     else:
         queries = {step: [shifted(cross_queries, "enc", ring - step)] for step in range(1, ring)}
     queries[0] = [cross_queries]
-    table = seen_table(position, block_images, image_owner)
-
-    text = text_kv.reshape(rows, 2 * HEAD_SIZE)
-    texts = []
-    onward = after(text, images[-1])
-    for _ in range(1, cycle):
-        onward = shifted(onward, "blk", 1)
-        texts.append(onward)
+    table = seen_table(position, inside, block_images, image_owner)
 
     latest = [None]
 
@@ -495,16 +488,20 @@
         return latest[0]
 
     split = cycle > 1
-    self_state = latest[0] = self_first(self_queries, text)
     own = begun(0) if split else None
     steps = [2, 3, 1] if ring == 4 else list(range(1, ring))
     states = {step: begun(step) for step in steps[:1]} if split else {}
-    received = []
+    received, texts = [], []
     for step in steps:
         part = finished(step, states.get(step))
+        if not texts:
+            texts.append(after(text_kv, part).reshape(rows, 2 * HEAD_SIZE))
+            for _ in range(1, cycle):
+                texts.append(shifted(texts[-1], "blk", 1))
         received.append(swapped(part, "enc", step) if ring == 4 else shifted(part, "enc", step))
     own_part = finished(0, own)
-    self_out = latest[0] = self_last(position, in_turn([self_queries])[0], self_state, texts)
+    self_state = latest[0] = self_first(in_turn([self_queries])[0], texts[0])
+    self_out = latest[0] = self_last(position, in_turn([self_queries])[0], self_state, texts[1:])
     so_far = in_turn([own_part])
     for index, part in enumerate(received):
         so_far = combined(so_far, part, cross_queries.shape, index + 1 == len(received))

time: 54.1 us -> 53.6 us (level)
  local copies, waits for them, and re-layouts: 4.21 us -> 1.87 us
  Pallas kernels: 19.9 us -> 22.2 us
  starting transfers between devices: 15.3 us -> 16.4 us
  waiting for transfers between devices: 13.4 us -> 12.6 us
  other arithmetic: 0.61 us -> 0 us
    pallas_call x6, Pallas kernels: 14.8 us -> 17.6 us  [cross_part(): pl.pallas_call(functools.partial(cross_kernel, key_count, len(images), of...]
    unnamed x15 -> x10, local copies, waits for them, and re-layouts: 4.21 us -> 1.87 us
    ppermute x6, starting transfers between devices: 9.19 us -> 10.1 us  [swapped(): lax.ppermute(value, axis, [(source, source ^ bits) for source in range(la...]
    ppermute x2, starting transfers between devices: 4.81 us -> 5.59 us  [shifted(): lax.ppermute(value, axis, [(source, (source + steps) % count) for source...]
    ppermute x1, starting transfers between devices: 1.34 us -> 0.67 us  [per_device(): lax.ppermute(cross_queries, 'enc', [(0, 0), (1, 2), (2, 1), (3, 3)])]
    another operation x1 -> x0, other arithmetic: 0.61 us -> none  [per_device(): position = jnp.stack([lax.axis_index('blk'), inside]).astype(jnp.int32)]
  transfers between devices with their start and end apart: 9 -> 9, of which waited for: 4 -> 4; matrix products, arithmetic and copies ran while one was open for 2% -> 0% of each run, Pallas kernels for 35% -> 39%
where the time goes in v4:
time: 53.6 us; the launch traced here: 53.9 us
  Pallas kernels  22.2 us (41%)
  starting transfers between devices  16.4 us (31%)
  waiting for transfers between devices  12.6 us (24%)
  local copies, waits for them, and re-layouts  1.87 us (3%)
  between operations  0.79 us (1%)
    pallas_call x6, Pallas kernels, cross_part(): pl.pallas_call(functools.partial(cross_kernel, key_count, len(images), of...  17.6 us
    ppermute x6, waiting for transfers between devices, swapped(): lax.ppermute(value, axis, [(source, source ^ bits) for source in range(la...  11.1 us
    ppermute x6, starting transfers between devices, swapped(): lax.ppermute(value, axis, [(source, source ^ bits) for source in range(la...  10.1 us
    ppermute x2, starting transfers between devices, shifted(): lax.ppermute(value, axis, [(source, (source + steps) % count) for source...  5.59 us
    unnamed x10, local copies, waits for them, and re-layouts  1.87 us
    ppermute x2, waiting for transfers between devices, shifted(): lax.ppermute(value, axis, [(source, (source + steps) % count) for source...  1.56 us
    pallas_call x1, Pallas kernels, seen_table(): pl.pallas_call(table_kernel, out_shape=jax.ShapeDtypeStruct((slots * (blo...  1.33 us
    pallas_call x1, Pallas kernels, self_first(): pl.pallas_call(functools.partial(self_first_kernel, group), out_shape=(ja...  1.09 us
  transfers between devices with their start and end apart: 9, of which 4 were waited for; matrix products, arithmetic and copies ran while one was open for 0% of the time, Pallas kernels for 39%

profile of v4, /device:TPU:0, one launch (start us, length us, event | category | flops | bytes accessed | tf_op | source)
XLA Modules:
  0.0 53.9 jit_solution(10226445767392622704)
XLA Ops:
  0.6 1.3 %copy.12 = bf16[1,2,1601,128]{3,2,1,0:T(8,128)(2,1)S(1)} copy(bf16[1,2,1601,128]{3,1,2,0:T(2,128)(2,1)} %param.9) | data formatting | bytes 1639424 | tf_op args[3]
  1.9 0.0 copy-start.2
  1.9 0.2 prepare.1.refs_1_.refs_2_
  2.1 3.0 %collective-permute-start.3 = (bf16[2,1664,128]{2,1,0:T(8,128)(2,1)S(1)}, bf16[2,1664,128]{2,1,0:T(8,128)(2,1)S(1)}, u32[]{:S(2)}, u32[]{:S(2)}) collective-permute-start(bf16[2,1664,128]{2,1,0:T(8,128)(2,1)S(1)} %prepare.1.refs_1_.refs_2_), channel_id=1, source_target_pairs={{0,16},{16,0},{1,17},{17,1},{2,18},{18,2},{3,19},{19,3},{4,20},{20... | collective-permute-start | bytes 2555912 | tf_op jit(solution)/shard_map/ppermute | solution.py:440
  5.1 0.0 copy-done.2
  5.1 2.6 %collective-permute-start.2 = (bf16[512,256]{1,0:T(8,128)(2,1)S(1)}, bf16[512,256]{1,0:T(8,128)(2,1)S(1)}, u32[]{:S(2)}, u32[]{:S(2)}) collective-permute-start(bf16[512,256]{1,0:T(8,128)(2,1)S(1)} %copy-done.2), channel_id=1, source_target_pairs={{0,2},{1,3},{2,0},{3,1},{4,6},{5,7},{6,4},{7,5},{8,10},{9,11},{10,... | collective-permute-start | bytes 786440 | tf_op jit(solution)/shard_map/ppermute | solution.py:444
  7.7 0.7 %collective-permute-start.1 = (bf16[512,256]{1,0:T(8,128)(2,1)S(1)}, bf16[512,256]{1,0:T(8,128)(2,1)S(1)}, u32[]{:S(2)}, u32[]{:S(2)}) collective-permute-start(bf16[512,256]{1,0:T(8,128)(2,1)S(1)} %copy-done.2), channel_id=1, source_target_pairs={{0,0},{1,2},{2,1},{3,3},{4,4},{5,6},{6,5},{7,7},{8,8},{9,10},{10,9... | collective-permute-start | bytes 786440 | tf_op jit(solution)/shard_map/ppermute | solution.py:467
  8.4 2.9 %collective-permute-start = (bf16[512,256]{1,0:T(8,128)(2,1)S(1)}, bf16[512,256]{1,0:T(8,128)(2,1)S(1)}, u32[]{:S(2)}, u32[]{:S(2)}) collective-permute-start(bf16[512,256]{1,0:T(8,128)(2,1)S(1)} %copy-done.2), channel_id=1, source_target_pairs={{0,1},{1,0},{2,3},{3,2},{4,5},{5,4},{6,7},{7,6},{8,9},{9,8},{10,11... | collective-permute-start | bytes 786440 | tf_op jit(solution)/shard_map/ppermute | solution.py:444
  11.2 1.3 %seen_table.1.table_ref = s32[11]{0:T(128)} custom-call(s32[1]{0:T(128)} %bitcast.position_ref, s32[1]{0:T(128)} %bitcast.1.inside_ref, s32[2,4]{1,0:T(2,128)} %bitcast.14, s32[2]{0:T(128)} %owner_ref.1), custom_call_target="tpu_custom_call" | custom-call | tf_op jit(solution)/shard_map/seen_table/pallas_call | solution.py:123
  12.6 0.0 copy-start.1
  12.6 0.6 %copy-done.1 = s32[11]{0:T(128)S(1)} copy-done((s32[11]{0:T(128)S(1)}, s32[11]{0:T(128)}, u32[]{:S(2)}) %copy-start.1) | copy-done | bytes 68
  13.2 1.9 %cross_first.2 = (f32[4,8,256]{2,1,0:T(8,128)S(1)}, f32[4,144,256]{2,1,0:T(8,128)S(1)}) custom-call(s32[11]{0:T(128)S(1)} %copy-done.1, bf16[512,256]{1,0:T(8,128)(2,1)S(1)} %copy-done.2, bf16[2,1664,128]{2,1,0:T(8,128)(2,1)S(1)} %prepare.1.refs_1_.refs_2_), custom_call_target="tpu_custom_call" | custom-call | flops 2000000000 | bytes 1024 | tf_op jit(solution)/shard_map/cross_first/pallas_call | solution.py:261
  15.0 5.5 %collective-permute-done.2.refs_0_ = bf16[512,256]{1,0:T(8,128)(2,1)S(1)} collective-permute-done((bf16[512,256]{1,0:T(8,128)(2,1)S(1)}, bf16[512,256]{1,0:T(8,128)(2,1)S(1)}, u32[]{:S(2)}, u32[]{:S(2)}) %collective-permute-start.2) | collective-permute-done | bytes 262176 | tf_op jit(solution)/shard_map/ppermute | solution.py:444
  20.6 0.0 collective-permute-start.4
  20.6 1.9 %cross_first.3 = (f32[4,8,256]{2,1,0:T(8,128)S(1)}, f32[4,144,256]{2,1,0:T(8,128)S(1)}) custom-call(s32[11]{0:T(128)S(1)} %copy-done.1, bf16[512,256]{1,0:T(8,128)(2,1)S(1)} %collective-permute-done.2.refs_0_, bf16[2,1664,128]{2,1,0:T(8,128)(2,1)S(1)} %prepare.1.refs_1_.refs_2_), custom_call_target="tpu_custom_call" | custom-call | flops 2000000000 | bytes 1024 | tf_op jit(solution)/shard_map/cross_first/pallas_call | solution.py:261
  22.5 1.6 %collective-permute-done.3.refs_1_.refs_3_.refs_2_ = bf16[2,1664,128]{2,1,0:T(8,128)(2,1)S(1)} collective-permute-done((bf16[2,1664,128]{2,1,0:T(8,128)(2,1)S(1)}, bf16[2,1664,128]{2,1,0:T(8,128)(2,1)S(1)}, u32[]{:S(2)}, u32[]{:S(2)}) %collective-permute-start.3) | collective-permute-done | bytes 852000 | tf_op jit(solution)/shard_map/ppermute | solution.py:440
  24.0 2.9 %cross_last.4 = bf16[528,256]{1,0:T(8,128)(2,1)S(1)} custom-call(s32[11]{0:T(128)S(1)} %copy-done.1, bf16[512,256]{1,0:T(8,128)(2,1)S(1)} %collective-permute-done.2.refs_0_, bf16[2,1664,128]{2,1,0:T(8,128)(2,1)S(1)} %collective-permute-done.3.refs_1_.refs_3_.refs_2_, f32[4,8,256]{2,1,0:T(8,128)S(1)} %get-tuple-element.25.refs_2_, ...), custom_call_target="tpu_custom_call" | custom-call | flops 2000000000 | bytes 1024 | tf_op jit(solution)/shard_map/cross_last/pallas_call | solution.py:261
  27.0 0.0 copy-start.3
  27.0 2.9 %collective-permute-start.6 = (bf16[528,256]{1,0:T(8,128)(2,1)S(1)}, bf16[528,256]{1,0:T(8,128)(2,1)S(1)}, u32[]{:S(2)}, u32[]{:S(2)}) collective-permute-start(bf16[528,256]{1,0:T(8,128)(2,1)S(1)} %cross_last.4), channel_id=1, source_target_pairs={{0,2},{1,3},{2,0},{3,1},{4,6},{5,7},{6,4},{7,5},{8,10},{9,11},{10,... | collective-permute-start | bytes 811016 | tf_op jit(solution)/shard_map/ppermute | solution.py:444
  29.9 0.0 collective-permute-done.4.refs_1_
  29.9 0.0 collective-permute-done.1.refs_0_
  29.9 4.0 %cross_last.5 = bf16[528,256]{1,0:T(8,128)(2,1)S(1)} custom-call(s32[11]{0:T(128)S(1)} %copy-done.1, bf16[512,256]{1,0:T(8,128)(2,1)S(1)} %collective-permute-done.1.refs_0_, bf16[512,256]{1,0:T(8,128)(2,1)S(1)} %collective-permute-done.4.refs_1_, bf16[2,1664,128]{2,1,0:T(8,128)(2,1)S(1)} %prepare.1.refs_1_.refs_2_, ...), custom_call_target="tpu_custom_call" | custom-call | flops 2000000000 | bytes 1024 | tf_op jit(solution)/shard_map/cross_last/pallas_call | solution.py:261
  33.9 1.4 %collective-permute-start.7 = (bf16[528,256]{1,0:T(8,128)(2,1)S(1)}, bf16[528,256]{1,0:T(8,128)(2,1)S(1)}, u32[]{:S(2)}, u32[]{:S(2)}) collective-permute-start(bf16[528,256]{1,0:T(8,128)(2,1)S(1)} %cross_last.5), channel_id=1, source_target_pairs={{0,3},{1,2},{2,1},{3,0},{4,7},{5,6},{6,5},{7,4},{8,11},{9,10},{10,... | collective-permute-start | bytes 811016 | tf_op jit(solution)/shard_map/ppermute | solution.py:444
  35.3 0.0 collective-permute-done.refs_0_
  35.3 0.0 copy-done.3
  35.4 2.6 %collective-permute-start.5 = (bf16[512,256]{1,0:T(8,128)(2,1)S(1)}, bf16[512,256]{1,0:T(8,128)(2,1)S(1)}, u32[]{:S(2)}, u32[]{:S(2)}) collective-permute-start(bf16[512,256]{1,0:T(8,128)(2,1)S(1)} %bitcast.11), channel_id=1, source_target_pairs={{0,16},{16,0},{1,17},{17,1},{2,18},{18,2},{3,19},{19,3},{4,20},{20... | collective-permute-start | bytes 786440 | tf_op jit(solution)/shard_map/ppermute | solution.py:440
  37.9 4.0 %cross_last.6 = bf16[528,256]{1,0:T(8,128)(2,1)S(1)} custom-call(s32[11]{0:T(128)S(1)} %copy-done.1, bf16[512,256]{1,0:T(8,128)(2,1)S(1)} %collective-permute-done.refs_0_, bf16[2,1664,128]{2,1,0:T(8,128)(2,1)S(1)} %prepare.1.refs_1_.refs_2_, bf16[2,1664,128]{2,1,0:T(8,128)(2,1)S(1)} %collective-permute-done.3.refs_1_.refs_3_.refs_2_), custom_call_target="tpu_custom_call" | custom-call | flops 2000000000 | bytes 1024 | tf_op jit(solution)/shard_map/cross_last/pallas_call | solution.py:261
  41.9 0.0 copy-start
  41.9 0.4 collective-permute-start.8
  42.3 2.9 %cross_last.7.refs_0_ = bf16[528,256]{1,0:T(8,128)(2,1)S(1)} custom-call(s32[11]{0:T(128)S(1)} %copy-done.1, bf16[512,256]{1,0:T(8,128)(2,1)S(1)} %copy-done.2, bf16[2,1664,128]{2,1,0:T(8,128)(2,1)S(1)} %collective-permute-done.3.refs_1_.refs_3_.refs_2_, f32[4,8,256]{2,1,0:T(8,128)S(1)} %get-tuple-element.22.refs_2_, ...), custom_call_target="tpu_custom_call" | custom-call | flops 2000000000 | bytes 1024 | tf_op jit(solution)/shard_map/cross_last/pallas_call | solution.py:261
  45.2 0.0 copy-done
  45.2 1.1 %self_first.1 = (f32[2,8,512]{2,1,0:T(8,128)S(1)}, f32[2,144,512]{2,1,0:T(8,128)S(1)}) custom-call(bf16[512,256]{1,0:T(8,128)(2,1)S(1)} %copy-done, bf16[512,256]{1,0:T(8,128)(2,1)S(1)} %bitcast.12), custom_call_target="tpu_custom_call" | custom-call | bytes 1024 | tf_op jit(solution)/shard_map/self_first/pallas_call | solution.py:407
  46.3 0.0 collective-permute-done.5.refs_0_
  46.3 0.9 %self_last.1 = bf16[512,256]{1,0:T(8,128)(2,1)} custom-call(s32[1]{0:T(128)} %bitcast.position_ref, bf16[512,256]{1,0:T(8,128)(2,1)S(1)} %copy-done, f32[2,8,512]{2,1,0:T(8,128)S(1)} %get-tuple-element.34.high_ref, f32[2,144,512]{2,1,0:T(8,128)S(1)} %get-tuple-element.35.mixed_ref, bf16[512,256]{1,0:T(8,128)(2,1)S(1)} %collective-permute-done.5.refs_0_), custom_call_target="tpu_custom_call" | custom-call | bytes 1024 | tf_op jit(solution)/shard_map/self_last/pallas_call | solution.py:425
  47.2 1.1 %collective-permute-done.6.refs_1_ = bf16[528,256]{1,0:T(8,128)(2,1)S(1)} collective-permute-done((bf16[528,256]{1,0:T(8,128)(2,1)S(1)}, bf16[528,256]{1,0:T(8,128)(2,1)S(1)}, u32[]{:S(2)}, u32[]{:S(2)}) %collective-permute-start.6) | collective-permute-done | bytes 270368 | tf_op jit(solution)/shard_map/ppermute | solution.py:444
  48.3 0.1 combine.2
  48.5 0.0 collective-permute-done.7.refs_2_
  48.5 0.1 combine.3
  48.6 4.4 %collective-permute-done.8.refs_2_ = bf16[528,256]{1,0:T(8,128)(2,1)S(1)} collective-permute-done((bf16[528,256]{1,0:T(8,128)(2,1)S(1)}, bf16[528,256]{1,0:T(8,128)(2,1)S(1)}, u32[]{:S(2)}, u32[]{:S(2)}) %collective-permute-start.8) | collective-permute-done | bytes 270368 | tf_op jit(solution)/shard_map/ppermute | solution.py:444
  53.0 0.9 %combine_last.1 = bf16[512,256]{1,0:T(8,128)(2,1)} custom-call(f32[512,256]{1,0:T(8,128)S(1)} %get-tuple-element.40.refs_0_, f32[4,256]{1,0:T(4,128)S(1)} %get-tuple-element.41.refs_1_, bf16[528,256]{1,0:T(8,128)(2,1)S(1)} %collective-permute-done.8.refs_2_), custom_call_target="tpu_custom_call" | custom-call | flops 2000000000 | bytes 1024 | tf_op jit(solution)/shard_map/combine_last/pallas_call | solution.py:336
  (1 shorter events, 0.0 us)
Async XLA Ops:
  1.9 3.2 %copy-start.2 = (bf16[512,256]{1,0:T(8,128)(2,1)S(1)}, bf16[512,256]{1,0:T(8,128)(2,1)}, u32[]{:S(2)}) copy-start(bf16[512,256]{1,0:T(8,128)(2,1)} %refs_0_.2) | copy-start | bytes 786436
  2.1 21.9 %collective-permute-start.3 = (bf16[2,1664,128]{2,1,0:T(8,128)(2,1)S(1)}, bf16[2,1664,128]{2,1,0:T(8,128)(2,1)S(1)}, u32[]{:S(2)}, u32[]{:S(2)}) collective-permute-start(bf16[2,1664,128]{2,1,0:T(8,128)(2,1)S(1)} %prepare.1.refs_1_.refs_2_), channel_id=1, source_target_pairs={{0,16},{16,0},{1,17},{17,1},{2,18},{18,2},{3,19},{19,3},{4,20},{20... | collective-permute-start | bytes 2555912 | tf_op jit(solution)/shard_map/ppermute | solution.py:440
  5.1 15.5 %collective-permute-start.2 = (bf16[512,256]{1,0:T(8,128)(2,1)S(1)}, bf16[512,256]{1,0:T(8,128)(2,1)S(1)}, u32[]{:S(2)}, u32[]{:S(2)}) collective-permute-start(bf16[512,256]{1,0:T(8,128)(2,1)S(1)} %copy-done.2), channel_id=1, source_target_pairs={{0,2},{1,3},{2,0},{3,1},{4,6},{5,7},{6,4},{7,5},{8,10},{9,11},{10,... | collective-permute-start | bytes 786440 | tf_op jit(solution)/shard_map/ppermute | solution.py:444
  7.7 22.2 %collective-permute-start.1 = (bf16[512,256]{1,0:T(8,128)(2,1)S(1)}, bf16[512,256]{1,0:T(8,128)(2,1)S(1)}, u32[]{:S(2)}, u32[]{:S(2)}) collective-permute-start(bf16[512,256]{1,0:T(8,128)(2,1)S(1)} %copy-done.2), channel_id=1, source_target_pairs={{0,0},{1,2},{2,1},{3,3},{4,4},{5,6},{6,5},{7,7},{8,8},{9,10},{10,9... | collective-permute-start | bytes 786440 | tf_op jit(solution)/shard_map/ppermute | solution.py:467
  8.4 27.0 %collective-permute-start = (bf16[512,256]{1,0:T(8,128)(2,1)S(1)}, bf16[512,256]{1,0:T(8,128)(2,1)S(1)}, u32[]{:S(2)}, u32[]{:S(2)}) collective-permute-start(bf16[512,256]{1,0:T(8,128)(2,1)S(1)} %copy-done.2), channel_id=1, source_target_pairs={{0,1},{1,0},{2,3},{3,2},{4,5},{5,4},{6,7},{7,6},{8,9},{9,8},{10,11... | collective-permute-start | bytes 786440 | tf_op jit(solution)/shard_map/ppermute | solution.py:444
  12.6 0.6 %copy-start.1 = (s32[11]{0:T(128)S(1)}, s32[11]{0:T(128)}, u32[]{:S(2)}) copy-start(s32[11]{0:T(128)} %seen_table.1.table_ref) | copy-start | bytes 136
  20.6 9.3 %collective-permute-start.4 = (bf16[512,256]{1,0:T(8,128)(2,1)S(1)}, bf16[512,256]{1,0:T(8,128)(2,1)S(1)}, u32[]{:S(2)}, u32[]{:S(2)}) collective-permute-start(bf16[512,256]{1,0:T(8,128)(2,1)S(1)} %collective-permute-done.2.refs_0_), channel_id=1, source_target_pairs={{0,1},{1,0},{2,3},{3,2},{4,5},{5,4},{6,7},{7,6},{8,9},{9,8},{10,11... | collective-permute-start | bytes 786440 | tf_op jit(solution)/shard_map/ppermute | solution.py:444
  27.0 8.4 %copy-start.3 = (bf16[512,2,128]{2,1,0:T(2,128)(2,1)S(1)}, bf16[512,2,128]{2,1,0:T(2,128)(2,1)}, u32[]{:S(2)}) copy-start(bf16[512,2,128]{2,1,0:T(2,128)(2,1)} %param.7) | copy-start | bytes 786436
  27.0 21.4 %collective-permute-start.6 = (bf16[528,256]{1,0:T(8,128)(2,1)S(1)}, bf16[528,256]{1,0:T(8,128)(2,1)S(1)}, u32[]{:S(2)}, u32[]{:S(2)}) collective-permute-start(bf16[528,256]{1,0:T(8,128)(2,1)S(1)} %cross_last.4), channel_id=1, source_target_pairs={{0,2},{1,3},{2,0},{3,1},{4,6},{5,7},{6,4},{7,5},{8,10},{9,11},{10,... | collective-permute-start | bytes 811016 | tf_op jit(solution)/shard_map/ppermute | solution.py:444
  33.9 14.6 %collective-permute-start.7 = (bf16[528,256]{1,0:T(8,128)(2,1)S(1)}, bf16[528,256]{1,0:T(8,128)(2,1)S(1)}, u32[]{:S(2)}, u32[]{:S(2)}) collective-permute-start(bf16[528,256]{1,0:T(8,128)(2,1)S(1)} %cross_last.5), channel_id=1, source_target_pairs={{0,3},{1,2},{2,1},{3,0},{4,7},{5,6},{6,5},{7,4},{8,11},{9,10},{10,... | collective-permute-start | bytes 811016 | tf_op jit(solution)/shard_map/ppermute | solution.py:444
  35.4 11.0 %collective-permute-start.5 = (bf16[512,256]{1,0:T(8,128)(2,1)S(1)}, bf16[512,256]{1,0:T(8,128)(2,1)S(1)}, u32[]{:S(2)}, u32[]{:S(2)}) collective-permute-start(bf16[512,256]{1,0:T(8,128)(2,1)S(1)} %bitcast.11), channel_id=1, source_target_pairs={{0,16},{16,0},{1,17},{17,1},{2,18},{18,2},{3,19},{19,3},{4,20},{20... | collective-permute-start | bytes 786440 | tf_op jit(solution)/shard_map/ppermute | solution.py:440
  41.9 3.3 %copy-start = (bf16[512,256]{1,0:T(8,128)(2,1)S(1)}, bf16[512,256]{1,0:T(8,128)(2,1)}, u32[]{:S(2)}) copy-start(bf16[512,256]{1,0:T(8,128)(2,1)} %q_ref.1) | copy-start | bytes 786436
  41.9 11.0 %collective-permute-start.8 = (bf16[528,256]{1,0:T(8,128)(2,1)S(1)}, bf16[528,256]{1,0:T(8,128)(2,1)S(1)}, u32[]{:S(2)}, u32[]{:S(2)}) collective-permute-start(bf16[528,256]{1,0:T(8,128)(2,1)S(1)} %cross_last.6), channel_id=1, source_target_pairs={{0,1},{1,0},{2,3},{3,2},{4,5},{5,4},{6,7},{7,6},{8,9},{9,8},{10,11... | collective-permute-start | bytes 811016 | tf_op jit(solution)/shard_map/ppermute | solution.py:444

commit v5 on v4

--- a/solution.py
+++ b/solution.py
@@ -129,14 +129,19 @@
     )(position, inside, block_images.T, image_owner)
 
 
-def chunks_of(width):
-    half = width // LANES // 2 * LANES
-    return [(0, half), (half, width)] if half else [(0, width)]
-
-
-def cross_kernel(key_count, pieces, offset, last, parts, table_ref, *refs):
-    q_refs, images, refs = refs[:parts], refs[parts : parts + pieces], refs[parts + pieces :]
-    if offset:
+def halves_of(count):
+    half = padded(count) // LANES // 2 * LANES
+    return [(0, half), (half, count)] if half else [(0, count)]
+
+
+def cross_kernel(layout, held_before, last, parts, table_ref, *refs):
+    q_refs, refs = refs[:parts], refs[parts:]
+    images = []
+    for step, counts in layout:
+        images.append((step, list(zip(refs[: len(counts)], counts))))
+        refs = refs[len(counts) :]
+    before = None
+    if held_before:
         before, refs = refs[:2], refs[2:]
     if last:
         out_ref, lse_ref, high_ref, mixed_ref, peak_ref, redo_ref = refs
@@ -147,22 +152,21 @@
     peak_ref[...] = jnp.full_like(peak_ref, LOWEST)
     redo_ref[0] = jnp.int32(0)
 
-    def fold_pair(blocks, image, exact, held):
-        width = image.shape[1]
+    def fold_pair(blocks, chunks, exact, held):
         queries = [q_refs[0][at_block(block), :] for block in blocks]
         if parts > 1:
             first = table_ref[table_ref.shape[0] - 1] > 0
             queries = [jnp.where(first, one, q_refs[1][at_block(block), :]) for one, block in zip(queries, blocks)]
         queries = jnp.concatenate([stacked_heads(one) for one in queries], axis=0)
-        chunks = chunks_of(width)
-
-        def scores_of(start, stop):
-            scores = nt_dot(image[0, start:stop, :], queries)
-            if stop > key_count:
-                body = stop - start - LANES
+
+        def scores_of(keys, count):
+            scores = nt_dot(keys[0], queries)
+            width = keys.shape[1]
+            if width > count:
+                body = width - LANES
                 tail = scores[body:, :]
-                key_id = start + body + lax.broadcasted_iota(jnp.int32, tail.shape, 0)
-                tail = jnp.where(key_id < key_count, tail, LOWEST)
+                key_id = body + lax.broadcasted_iota(jnp.int32, tail.shape, 0)
+                tail = jnp.where(key_id < count, tail, LOWEST)
                 scores = jnp.concatenate([scores[:body, :], tail], axis=0) if body else tail
             return scores
 
@@ -182,10 +186,10 @@
         new_high = jnp.maximum(jnp.maximum(high, seen), peak_ref[0:1, :])
         shift = new_high * LOG2_SCALE
         mixed = mixed * jnp.exp2((high - new_high) * LOG2_SCALE)
-        for index, (start, stop) in enumerate(chunks):
+        for index, (keys, _) in enumerate(chunks):
             following = scores_of(*chunks[index + 1]) if index + 1 < len(chunks) else None
             weights = jnp.exp2(scores * LOG2_SCALE - shift).astype(jnp.bfloat16)
-            value_t = jnp.concatenate([image[1, c : c + LANES, :] for c in range(start, stop, LANES)], axis=1)
+            value_t = jnp.concatenate([keys[1, c : c + LANES, :] for c in range(0, keys.shape[1], LANES)], axis=1)
             mixed = mixed + jnp.dot(with_ones(value_t), weights, preferred_element_type=jnp.float32)
             scores = following
         for index, block in enumerate(blocks):
@@ -205,11 +209,11 @@
     def attempt(trial, carry):
         @pl.when((trial == 0) | (redo_ref[0] > 0))
         def _():
-            for piece in range(pieces):
-                base = (offset + piece) * (block_count + 1)
+            for piece, (step, chunks) in enumerate(images):
+                base = step * (block_count + 1)
                 count = table_ref[base]
                 if piece == 0:
-                    held = before if offset else None
+                    held = before
                     for block in range(block_count):
                         seen = functools.reduce(
                             jnp.logical_or,
@@ -228,9 +232,9 @@
                 else:
                     held = (high_ref, mixed_ref)
 
-                def pair_step(pair, carry, piece=piece, base=base, count=count, held=held):
+                def pair_step(pair, carry, chunks=chunks, base=base, count=count, held=held):
                     blocks = [table_ref[base + 1 + 2 * pair], table_ref[base + jnp.minimum(2 * pair + 2, count)]]
-                    fold_pair(blocks, images[piece], trial > 0, held)
+                    fold_pair(blocks, chunks, trial > 0, held)
                     return carry
 
                 lax.fori_loop(0, (count + 1) // 2, pair_step, 0)
@@ -246,7 +250,7 @@
     lax.fori_loop(0, 2, attempt, 0)
 
 
-def cross_part(table, queries, images, key_count, offset, last, before=()):
+def cross_part(table, queries, images, last, before=()):
     tokens, columns = queries[0].shape
     block_count = tokens // MASK_BLOCK_TOKENS
     rows = columns // HEAD_SIZE * MASK_BLOCK_TOKENS
@@ -258,16 +262,18 @@
         scratch = [pltpu.VMEM((-(-block_count // 8) * 8, rows), jnp.float32)] + scratch
     else:
         out_shape = tuple(jax.ShapeDtypeStruct(shape, jnp.float32) for shape in state)
+    layout = tuple((step, tuple(count for _, count in parts)) for step, parts in images)
+    arrays = [part for _, parts in images for part, _ in parts]
     return pl.pallas_call(
-        functools.partial(cross_kernel, key_count, len(images), offset, last, len(queries)),
+        functools.partial(cross_kernel, layout, bool(before), last, len(queries)),
         out_shape=out_shape,
-        in_specs=[SMEM] + [VMEM] * (len(queries) + len(images) + len(before)),
+        in_specs=[SMEM] + [VMEM] * (len(queries) + len(arrays) + len(before)),
         out_specs=VMEM if last else (VMEM,) * 2,
         scratch_shapes=scratch,
         compiler_params=pltpu.CompilerParams(vmem_limit_bytes=VMEM_LIMIT),
         cost_estimate=MUCH,
         name="cross_last" if last else "cross_first",
-    )(table, *queries, *images, *before)
+    )(table, *queries, *arrays, *before)
 
 
 def lse_of(ref, block_count):
@@ -459,9 +465,11 @@
     inside = ((place > 0) & (place < ring - 1)).astype(jnp.int32)[None]
     position = lax.axis_index("blk").astype(jnp.int32)[None]
 
-    images = [prepare(image_kv[0])]
+    halves = halves_of(key_count)
+    images = [[(prepare(image_kv[0, :, start:stop, :]), stop - start) for start, stop in halves]]
     for _ in range(1, cycle):
-        images.append(shifted(images[-1], "blk", 1))
+        images.append([(shifted(part, "blk", 1), count) for part, count in images[-1]])
+    images = list(enumerate(images))
     if ring == 4:
         queries = {step: [swapped(cross_queries, "enc", step)] for step in (2, 1)}
         middle = lax.ppermute(cross_queries, "enc", [(0, 0), (1, 2), (2, 1), (3, 3)])
@@ -476,30 +484,31 @@
     def in_turn(arrays):
         return arrays if latest[0] is None else [after(one, latest[0]) for one in arrays]
 
-    def begun(step):
-        latest[0] = cross_part(table, in_turn(queries[step]), images[:1], key_count, 0, False)
+    def begun(step, given):
+        latest[0] = cross_part(table, in_turn(queries[step]), given, False)
         return latest[0]
 
-    def finished(step, state=None):
-        used = images if state is None else images[1:]
-        before = () if state is None else state
-        offset = 0 if state is None else 1
-        latest[0] = cross_part(table, in_turn(queries[step]), used, key_count, offset, True, before)
+    def finished(step, given, state=()):
+        latest[0] = cross_part(table, in_turn(queries[step]), given, True, state)
         return latest[0]
 
     split = cycle > 1
-    own = begun(0) if split else None
+    own = begun(0, images[:1]) if split else ()
     steps = [2, 3, 1] if ring == 4 else list(range(1, ring))
-    states = {step: begun(step) for step in steps[:1]} if split else {}
+    early, late = (), images
+    if split:
+        halfway = (1, images[1][1][:-1])
+        early = begun(steps[0], images[:1] + ([halfway] if halfway[1] else []))
+        late = [(1, images[1][1][-1:])] + images[2:]
     received, texts = [], []
     for step in steps:
-        part = finished(step, states.get(step))
-        if not texts:
+        part = finished(step, late, early) if step == steps[0] else finished(step, images)
+        if not texts and (step != steps[0] or len(steps) == 1):
             texts.append(after(text_kv, part).reshape(rows, 2 * HEAD_SIZE))
             for _ in range(1, cycle):
                 texts.append(shifted(texts[-1], "blk", 1))
         received.append(swapped(part, "enc", step) if ring == 4 else shifted(part, "enc", step))
-    own_part = finished(0, own)
+    own_part = finished(0, images[1:] if split else images, own)
     self_state = latest[0] = self_first(in_turn([self_queries])[0], texts[0])
     self_out = latest[0] = self_last(position, in_turn([self_queries])[0], self_state, texts[1:])
     so_far = in_turn([own_part])

time: 53.6 us -> 54.2 us (1.011); the launches traced: 53.9 us -> 53.6 us
  Pallas kernels: 22.2 us -> 18.8 us
  starting transfers between devices: 16.4 us -> 18.4 us
  waiting for transfers between devices: 12.6 us -> 13.8 us
    pallas_call x6, Pallas kernels: 17.6 us -> 14.2 us  [cross_part(): pl.pallas_call(functools.partial(cross_kernel, layout, bool(before), last...]
    ppermute x6, waiting for transfers between devices: 11.1 us -> 13.8 us  [swapped(): lax.ppermute(value, axis, [(source, source ^ bits) for source in range(la...]
    ppermute x2 -> x3, waiting for transfers between devices: 1.56 us -> 0.01 us  [shifted(): lax.ppermute(value, axis, [(source, (source + steps) % count) for source...]
    ppermute x6, starting transfers between devices: 10.1 us -> 11.6 us  [swapped(): lax.ppermute(value, axis, [(source, source ^ bits) for source in range(la...]
    unnamed x10 -> x11, local copies, waits for them, and re-layouts: 1.87 us -> 0.8 us
    slice x0 -> x4, local copies, waits for them, and re-layouts: none -> 1 us  [per_device(): image_kv[0, :, start:stop, :]]
    ppermute x2 -> x3, starting transfers between devices: 5.59 us -> 6.1 us  [shifted(): lax.ppermute(value, axis, [(source, (source + steps) % count) for source...]
  transfers between devices with their start and end apart: 9 -> 10, of which waited for: 4 -> 3; matrix products, arithmetic and copies ran while one was open for 0% -> 0% of each run, Pallas kernels for 39% -> 33%
where the time goes in v5:
time: 54.2 us; the launch traced here: 53.6 us
  Pallas kernels  18.8 us (35%)
  starting transfers between devices  18.4 us (34%)
  waiting for transfers between devices  13.8 us (25%)
  local copies, waits for them, and re-layouts  1.8 us (3%)
  between operations  0.83 us (2%)
    pallas_call x6, Pallas kernels, cross_part(): pl.pallas_call(functools.partial(cross_kernel, layout, bool(before), last...  14.2 us
    ppermute x6, waiting for transfers between devices, swapped(): lax.ppermute(value, axis, [(source, source ^ bits) for source in range(la...  13.8 us
    ppermute x6, starting transfers between devices, swapped(): lax.ppermute(value, axis, [(source, source ^ bits) for source in range(la...  11.6 us
    ppermute x3, starting transfers between devices, shifted(): lax.ppermute(value, axis, [(source, (source + steps) % count) for source...  6.1 us
    pallas_call x1, Pallas kernels, seen_table(): pl.pallas_call(table_kernel, out_shape=jax.ShapeDtypeStruct((slots * (blo...  1.33 us
    pallas_call x3, Pallas kernels, combined(): pl.pallas_call(functools.partial(combine_kernel, held, last), out_shape=o...  1.09 us
    pallas_call x1, Pallas kernels, self_first(): pl.pallas_call(functools.partial(self_first_kernel, group), out_shape=(ja...  1.09 us
  transfers between devices with their start and end apart: 10, of which 3 were waited for; matrix products, arithmetic and copies ran while one was open for 0% of the time, Pallas kernels for 33%

profile of v5, /device:TPU:0, one launch (start us, length us, event | category | flops | bytes accessed | tf_op | source)
XLA Modules:
  0.0 53.6 jit_solution(17006928031874643953)
XLA Ops:
  0.6 0.0 slice-start
  0.6 1.0 %slice-done = bf16[1,2,768,128]{3,1,2,0:T(2,128)(2,1)S(1)} async-done(((bf16[1,2,1601,128]{3,1,2,0:T(2,128)(2,1)}), bf16[1,2,768,128]{3,1,2,0:T(2,128)(2,1)S(1)}, s32[]{:S(2)}) %slice-start) | async-done | bytes 393240 | tf_op jit(solution)/shard_map/slice | solution.py:469
  1.6 0.1 copy.17
  1.7 0.1 prepare.2.refs_1_.refs_2_
  1.8 0.0 slice-start.1
  1.8 3.0 %collective-permute-start.3 = (bf16[2,768,128]{2,1,0:T(8,128)(2,1)S(1)}, bf16[2,768,128]{2,1,0:T(8,128)(2,1)S(1)}, u32[]{:S(2)}, u32[]{:S(2)}) collective-permute-start(bf16[2,768,128]{2,1,0:T(8,128)(2,1)S(1)} %prepare.2.refs_1_.refs_2_), channel_id=1, source_target_pairs={{0,16},{16,0},{1,17},{17,1},{2,18},{18,2},{3,19},{19,3},{4,20},{20... | collective-permute-start | bytes 1179656 | tf_op jit(solution)/shard_map/ppermute | solution.py:446
  4.8 0.0 slice-done.1
  4.8 0.1 copy.16
  4.9 0.0 copy-start.2
  4.9 0.1 prepare.3.refs_2_.refs_3_
  5.0 1.0 %collective-permute-start.4 = (bf16[2,896,128]{2,1,0:T(8,128)(2,1)S(1)}, bf16[2,896,128]{2,1,0:T(8,128)(2,1)S(1)}, u32[]{:S(2)}, u32[]{:S(2)}) collective-permute-start(bf16[2,896,128]{2,1,0:T(8,128)(2,1)S(1)} %prepare.3.refs_2_.refs_3_), channel_id=1, source_target_pairs={{0,16},{16,0},{1,17},{17,1},{2,18},{18,2},{3,19},{19,3},{4,20},{20... | collective-permute-start | bytes 1376264 | tf_op jit(solution)/shard_map/ppermute | solution.py:446
  6.0 0.0 copy-done.2
  6.0 2.6 %collective-permute-start.2 = (bf16[512,256]{1,0:T(8,128)(2,1)S(1)}, bf16[512,256]{1,0:T(8,128)(2,1)S(1)}, u32[]{:S(2)}, u32[]{:S(2)}) collective-permute-start(bf16[512,256]{1,0:T(8,128)(2,1)S(1)} %copy-done.2), channel_id=1, source_target_pairs={{0,2},{1,3},{2,0},{3,1},{4,6},{5,7},{6,4},{7,5},{8,10},{9,11},{10,... | collective-permute-start | bytes 786440 | tf_op jit(solution)/shard_map/ppermute | solution.py:450
  8.6 0.7 %collective-permute-start.1 = (bf16[512,256]{1,0:T(8,128)(2,1)S(1)}, bf16[512,256]{1,0:T(8,128)(2,1)S(1)}, u32[]{:S(2)}, u32[]{:S(2)}) collective-permute-start(bf16[512,256]{1,0:T(8,128)(2,1)S(1)} %copy-done.2), channel_id=1, source_target_pairs={{0,0},{1,2},{2,1},{3,3},{4,4},{5,6},{6,5},{7,7},{8,8},{9,10},{10,9... | collective-permute-start | bytes 786440 | tf_op jit(solution)/shard_map/ppermute | solution.py:475
  9.3 2.9 %collective-permute-start = (bf16[512,256]{1,0:T(8,128)(2,1)S(1)}, bf16[512,256]{1,0:T(8,128)(2,1)S(1)}, u32[]{:S(2)}, u32[]{:S(2)}) collective-permute-start(bf16[512,256]{1,0:T(8,128)(2,1)S(1)} %copy-done.2), channel_id=1, source_target_pairs={{0,1},{1,0},{2,3},{3,2},{4,5},{5,4},{6,7},{7,6},{8,9},{9,8},{10,11... | collective-permute-start | bytes 786440 | tf_op jit(solution)/shard_map/ppermute | solution.py:450
  12.2 1.3 %seen_table.1.table_ref = s32[11]{0:T(128)} custom-call(s32[1]{0:T(128)} %bitcast.position_ref, s32[1]{0:T(128)} %bitcast.1.inside_ref, s32[2,4]{1,0:T(2,128)} %bitcast.18, s32[2]{0:T(128)} %owner_ref.1), custom_call_target="tpu_custom_call" | custom-call | tf_op jit(solution)/shard_map/seen_table/pallas_call | solution.py:123
  13.5 0.0 copy-start.1
  13.5 0.6 %copy-done.1 = s32[11]{0:T(128)S(1)} copy-done((s32[11]{0:T(128)S(1)}, s32[11]{0:T(128)}, u32[]{:S(2)}) %copy-start.1) | copy-done | bytes 68
  14.2 0.9 %cross_first.2 = (f32[4,8,256]{2,1,0:T(8,128)S(1)}, f32[4,144,256]{2,1,0:T(8,128)S(1)}) custom-call(s32[11]{0:T(128)S(1)} %copy-done.1, bf16[512,256]{1,0:T(8,128)(2,1)S(1)} %copy-done.2, bf16[2,768,128]{2,1,0:T(8,128)(2,1)S(1)} %prepare.2.refs_1_.refs_2_, bf16[2,896,128]{2,1,0:T(8,128)(2,1)S(1)} %prepare.3.refs_2_.refs_3_), custom_call_target="tpu_custom_call" | custom-call | flops 2000000000 | bytes 1024 | tf_op jit(solution)/shard_map/cross_first/pallas_call | solution.py:267
  15.0 6.5 %collective-permute-done.2.refs_0_ = bf16[512,256]{1,0:T(8,128)(2,1)S(1)} collective-permute-done((bf16[512,256]{1,0:T(8,128)(2,1)S(1)}, bf16[512,256]{1,0:T(8,128)(2,1)S(1)}, u32[]{:S(2)}, u32[]{:S(2)}) %collective-permute-start.2) | collective-permute-done | bytes 262176 | tf_op jit(solution)/shard_map/ppermute | solution.py:450
  21.5 0.0 collective-permute-start.5
  21.5 0.0 collective-permute-done.3.refs_3_.refs_4_.refs_1_
  21.5 2.2 %cross_first.3 = (f32[4,8,256]{2,1,0:T(8,128)S(1)}, f32[4,144,256]{2,1,0:T(8,128)S(1)}) custom-call(s32[11]{0:T(128)S(1)} %copy-done.1, bf16[512,256]{1,0:T(8,128)(2,1)S(1)} %collective-permute-done.2.refs_0_, bf16[2,768,128]{2,1,0:T(8,128)(2,1)S(1)} %prepare.2.refs_1_.refs_2_, bf16[2,896,128]{2,1,0:T(8,128)(2,1)S(1)} %prepare.3.refs_2_.refs_3_, ...), custom_call_target="tpu_custom_call" | custom-call | flops 2000000000 | bytes 1024 | tf_op jit(solution)/shard_map/cross_first/pallas_call | solution.py:267
  23.8 0.0 collective-permute-done.4.refs_1_.refs_5_.refs_4_.refs_2_
  23.8 2.3 %cross_last.4 = bf16[528,256]{1,0:T(8,128)(2,1)S(1)} custom-call(s32[11]{0:T(128)S(1)} %copy-done.1, bf16[512,256]{1,0:T(8,128)(2,1)S(1)} %collective-permute-done.2.refs_0_, bf16[2,896,128]{2,1,0:T(8,128)(2,1)S(1)} %collective-permute-done.4.refs_1_.refs_5_.refs_4_.refs_2_, f32[4,8,256]{2,1,0:T(8,128)S(1)} %get-tuple-element.25.refs_2_, ...), custom_call_target="tpu_custom_call" | custom-call | flops 2000000000 | bytes 1024 | tf_op jit(solution)/shard_map/cross_last/pallas_call | solution.py:267
  26.0 0.0 copy-start.3
  26.1 3.0 %collective-permute-start.7 = (bf16[528,256]{1,0:T(8,128)(2,1)S(1)}, bf16[528,256]{1,0:T(8,128)(2,1)S(1)}, u32[]{:S(2)}, u32[]{:S(2)}) collective-permute-start(bf16[528,256]{1,0:T(8,128)(2,1)S(1)} %cross_last.4), channel_id=1, source_target_pairs={{0,2},{1,3},{2,0},{3,1},{4,6},{5,7},{6,4},{7,5},{8,10},{9,11},{10,... | collective-permute-start | bytes 811016 | tf_op jit(solution)/shard_map/ppermute | solution.py:450
  29.1 0.0 collective-permute-done.1.refs_0_
  29.1 0.0 collective-permute-done.5.refs_1_
  29.1 3.0 %cross_last.5 = bf16[528,256]{1,0:T(8,128)(2,1)S(1)} custom-call(s32[11]{0:T(128)S(1)} %copy-done.1, bf16[512,256]{1,0:T(8,128)(2,1)S(1)} %collective-permute-done.1.refs_0_, bf16[512,256]{1,0:T(8,128)(2,1)S(1)} %collective-permute-done.5.refs_1_, bf16[2,768,128]{2,1,0:T(8,128)(2,1)S(1)} %prepare.2.refs_1_.refs_2_, ...), custom_call_target="tpu_custom_call" | custom-call | flops 2000000000 | bytes 1024 | tf_op jit(solution)/shard_map/cross_last/pallas_call | solution.py:267
  32.1 3.0 %collective-permute-start.8 = (bf16[528,256]{1,0:T(8,128)(2,1)S(1)}, bf16[528,256]{1,0:T(8,128)(2,1)S(1)}, u32[]{:S(2)}, u32[]{:S(2)}) collective-permute-start(bf16[528,256]{1,0:T(8,128)(2,1)S(1)} %cross_last.5), channel_id=1, source_target_pairs={{0,3},{1,2},{2,1},{3,0},{4,7},{5,6},{6,5},{7,4},{8,11},{9,10},{10,... | collective-permute-start | bytes 811016 | tf_op jit(solution)/shard_map/ppermute | solution.py:450
  35.1 0.0 collective-permute-done.refs_0_
  35.1 0.0 copy-done.3
  35.2 2.1 %collective-permute-start.6 = (bf16[512,256]{1,0:T(8,128)(2,1)S(1)}, bf16[512,256]{1,0:T(8,128)(2,1)S(1)}, u32[]{:S(2)}, u32[]{:S(2)}) collective-permute-start(bf16[512,256]{1,0:T(8,128)(2,1)S(1)} %bitcast.15), channel_id=1, source_target_pairs={{0,16},{16,0},{1,17},{17,1},{2,18},{18,2},{3,19},{19,3},{4,20},{20... | collective-permute-start | bytes 786440 | tf_op jit(solution)/shard_map/ppermute | solution.py:446
  37.3 2.9 %cross_last.6 = bf16[528,256]{1,0:T(8,128)(2,1)S(1)} custom-call(s32[11]{0:T(128)S(1)} %copy-done.1, bf16[512,256]{1,0:T(8,128)(2,1)S(1)} %collective-permute-done.refs_0_, bf16[2,768,128]{2,1,0:T(8,128)(2,1)S(1)} %prepare.2.refs_1_.refs_2_, bf16[2,896,128]{2,1,0:T(8,128)(2,1)S(1)} %prepare.3.refs_2_.refs_3_, ...), custom_call_target="tpu_custom_call" | custom-call | flops 2000000000 | bytes 1024 | tf_op jit(solution)/shard_map/cross_last/pallas_call | solution.py:267
  40.2 0.0 copy-start
  40.2 0.1 collective-permute-start.9
  40.3 2.9 %cross_last.7.refs_0_ = bf16[528,256]{1,0:T(8,128)(2,1)S(1)} custom-call(s32[11]{0:T(128)S(1)} %copy-done.1, bf16[512,256]{1,0:T(8,128)(2,1)S(1)} %copy-done.2, bf16[2,768,128]{2,1,0:T(8,128)(2,1)S(1)} %collective-permute-done.3.refs_3_.refs_4_.refs_1_, bf16[2,896,128]{2,1,0:T(8,128)(2,1)S(1)} %collective-permute-done.4.refs_1_.refs_5_.refs_4_.refs_2_, ...), custom_call_target="tpu_custom_call" | custom-call | flops 2000000000 | bytes 1024 | tf_op jit(solution)/shard_map/cross_last/pallas_call | solution.py:267
  43.2 0.0 copy-done
  43.3 1.1 %self_first.1 = (f32[2,8,512]{2,1,0:T(8,128)S(1)}, f32[2,144,512]{2,1,0:T(8,128)S(1)}) custom-call(bf16[512,256]{1,0:T(8,128)(2,1)S(1)} %copy-done, bf16[512,256]{1,0:T(8,128)(2,1)S(1)} %bitcast.16), custom_call_target="tpu_custom_call" | custom-call | bytes 1024 | tf_op jit(solution)/shard_map/self_first/pallas_call | solution.py:413
  44.3 0.0 collective-permute-done.6.refs_0_
  44.4 0.9 %self_last.1 = bf16[512,256]{1,0:T(8,128)(2,1)} custom-call(s32[1]{0:T(128)} %bitcast.position_ref, bf16[512,256]{1,0:T(8,128)(2,1)S(1)} %copy-done, f32[2,8,512]{2,1,0:T(8,128)S(1)} %get-tuple-element.34.high_ref, f32[2,144,512]{2,1,0:T(8,128)S(1)} %get-tuple-element.35.mixed_ref, bf16[512,256]{1,0:T(8,128)(2,1)S(1)} %collective-permute-done.6.refs_0_), custom_call_target="tpu_custom_call" | custom-call | bytes 1024 | tf_op jit(solution)/shard_map/self_last/pallas_call | solution.py:431
  45.3 2.4 %collective-permute-done.7.refs_1_ = bf16[528,256]{1,0:T(8,128)(2,1)S(1)} collective-permute-done((bf16[528,256]{1,0:T(8,128)(2,1)S(1)}, bf16[528,256]{1,0:T(8,128)(2,1)S(1)}, u32[]{:S(2)}, u32[]{:S(2)}) %collective-permute-start.7) | collective-permute-done | bytes 270368 | tf_op jit(solution)/shard_map/ppermute | solution.py:450
  47.7 0.1 combine.2
  47.8 0.0 collective-permute-done.8.refs_2_
  47.8 0.1 combine.3
  47.9 4.8 %collective-permute-done.9.refs_2_ = bf16[528,256]{1,0:T(8,128)(2,1)S(1)} collective-permute-done((bf16[528,256]{1,0:T(8,128)(2,1)S(1)}, bf16[528,256]{1,0:T(8,128)(2,1)S(1)}, u32[]{:S(2)}, u32[]{:S(2)}) %collective-permute-start.9) | collective-permute-done | bytes 270368 | tf_op jit(solution)/shard_map/ppermute | solution.py:450
  52.8 0.9 %combine_last.1 = bf16[512,256]{1,0:T(8,128)(2,1)} custom-call(f32[512,256]{1,0:T(8,128)S(1)} %get-tuple-element.40.refs_0_, f32[4,256]{1,0:T(4,128)S(1)} %get-tuple-element.41.refs_1_, bf16[528,256]{1,0:T(8,128)(2,1)S(1)} %collective-permute-done.9.refs_2_), custom_call_target="tpu_custom_call" | custom-call | flops 2000000000 | bytes 1024 | tf_op jit(solution)/shard_map/combine_last/pallas_call | solution.py:342
  (1 shorter events, 0.0 us)
Async XLA Ops:
  0.6 1.0 %slice-start = ((bf16[1,2,1601,128]{3,1,2,0:T(2,128)(2,1)}), bf16[1,2,768,128]{3,1,2,0:T(2,128)(2,1)S(1)}, s32[]{:S(2)}) async-start(bf16[1,2,1601,128]{3,1,2,0:T(2,128)(2,1)} %param.9), calls=%async_computation | async-start | bytes 786432 | tf_op jit(solution)/shard_map/slice | solution.py:469
  1.8 3.0 %slice-start.1 = ((bf16[1,2,1601,128]{3,1,2,0:T(2,128)(2,1)}), bf16[1,2,833,128]{3,1,2,0:T(2,128)(2,1)S(1)}, s32[]{:S(2)}) async-start(bf16[1,2,1601,128]{3,1,2,0:T(2,128)(2,1)} %param.9), calls=%async_computation.1 | async-start | bytes 852992 | tf_op jit(solution)/shard_map/slice | solution.py:469
  1.8 19.7 %collective-permute-start.3 = (bf16[2,768,128]{2,1,0:T(8,128)(2,1)S(1)}, bf16[2,768,128]{2,1,0:T(8,128)(2,1)S(1)}, u32[]{:S(2)}, u32[]{:S(2)}) collective-permute-start(bf16[2,768,128]{2,1,0:T(8,128)(2,1)S(1)} %prepare.2.refs_1_.refs_2_), channel_id=1, source_target_pairs={{0,16},{16,0},{1,17},{17,1},{2,18},{18,2},{3,19},{19,3},{4,20},{20... | collective-permute-start | bytes 1179656 | tf_op jit(solution)/shard_map/ppermute | solution.py:446
  4.9 1.2 %copy-start.2 = (bf16[512,256]{1,0:T(8,128)(2,1)S(1)}, bf16[512,256]{1,0:T(8,128)(2,1)}, u32[]{:S(2)}) copy-start(bf16[512,256]{1,0:T(8,128)(2,1)} %refs_0_.2) | copy-start | bytes 786436
  5.0 18.7 %collective-permute-start.4 = (bf16[2,896,128]{2,1,0:T(8,128)(2,1)S(1)}, bf16[2,896,128]{2,1,0:T(8,128)(2,1)S(1)}, u32[]{:S(2)}, u32[]{:S(2)}) collective-permute-start(bf16[2,896,128]{2,1,0:T(8,128)(2,1)S(1)} %prepare.3.refs_2_.refs_3_), channel_id=1, source_target_pairs={{0,16},{16,0},{1,17},{17,1},{2,18},{18,2},{3,19},{19,3},{4,20},{20... | collective-permute-start | bytes 1376264 | tf_op jit(solution)/shard_map/ppermute | solution.py:446
  6.0 15.5 %collective-permute-start.2 = (bf16[512,256]{1,0:T(8,128)(2,1)S(1)}, bf16[512,256]{1,0:T(8,128)(2,1)S(1)}, u32[]{:S(2)}, u32[]{:S(2)}) collective-permute-start(bf16[512,256]{1,0:T(8,128)(2,1)S(1)} %copy-done.2), channel_id=1, source_target_pairs={{0,2},{1,3},{2,0},{3,1},{4,6},{5,7},{6,4},{7,5},{8,10},{9,11},{10,... | collective-permute-start | bytes 786440 | tf_op jit(solution)/shard_map/ppermute | solution.py:450
  8.6 20.5 %collective-permute-start.1 = (bf16[512,256]{1,0:T(8,128)(2,1)S(1)}, bf16[512,256]{1,0:T(8,128)(2,1)S(1)}, u32[]{:S(2)}, u32[]{:S(2)}) collective-permute-start(bf16[512,256]{1,0:T(8,128)(2,1)S(1)} %copy-done.2), channel_id=1, source_target_pairs={{0,0},{1,2},{2,1},{3,3},{4,4},{5,6},{6,5},{7,7},{8,8},{9,10},{10,9... | collective-permute-start | bytes 786440 | tf_op jit(solution)/shard_map/ppermute | solution.py:475
  9.3 25.8 %collective-permute-start = (bf16[512,256]{1,0:T(8,128)(2,1)S(1)}, bf16[512,256]{1,0:T(8,128)(2,1)S(1)}, u32[]{:S(2)}, u32[]{:S(2)}) collective-permute-start(bf16[512,256]{1,0:T(8,128)(2,1)S(1)} %copy-done.2), channel_id=1, source_target_pairs={{0,1},{1,0},{2,3},{3,2},{4,5},{5,4},{6,7},{7,6},{8,9},{9,8},{10,11... | collective-permute-start | bytes 786440 | tf_op jit(solution)/shard_map/ppermute | solution.py:450
  13.5 0.6 %copy-start.1 = (s32[11]{0:T(128)S(1)}, s32[11]{0:T(128)}, u32[]{:S(2)}) copy-start(s32[11]{0:T(128)} %seen_table.1.table_ref) | copy-start | bytes 136
  21.5 7.6 %collective-permute-start.5 = (bf16[512,256]{1,0:T(8,128)(2,1)S(1)}, bf16[512,256]{1,0:T(8,128)(2,1)S(1)}, u32[]{:S(2)}, u32[]{:S(2)}) collective-permute-start(bf16[512,256]{1,0:T(8,128)(2,1)S(1)} %collective-permute-done.2.refs_0_), channel_id=1, source_target_pairs={{0,1},{1,0},{2,3},{3,2},{4,5},{5,4},{6,7},{7,6},{8,9},{9,8},{10,11... | collective-permute-start | bytes 786440 | tf_op jit(solution)/shard_map/ppermute | solution.py:450
  26.0 9.1 %copy-start.3 = (bf16[512,2,128]{2,1,0:T(2,128)(2,1)S(1)}, bf16[512,2,128]{2,1,0:T(2,128)(2,1)}, u32[]{:S(2)}) copy-start(bf16[512,2,128]{2,1,0:T(2,128)(2,1)} %param.7) | copy-start | bytes 786436
  26.1 21.6 %collective-permute-start.7 = (bf16[528,256]{1,0:T(8,128)(2,1)S(1)}, bf16[528,256]{1,0:T(8,128)(2,1)S(1)}, u32[]{:S(2)}, u32[]{:S(2)}) collective-permute-start(bf16[528,256]{1,0:T(8,128)(2,1)S(1)} %cross_last.4), channel_id=1, source_target_pairs={{0,2},{1,3},{2,0},{3,1},{4,6},{5,7},{6,4},{7,5},{8,10},{9,11},{10,... | collective-permute-start | bytes 811016 | tf_op jit(solution)/shard_map/ppermute | solution.py:450
  32.1 15.7 %collective-permute-start.8 = (bf16[528,256]{1,0:T(8,128)(2,1)S(1)}, bf16[528,256]{1,0:T(8,128)(2,1)S(1)}, u32[]{:S(2)}, u32[]{:S(2)}) collective-permute-start(bf16[528,256]{1,0:T(8,128)(2,1)S(1)} %cross_last.5), channel_id=1, source_target_pairs={{0,3},{1,2},{2,1},{3,0},{4,7},{5,6},{6,5},{7,4},{8,11},{9,10},{10,... | collective-permute-start | bytes 811016 | tf_op jit(solution)/shard_map/ppermute | solution.py:450
  35.2 9.2 %collective-permute-start.6 = (bf16[512,256]{1,0:T(8,128)(2,1)S(1)}, bf16[512,256]{1,0:T(8,128)(2,1)S(1)}, u32[]{:S(2)}, u32[]{:S(2)}) collective-permute-start(bf16[512,256]{1,0:T(8,128)(2,1)S(1)} %bitcast.15), channel_id=1, source_target_pairs={{0,16},{16,0},{1,17},{17,1},{2,18},{18,2},{3,19},{19,3},{4,20},{20... | collective-permute-start | bytes 786440 | tf_op jit(solution)/shard_map/ppermute | solution.py:446
  40.2 3.0 %copy-start = (bf16[512,256]{1,0:T(8,128)(2,1)S(1)}, bf16[512,256]{1,0:T(8,128)(2,1)}, u32[]{:S(2)}) copy-start(bf16[512,256]{1,0:T(8,128)(2,1)} %q_ref.1) | copy-start | bytes 786436
  40.2 12.5 %collective-permute-start.9 = (bf16[528,256]{1,0:T(8,128)(2,1)S(1)}, bf16[528,256]{1,0:T(8,128)(2,1)S(1)}, u32[]{:S(2)}, u32[]{:S(2)}) collective-permute-start(bf16[528,256]{1,0:T(8,128)(2,1)S(1)} %cross_last.6), channel_id=1, source_target_pairs={{0,1},{1,0},{2,3},{3,2},{4,5},{5,4},{6,7},{7,6},{8,9},{9,8},{10,11... | collective-permute-start | bytes 811016 | tf_op jit(solution)/shard_map/ppermute | solution.py:450

commit v6 on v4

--- a/solution.py
+++ b/solution.py
@@ -459,9 +459,10 @@
     inside = ((place > 0) & (place < ring - 1)).astype(jnp.int32)[None]
     position = lax.axis_index("blk").astype(jnp.int32)[None]
 
-    images = [prepare(image_kv[0])]
+    raw = [image_kv]
     for _ in range(1, cycle):
-        images.append(shifted(images[-1], "blk", 1))
+        raw.append(shifted(raw[-1], "blk", 1))
+    images = [prepare(image[0]) for image in raw]
     if ring == 4:
         queries = {step: [swapped(cross_queries, "enc", step)] for step in (2, 1)}
         middle = lax.ppermute(cross_queries, "enc", [(0, 0), (1, 2), (2, 1), (3, 3)])

time: 53.6 us -> 52.9 us (0.987); the launches traced: 53.9 us -> 52.6 us
  waiting for transfers between devices: 12.6 us -> 9.26 us
  starting transfers between devices: 16.4 us -> 17.2 us
  local copies, waits for them, and re-layouts: 1.87 us -> 2.56 us
    ppermute x6, waiting for transfers between devices: 11.1 us -> 9.25 us  [swapped(): lax.ppermute(value, axis, [(source, source ^ bits) for source in range(la...]
    ppermute x2, waiting for transfers between devices: 1.56 us -> 0.01 us  [shifted(): lax.ppermute(value, axis, [(source, (source + steps) % count) for source...]
    ppermute x1, starting transfers between devices: 0.67 us -> 1.6 us  [per_device(): lax.ppermute(cross_queries, 'enc', [(0, 0), (1, 2), (2, 1), (3, 3)])]
    unnamed x10 -> x12, local copies, waits for them, and re-layouts: 1.87 us -> 2.45 us
  transfers between devices with their start and end apart: 9 -> 9, of which waited for: 4 -> 3; matrix products, arithmetic and copies ran while one was open for 0% -> 3% of each run, Pallas kernels for 39% -> 42%
where the time goes in v6:
time: 52.9 us; the launch traced here: 52.6 us
  Pallas kernels  22.7 us (43%)
  starting transfers between devices  17.2 us (33%)
  waiting for transfers between devices  9.26 us (18%)
  local copies, waits for them, and re-layouts  2.56 us (5%)
  between operations  0.83 us (2%)
    pallas_call x6, Pallas kernels, cross_part(): pl.pallas_call(functools.partial(cross_kernel, key_count, len(images), of...  17.9 us
    ppermute x6, starting transfers between devices, swapped(): lax.ppermute(value, axis, [(source, source ^ bits) for source in range(la...  9.79 us
    ppermute x6, waiting for transfers between devices, swapped(): lax.ppermute(value, axis, [(source, source ^ bits) for source in range(la...  9.25 us
    ppermute x2, starting transfers between devices, shifted(): lax.ppermute(value, axis, [(source, (source + steps) % count) for source...  5.85 us
    unnamed x12, local copies, waits for them, and re-layouts  2.45 us
    ppermute x1, starting transfers between devices, per_device(): lax.ppermute(cross_queries, 'enc', [(0, 0), (1, 2), (2, 1), (3, 3)])  1.6 us
    pallas_call x1, Pallas kernels, seen_table(): pl.pallas_call(table_kernel, out_shape=jax.ShapeDtypeStruct((slots * (blo...  1.34 us
    pallas_call x1, Pallas kernels, self_first(): pl.pallas_call(functools.partial(self_first_kernel, group), out_shape=(ja...  1.09 us
  transfers between devices with their start and end apart: 9, of which 3 were waited for; matrix products, arithmetic and copies ran while one was open for 3% of the time, Pallas kernels for 42%

profile of v6, /device:TPU:0, one launch (start us, length us, event | category | flops | bytes accessed | tf_op | source)
XLA Modules:
  0.0 52.6 jit_solution(12124051110882114129)
XLA Ops:
  0.6 3.0 %collective-permute-start.3 = (bf16[1,2,1601,128]{3,1,2,0:T(2,128)(2,1)}, bf16[1,2,1601,128]{3,1,2,0:T(2,128)(2,1)S(1)}, u32[]{:S(2)}, u32[]{:S(2)}) collective-permute-start(bf16[1,2,1601,128]{3,1,2,0:T(2,128)(2,1)} %param.9), channel_id=1, source_target_pairs={{0,16},{16,0},{1,17},{17,1},{2,18},{18,2},{3,19},{19,3},{4,20},{20... | collective-permute-start | bytes 2459144 | tf_op jit(solution)/shard_map/ppermute | solution.py:440
  3.6 2.6 %collective-permute-start.2 = (bf16[512,256]{1,0:T(8,128)(2,1)}, bf16[512,256]{1,0:T(8,128)(2,1)S(1)}, u32[]{:S(2)}, u32[]{:S(2)}) collective-permute-start(bf16[512,256]{1,0:T(8,128)(2,1)} %refs_0_.2), channel_id=1, source_target_pairs={{0,2},{1,3},{2,0},{3,1},{4,6},{5,7},{6,4},{7,5},{8,10},{9,11},{10,... | collective-permute-start | bytes 786440 | tf_op jit(solution)/shard_map/ppermute | solution.py:444
  6.2 1.6 %collective-permute-start.1 = (bf16[512,256]{1,0:T(8,128)(2,1)}, bf16[512,256]{1,0:T(8,128)(2,1)S(1)}, u32[]{:S(2)}, u32[]{:S(2)}) collective-permute-start(bf16[512,256]{1,0:T(8,128)(2,1)} %refs_0_.2), channel_id=1, source_target_pairs={{0,0},{1,2},{2,1},{3,3},{4,4},{5,6},{6,5},{7,7},{8,8},{9,10},{10,9... | collective-permute-start | bytes 786440 | tf_op jit(solution)/shard_map/ppermute | solution.py:468
  7.8 2.0 %collective-permute-start = (bf16[512,256]{1,0:T(8,128)(2,1)}, bf16[512,256]{1,0:T(8,128)(2,1)S(1)}, u32[]{:S(2)}, u32[]{:S(2)}) collective-permute-start(bf16[512,256]{1,0:T(8,128)(2,1)} %refs_0_.2), channel_id=1, source_target_pairs={{0,1},{1,0},{2,3},{3,2},{4,5},{5,4},{6,7},{7,6},{8,9},{9,8},{10,11... | collective-permute-start | bytes 786440 | tf_op jit(solution)/shard_map/ppermute | solution.py:444
  9.8 1.3 %copy.17 = bf16[1,2,1601,128]{3,2,1,0:T(8,128)(2,1)S(1)} copy(bf16[1,2,1601,128]{3,1,2,0:T(2,128)(2,1)} %param.9) | data formatting | bytes 1639424 | tf_op args[3]
  11.0 0.0 copy-start.3
  11.1 0.2 prepare.2.refs_1_.refs_2_
  11.3 1.3 %seen_table.1.table_ref = s32[11]{0:T(128)} custom-call(s32[1]{0:T(128)} %bitcast.position_ref, s32[1]{0:T(128)} %bitcast.1.inside_ref, s32[2,4]{1,0:T(2,128)} %bitcast.18, s32[2]{0:T(128)} %owner_ref.1), custom_call_target="tpu_custom_call" | custom-call | tf_op jit(solution)/shard_map/seen_table/pallas_call | solution.py:123
  12.6 0.0 copy-done.3
  12.6 0.0 copy-start.1
  12.6 0.7 %copy-done.1 = s32[11]{0:T(128)S(1)} copy-done((s32[11]{0:T(128)S(1)}, s32[11]{0:T(128)}, u32[]{:S(2)}) %copy-start.1) | copy-done | bytes 68
  13.3 2.9 %cross_first.2 = (f32[4,8,256]{2,1,0:T(8,128)S(1)}, f32[4,144,256]{2,1,0:T(8,128)S(1)}) custom-call(s32[11]{0:T(128)S(1)} %copy-done.1, bf16[512,256]{1,0:T(8,128)(2,1)S(1)} %copy-done.3, bf16[2,1664,128]{2,1,0:T(8,128)(2,1)S(1)} %prepare.2.refs_1_.refs_2_), custom_call_target="tpu_custom_call" | custom-call | flops 2000000000 | bytes 1024 | tf_op jit(solution)/shard_map/cross_first/pallas_call | solution.py:261
  16.2 3.1 %collective-permute-done.2.refs_0_ = bf16[512,256]{1,0:T(8,128)(2,1)S(1)} collective-permute-done((bf16[512,256]{1,0:T(8,128)(2,1)}, bf16[512,256]{1,0:T(8,128)(2,1)S(1)}, u32[]{:S(2)}, u32[]{:S(2)}) %collective-permute-start.2) | collective-permute-done | bytes 262176 | tf_op jit(solution)/shard_map/ppermute | solution.py:444
  19.3 0.0 collective-permute-start.4
  19.3 2.9 %cross_first.3 = (f32[4,8,256]{2,1,0:T(8,128)S(1)}, f32[4,144,256]{2,1,0:T(8,128)S(1)}) custom-call(s32[11]{0:T(128)S(1)} %copy-done.1, bf16[512,256]{1,0:T(8,128)(2,1)S(1)} %collective-permute-done.2.refs_0_, bf16[2,1664,128]{2,1,0:T(8,128)(2,1)S(1)} %prepare.2.refs_1_.refs_2_), custom_call_target="tpu_custom_call" | custom-call | flops 2000000000 | bytes 1024 | tf_op jit(solution)/shard_map/cross_first/pallas_call | solution.py:261
  22.3 0.0 collective-permute-done.3
  22.3 0.1 copy.16
  22.4 0.0 copy-start.2
  22.4 0.2 prepare.3.refs_1_.refs_3_.refs_2_
  22.6 0.5 copy-done.2
  23.1 1.9 %cross_last.4 = bf16[528,256]{1,0:T(8,128)(2,1)S(1)} custom-call(s32[11]{0:T(128)S(1)} %copy-done.2, bf16[512,256]{1,0:T(8,128)(2,1)S(1)} %collective-permute-done.2.refs_0_, bf16[2,1664,128]{2,1,0:T(8,128)(2,1)S(1)} %prepare.3.refs_1_.refs_3_.refs_2_, f32[4,8,256]{2,1,0:T(8,128)S(1)} %get-tuple-element.25.refs_2_, f32[4,144,256]{2,1,0:T(8,128)S(1)} %get-tuple-element.26.refs_3_), custom_call_target="tpu_custom_call" | custom-call | flops 2000000000 | bytes 1024 | tf_op jit(solution)/shard_map/cross_last/pallas_call | solution.py:261
  25.0 0.0 copy-start.4
  25.0 3.0 %collective-permute-start.6 = (bf16[528,256]{1,0:T(8,128)(2,1)S(1)}, bf16[528,256]{1,0:T(8,128)(2,1)S(1)}, u32[]{:S(2)}, u32[]{:S(2)}) collective-permute-start(bf16[528,256]{1,0:T(8,128)(2,1)S(1)} %cross_last.4), channel_id=1, source_target_pairs={{0,2},{1,3},{2,0},{3,1},{4,6},{5,7},{6,4},{7,5},{8,10},{9,11},{10,... | collective-permute-start | bytes 811016 | tf_op jit(solution)/shard_map/ppermute | solution.py:444
  28.1 0.0 collective-permute-done.4.refs_1_
  28.1 0.0 collective-permute-done.1.refs_0_
  28.1 4.1 %cross_last.5 = bf16[528,256]{1,0:T(8,128)(2,1)S(1)} custom-call(s32[11]{0:T(128)S(1)} %copy-done.2, bf16[512,256]{1,0:T(8,128)(2,1)S(1)} %collective-permute-done.1.refs_0_, bf16[512,256]{1,0:T(8,128)(2,1)S(1)} %collective-permute-done.4.refs_1_, bf16[2,1664,128]{2,1,0:T(8,128)(2,1)S(1)} %prepare.2.refs_1_.refs_2_, ...), custom_call_target="tpu_custom_call" | custom-call | flops 2000000000 | bytes 1024 | tf_op jit(solution)/shard_map/cross_last/pallas_call | solution.py:261
  32.1 1.9 %collective-permute-start.7 = (bf16[528,256]{1,0:T(8,128)(2,1)S(1)}, bf16[528,256]{1,0:T(8,128)(2,1)S(1)}, u32[]{:S(2)}, u32[]{:S(2)}) collective-permute-start(bf16[528,256]{1,0:T(8,128)(2,1)S(1)} %cross_last.5), channel_id=1, source_target_pairs={{0,3},{1,2},{2,1},{3,0},{4,7},{5,6},{6,5},{7,4},{8,11},{9,10},{10,... | collective-permute-start | bytes 811016 | tf_op jit(solution)/shard_map/ppermute | solution.py:444
  34.0 0.0 collective-permute-done.refs_0_
  34.0 0.0 copy-done.4
  34.1 2.8 %collective-permute-start.5 = (bf16[512,256]{1,0:T(8,128)(2,1)S(1)}, bf16[512,256]{1,0:T(8,128)(2,1)S(1)}, u32[]{:S(2)}, u32[]{:S(2)}) collective-permute-start(bf16[512,256]{1,0:T(8,128)(2,1)S(1)} %bitcast.15), channel_id=1, source_target_pairs={{0,16},{16,0},{1,17},{17,1},{2,18},{18,2},{3,19},{19,3},{4,20},{20... | collective-permute-start | bytes 786440 | tf_op jit(solution)/shard_map/ppermute | solution.py:440
  36.9 4.0 %cross_last.6 = bf16[528,256]{1,0:T(8,128)(2,1)S(1)} custom-call(s32[11]{0:T(128)S(1)} %copy-done.2, bf16[512,256]{1,0:T(8,128)(2,1)S(1)} %collective-permute-done.refs_0_, bf16[2,1664,128]{2,1,0:T(8,128)(2,1)S(1)} %prepare.2.refs_1_.refs_2_, bf16[2,1664,128]{2,1,0:T(8,128)(2,1)S(1)} %prepare.3.refs_1_.refs_3_.refs_2_), custom_call_target="tpu_custom_call" | custom-call | flops 2000000000 | bytes 1024 | tf_op jit(solution)/shard_map/cross_last/pallas_call | solution.py:261
  41.0 0.0 copy-start
  41.0 0.3 collective-permute-start.8
  41.3 2.1 %cross_last.7.refs_0_ = bf16[528,256]{1,0:T(8,128)(2,1)S(1)} custom-call(s32[11]{0:T(128)S(1)} %copy-done.2, bf16[512,256]{1,0:T(8,128)(2,1)S(1)} %copy-done.3, bf16[2,1664,128]{2,1,0:T(8,128)(2,1)S(1)} %prepare.3.refs_1_.refs_3_.refs_2_, f32[4,8,256]{2,1,0:T(8,128)S(1)} %get-tuple-element.22.refs_2_, f32[4,144,256]{2,1,0:T(8,128)S(1)} %get-tuple-element.23.refs_3_), custom_call_target="tpu_custom_call" | custom-call | flops 2000000000 | bytes 1024 | tf_op jit(solution)/shard_map/cross_last/pallas_call | solution.py:261
  43.4 0.0 copy-done
  43.4 1.1 %self_first.1 = (f32[2,8,512]{2,1,0:T(8,128)S(1)}, f32[2,144,512]{2,1,0:T(8,128)S(1)}) custom-call(bf16[512,256]{1,0:T(8,128)(2,1)S(1)} %copy-done, bf16[512,256]{1,0:T(8,128)(2,1)S(1)} %bitcast.16), custom_call_target="tpu_custom_call" | custom-call | bytes 1024 | tf_op jit(solution)/shard_map/self_first/pallas_call | solution.py:407
  44.5 0.0 collective-permute-done.5.refs_0_
  44.5 0.9 %self_last.1 = bf16[512,256]{1,0:T(8,128)(2,1)} custom-call(s32[1]{0:T(128)} %bitcast.position_ref, bf16[512,256]{1,0:T(8,128)(2,1)S(1)} %copy-done, f32[2,8,512]{2,1,0:T(8,128)S(1)} %get-tuple-element.34.high_ref, f32[2,144,512]{2,1,0:T(8,128)S(1)} %get-tuple-element.35.mixed_ref, bf16[512,256]{1,0:T(8,128)(2,1)S(1)} %collective-permute-done.5.refs_0_), custom_call_target="tpu_custom_call" | custom-call | bytes 1024 | tf_op jit(solution)/shard_map/self_last/pallas_call | solution.py:425
  45.4 0.7 %collective-permute-done.6.refs_1_ = bf16[528,256]{1,0:T(8,128)(2,1)S(1)} collective-permute-done((bf16[528,256]{1,0:T(8,128)(2,1)S(1)}, bf16[528,256]{1,0:T(8,128)(2,1)S(1)}, u32[]{:S(2)}, u32[]{:S(2)}) %collective-permute-start.6) | collective-permute-done | bytes 270368 | tf_op jit(solution)/shard_map/ppermute | solution.py:444
  46.1 0.1 combine.2
  46.2 0.0 collective-permute-done.7.refs_2_
  46.2 0.1 combine.3
  46.3 5.4 %collective-permute-done.8.refs_2_ = bf16[528,256]{1,0:T(8,128)(2,1)S(1)} collective-permute-done((bf16[528,256]{1,0:T(8,128)(2,1)S(1)}, bf16[528,256]{1,0:T(8,128)(2,1)S(1)}, u32[]{:S(2)}, u32[]{:S(2)}) %collective-permute-start.8) | collective-permute-done | bytes 270368 | tf_op jit(solution)/shard_map/ppermute | solution.py:444
  51.7 0.9 %combine_last.1 = bf16[512,256]{1,0:T(8,128)(2,1)} custom-call(f32[512,256]{1,0:T(8,128)S(1)} %get-tuple-element.40.refs_0_, f32[4,256]{1,0:T(4,128)S(1)} %get-tuple-element.41.refs_1_, bf16[528,256]{1,0:T(8,128)(2,1)S(1)} %collective-permute-done.8.refs_2_), custom_call_target="tpu_custom_call" | custom-call | flops 2000000000 | bytes 1024 | tf_op jit(solution)/shard_map/combine_last/pallas_call | solution.py:336
  (1 shorter events, 0.0 us)
Async XLA Ops:
  0.6 21.7 %collective-permute-start.3 = (bf16[1,2,1601,128]{3,1,2,0:T(2,128)(2,1)}, bf16[1,2,1601,128]{3,1,2,0:T(2,128)(2,1)S(1)}, u32[]{:S(2)}, u32[]{:S(2)}) collective-permute-start(bf16[1,2,1601,128]{3,1,2,0:T(2,128)(2,1)} %param.9), channel_id=1, source_target_pairs={{0,16},{16,0},{1,17},{17,1},{2,18},{18,2},{3,19},{19,3},{4,20},{20... | collective-permute-start | bytes 2459144 | tf_op jit(solution)/shard_map/ppermute | solution.py:440
  3.6 15.7 %collective-permute-start.2 = (bf16[512,256]{1,0:T(8,128)(2,1)}, bf16[512,256]{1,0:T(8,128)(2,1)S(1)}, u32[]{:S(2)}, u32[]{:S(2)}) collective-permute-start(bf16[512,256]{1,0:T(8,128)(2,1)} %refs_0_.2), channel_id=1, source_target_pairs={{0,2},{1,3},{2,0},{3,1},{4,6},{5,7},{6,4},{7,5},{8,10},{9,11},{10,... | collective-permute-start | bytes 786440 | tf_op jit(solution)/shard_map/ppermute | solution.py:444
  6.2 21.8 %collective-permute-start.1 = (bf16[512,256]{1,0:T(8,128)(2,1)}, bf16[512,256]{1,0:T(8,128)(2,1)S(1)}, u32[]{:S(2)}, u32[]{:S(2)}) collective-permute-start(bf16[512,256]{1,0:T(8,128)(2,1)} %refs_0_.2), channel_id=1, source_target_pairs={{0,0},{1,2},{2,1},{3,3},{4,4},{5,6},{6,5},{7,7},{8,8},{9,10},{10,9... | collective-permute-start | bytes 786440 | tf_op jit(solution)/shard_map/ppermute | solution.py:468
  7.8 26.2 %collective-permute-start = (bf16[512,256]{1,0:T(8,128)(2,1)}, bf16[512,256]{1,0:T(8,128)(2,1)S(1)}, u32[]{:S(2)}, u32[]{:S(2)}) collective-permute-start(bf16[512,256]{1,0:T(8,128)(2,1)} %refs_0_.2), channel_id=1, source_target_pairs={{0,1},{1,0},{2,3},{3,2},{4,5},{5,4},{6,7},{7,6},{8,9},{9,8},{10,11... | collective-permute-start | bytes 786440 | tf_op jit(solution)/shard_map/ppermute | solution.py:444
  11.0 1.6 %copy-start.3 = (bf16[512,256]{1,0:T(8,128)(2,1)S(1)}, bf16[512,256]{1,0:T(8,128)(2,1)}, u32[]{:S(2)}) copy-start(bf16[512,256]{1,0:T(8,128)(2,1)} %refs_0_.2) | copy-start | bytes 786436
  12.6 0.7 %copy-start.1 = (s32[11]{0:T(128)S(1)}, s32[11]{0:T(128)}, u32[]{:S(2)}) copy-start(s32[11]{0:T(128)} %seen_table.1.table_ref) | copy-start | bytes 136
  19.3 8.7 %collective-permute-start.4 = (bf16[512,256]{1,0:T(8,128)(2,1)S(1)}, bf16[512,256]{1,0:T(8,128)(2,1)S(1)}, u32[]{:S(2)}, u32[]{:S(2)}) collective-permute-start(bf16[512,256]{1,0:T(8,128)(2,1)S(1)} %collective-permute-done.2.refs_0_), channel_id=1, source_target_pairs={{0,1},{1,0},{2,3},{3,2},{4,5},{5,4},{6,7},{7,6},{8,9},{9,8},{10,11... | collective-permute-start | bytes 786440 | tf_op jit(solution)/shard_map/ppermute | solution.py:444
  22.4 0.7 %copy-start.2 = (s32[11]{0:T(128)S(1)}, s32[11]{0:T(128)}, u32[]{:S(2)}) copy-start(s32[11]{0:T(128)} %seen_table.1.table_ref) | copy-start | bytes 136
  25.0 9.0 %copy-start.4 = (bf16[512,2,128]{2,1,0:T(2,128)(2,1)S(1)}, bf16[512,2,128]{2,1,0:T(2,128)(2,1)}, u32[]{:S(2)}) copy-start(bf16[512,2,128]{2,1,0:T(2,128)(2,1)} %param.7) | copy-start | bytes 786436
  25.0 21.1 %collective-permute-start.6 = (bf16[528,256]{1,0:T(8,128)(2,1)S(1)}, bf16[528,256]{1,0:T(8,128)(2,1)S(1)}, u32[]{:S(2)}, u32[]{:S(2)}) collective-permute-start(bf16[528,256]{1,0:T(8,128)(2,1)S(1)} %cross_last.4), channel_id=1, source_target_pairs={{0,2},{1,3},{2,0},{3,1},{4,6},{5,7},{6,4},{7,5},{8,10},{9,11},{10,... | collective-permute-start | bytes 811016 | tf_op jit(solution)/shard_map/ppermute | solution.py:444
  32.1 14.1 %collective-permute-start.7 = (bf16[528,256]{1,0:T(8,128)(2,1)S(1)}, bf16[528,256]{1,0:T(8,128)(2,1)S(1)}, u32[]{:S(2)}, u32[]{:S(2)}) collective-permute-start(bf16[528,256]{1,0:T(8,128)(2,1)S(1)} %cross_last.5), channel_id=1, source_target_pairs={{0,3},{1,2},{2,1},{3,0},{4,7},{5,6},{6,5},{7,4},{8,11},{9,10},{10,... | collective-permute-start | bytes 811016 | tf_op jit(solution)/shard_map/ppermute | solution.py:444
  34.1 10.4 %collective-permute-start.5 = (bf16[512,256]{1,0:T(8,128)(2,1)S(1)}, bf16[512,256]{1,0:T(8,128)(2,1)S(1)}, u32[]{:S(2)}, u32[]{:S(2)}) collective-permute-start(bf16[512,256]{1,0:T(8,128)(2,1)S(1)} %bitcast.15), channel_id=1, source_target_pairs={{0,16},{16,0},{1,17},{17,1},{2,18},{18,2},{3,19},{19,3},{4,20},{20... | collective-permute-start | bytes 786440 | tf_op jit(solution)/shard_map/ppermute | solution.py:440
  41.0 2.4 %copy-start = (bf16[512,256]{1,0:T(8,128)(2,1)S(1)}, bf16[512,256]{1,0:T(8,128)(2,1)}, u32[]{:S(2)}) copy-start(bf16[512,256]{1,0:T(8,128)(2,1)} %q_ref.1) | copy-start | bytes 786436
  41.0 10.8 %collective-permute-start.8 = (bf16[528,256]{1,0:T(8,128)(2,1)S(1)}, bf16[528,256]{1,0:T(8,128)(2,1)S(1)}, u32[]{:S(2)}, u32[]{:S(2)}) collective-permute-start(bf16[528,256]{1,0:T(8,128)(2,1)S(1)} %cross_last.6), channel_id=1, source_target_pairs={{0,1},{1,0},{2,3},{3,2},{4,5},{5,4},{6,7},{7,6},{8,9},{9,8},{10,11... | collective-permute-start | bytes 811016 | tf_op jit(solution)/shard_map/ppermute | solution.py:444

commit v7 on v6

--- a/solution.py
+++ b/solution.py
@@ -92,7 +92,7 @@
     return next(count for count in range(1, rows) if count * HEAD_SIZE + lse_rows(count) == rows)
 
 
-def table_kernel(position_ref, inside_ref, images_ref, owner_ref, table_ref):
+def table_kernel(position_ref, inside_ref, images_ref, owner_ref, out_ref, table_ref):
     slots, block_count = images_ref.shape
     for piece in range(slots):
         slot = lax.rem(position_ref[0] + (slots - piece), slots)
@@ -115,16 +115,22 @@
 
             count = count + jnp.where(seen > 0, 1, 0)
         table_ref[base] = count
-    table_ref[slots * (block_count + 1)] = inside_ref[0]
+    lane = lax.broadcasted_iota(jnp.int32, out_ref.shape, 1)
+    table = jnp.where(lane == out_ref.shape[1] - 1, inside_ref[0], 0)
+    for index in range(table_ref.shape[0]):
+        table = jnp.where(lane == index, table_ref[index], table)
+    out_ref[...] = table
 
 
 def seen_table(position, inside, block_images, image_owner):
     block_count, slots = block_images.shape
+    size = slots * (block_count + 1)
     return pl.pallas_call(
         table_kernel,
-        out_shape=jax.ShapeDtypeStruct((slots * (block_count + 1) + 1,), jnp.int32),
+        out_shape=jax.ShapeDtypeStruct((1, padded(size + 1)), jnp.int32),
         in_specs=[SMEM] * 4,
-        out_specs=SMEM,
+        out_specs=VMEM,
+        scratch_shapes=[pltpu.SMEM((size,), jnp.int32)],
         name="seen_table",
     )(position, inside, block_images.T, image_owner)
 
@@ -151,7 +157,7 @@
         width = image.shape[1]
         queries = [q_refs[0][at_block(block), :] for block in blocks]
         if parts > 1:
-            first = table_ref[table_ref.shape[0] - 1] > 0
+            first = table_ref[0, table_ref.shape[1] - 1] > 0
             queries = [jnp.where(first, one, q_refs[1][at_block(block), :]) for one, block in zip(queries, blocks)]
         queries = jnp.concatenate([stacked_heads(one) for one in queries], axis=0)
         chunks = chunks_of(width)
@@ -207,13 +213,13 @@
         def _():
             for piece in range(pieces):
                 base = (offset + piece) * (block_count + 1)
-                count = table_ref[base]
+                count = table_ref[0, base]
                 if piece == 0:
                     held = before if offset else None
                     for block in range(block_count):
                         seen = functools.reduce(
                             jnp.logical_or,
-                            [(count > index) & (table_ref[base + 1 + index] == block) for index in range(block_count)],
+                            [(count > index) & (table_ref[0, base + 1 + index] == block) for index in range(block_count)],
                         )
 
                         @pl.when(jnp.logical_not(seen))
@@ -229,7 +235,7 @@
                     held = (high_ref, mixed_ref)
 
                 def pair_step(pair, carry, piece=piece, base=base, count=count, held=held):
-                    blocks = [table_ref[base + 1 + 2 * pair], table_ref[base + jnp.minimum(2 * pair + 2, count)]]
+                    blocks = [table_ref[0, base + 1 + 2 * pair], table_ref[0, base + jnp.minimum(2 * pair + 2, count)]]
                     fold_pair(blocks, images[piece], trial > 0, held)
                     return carry
 

time: 52.9 us -> 51.8 us (0.979)
  Pallas kernels: 22.7 us -> 18.6 us
  starting transfers between devices: 17.2 us -> 19.4 us
  waiting for transfers between devices: 9.26 us -> 10.2 us
    pallas_call x6, Pallas kernels: 17.9 us -> 13.7 us  [cross_part(): pl.pallas_call(functools.partial(cross_kernel, key_count, len(images), of...]
    ppermute x6, starting transfers between devices: 9.79 us -> 10.9 us  [swapped(): lax.ppermute(value, axis, [(source, source ^ bits) for source in range(la...]
    ppermute x2, starting transfers between devices: 5.85 us -> 6.93 us  [shifted(): lax.ppermute(value, axis, [(source, (source + steps) % count) for source...]
    ppermute x6, waiting for transfers between devices: 9.25 us -> 10.2 us  [swapped(): lax.ppermute(value, axis, [(source, source ^ bits) for source in range(la...]
  transfers between devices with their start and end apart: 9 -> 9, of which waited for: 3 -> 3; matrix products, arithmetic and copies ran while one was open for 3% -> 3% of each run, Pallas kernels for 42% -> 34%
where the time goes in v7:
time: 51.8 us; the launch traced here: 51.6 us
  starting transfers between devices  19.4 us (37%)
  Pallas kernels  18.6 us (36%)
  waiting for transfers between devices  10.2 us (20%)
  local copies, waits for them, and re-layouts  2.57 us (5%)
  between operations  0.81 us (2%)
    pallas_call x6, Pallas kernels, cross_part(): pl.pallas_call(functools.partial(cross_kernel, key_count, len(images), of...  13.7 us
    ppermute x6, starting transfers between devices, swapped(): lax.ppermute(value, axis, [(source, source ^ bits) for source in range(la...  10.9 us
    ppermute x6, waiting for transfers between devices, swapped(): lax.ppermute(value, axis, [(source, source ^ bits) for source in range(la...  10.2 us
    ppermute x2, starting transfers between devices, shifted(): lax.ppermute(value, axis, [(source, (source + steps) % count) for source...  6.93 us
    unnamed x12, local copies, waits for them, and re-layouts  2.46 us
    ppermute x1, starting transfers between devices, per_device(): lax.ppermute(cross_queries, 'enc', [(0, 0), (1, 2), (2, 1), (3, 3)])  1.6 us
    pallas_call x1, Pallas kernels, seen_table(): pl.pallas_call(table_kernel, out_shape=jax.ShapeDtypeStruct((1, padded(si...  1.42 us
    pallas_call x1, Pallas kernels, self_first(): pl.pallas_call(functools.partial(self_first_kernel, group), out_shape=(ja...  1.09 us
  transfers between devices with their start and end apart: 9, of which 3 were waited for; matrix products, arithmetic and copies ran while one was open for 3% of the time, Pallas kernels for 34%

profile of v7, /device:TPU:0, one launch (start us, length us, event | category | flops | bytes accessed | tf_op | source)
XLA Modules:
  0.0 51.6 jit_solution(3792877185701386675)
XLA Ops:
  0.6 3.0 %collective-permute-start.3 = (bf16[1,2,1601,128]{3,1,2,0:T(2,128)(2,1)}, bf16[1,2,1601,128]{3,1,2,0:T(2,128)(2,1)S(1)}, u32[]{:S(2)}, u32[]{:S(2)}) collective-permute-start(bf16[1,2,1601,128]{3,1,2,0:T(2,128)(2,1)} %param.9), channel_id=1, source_target_pairs={{0,16},{16,0},{1,17},{17,1},{2,18},{18,2},{3,19},{19,3},{4,20},{20... | collective-permute-start | bytes 2459144 | tf_op jit(solution)/shard_map/ppermute | solution.py:446
  3.6 2.6 %collective-permute-start.2 = (bf16[512,256]{1,0:T(8,128)(2,1)}, bf16[512,256]{1,0:T(8,128)(2,1)S(1)}, u32[]{:S(2)}, u32[]{:S(2)}) collective-permute-start(bf16[512,256]{1,0:T(8,128)(2,1)} %refs_0_.2), channel_id=1, source_target_pairs={{0,2},{1,3},{2,0},{3,1},{4,6},{5,7},{6,4},{7,5},{8,10},{9,11},{10,... | collective-permute-start | bytes 786440 | tf_op jit(solution)/shard_map/ppermute | solution.py:450
  6.2 1.6 %collective-permute-start.1 = (bf16[512,256]{1,0:T(8,128)(2,1)}, bf16[512,256]{1,0:T(8,128)(2,1)S(1)}, u32[]{:S(2)}, u32[]{:S(2)}) collective-permute-start(bf16[512,256]{1,0:T(8,128)(2,1)} %refs_0_.2), channel_id=1, source_target_pairs={{0,0},{1,2},{2,1},{3,3},{4,4},{5,6},{6,5},{7,7},{8,8},{9,10},{10,9... | collective-permute-start | bytes 786440 | tf_op jit(solution)/shard_map/ppermute | solution.py:474
  7.8 2.0 %collective-permute-start = (bf16[512,256]{1,0:T(8,128)(2,1)}, bf16[512,256]{1,0:T(8,128)(2,1)S(1)}, u32[]{:S(2)}, u32[]{:S(2)}) collective-permute-start(bf16[512,256]{1,0:T(8,128)(2,1)} %refs_0_.2), channel_id=1, source_target_pairs={{0,1},{1,0},{2,3},{3,2},{4,5},{5,4},{6,7},{7,6},{8,9},{9,8},{10,11... | collective-permute-start | bytes 786440 | tf_op jit(solution)/shard_map/ppermute | solution.py:450
  9.8 1.3 %copy.17 = bf16[1,2,1601,128]{3,2,1,0:T(8,128)(2,1)S(1)} copy(bf16[1,2,1601,128]{3,1,2,0:T(2,128)(2,1)} %param.9) | data formatting | bytes 1639424 | tf_op args[3]
  11.0 0.0 copy-start.3
  11.1 0.2 prepare.2.refs_1_.refs_2_
  11.3 1.4 %seen_table.1.table_ref = s32[1,128]{1,0:T(1,128)} custom-call(s32[1]{0:T(128)} %bitcast.position_ref, s32[1]{0:T(128)} %bitcast.1.inside_ref, s32[2,4]{1,0:T(2,128)} %bitcast.18, s32[2]{0:T(128)} %owner_ref.1), custom_call_target="tpu_custom_call" | custom-call | tf_op jit(solution)/shard_map/seen_table/pallas_call | solution.py:128
  12.7 0.0 copy-done.3
  12.7 0.0 copy-start.1
  12.7 0.7 %copy-done.1 = s32[1,128]{1,0:T(1,128)S(1)} copy-done((s32[1,128]{1,0:T(1,128)S(1)}, s32[1,128]{1,0:T(1,128)}, u32[]{:S(2)}) %copy-start.1) | copy-done | bytes 536
  13.3 2.9 %cross_first.2 = (f32[4,8,256]{2,1,0:T(8,128)S(1)}, f32[4,144,256]{2,1,0:T(8,128)S(1)}) custom-call(s32[1,128]{1,0:T(1,128)S(1)} %copy-done.1, bf16[512,256]{1,0:T(8,128)(2,1)S(1)} %copy-done.3, bf16[2,1664,128]{2,1,0:T(8,128)(2,1)S(1)} %prepare.2.refs_1_.refs_2_), custom_call_target="tpu_custom_call" | custom-call | flops 2000000000 | bytes 1024 | tf_op jit(solution)/shard_map/cross_first/pallas_call | solution.py:267
  16.3 3.1 %collective-permute-done.2.refs_0_ = bf16[512,256]{1,0:T(8,128)(2,1)S(1)} collective-permute-done((bf16[512,256]{1,0:T(8,128)(2,1)}, bf16[512,256]{1,0:T(8,128)(2,1)S(1)}, u32[]{:S(2)}, u32[]{:S(2)}) %collective-permute-start.2) | collective-permute-done | bytes 262176 | tf_op jit(solution)/shard_map/ppermute | solution.py:450
  19.3 0.0 collective-permute-start.4
  19.3 2.9 %cross_first.3 = (f32[4,8,256]{2,1,0:T(8,128)S(1)}, f32[4,144,256]{2,1,0:T(8,128)S(1)}) custom-call(s32[1,128]{1,0:T(1,128)S(1)} %copy-done.1, bf16[512,256]{1,0:T(8,128)(2,1)S(1)} %collective-permute-done.2.refs_0_, bf16[2,1664,128]{2,1,0:T(8,128)(2,1)S(1)} %prepare.2.refs_1_.refs_2_), custom_call_target="tpu_custom_call" | custom-call | flops 2000000000 | bytes 1024 | tf_op jit(solution)/shard_map/cross_first/pallas_call | solution.py:267
  22.3 0.0 collective-permute-done.3
  22.3 0.1 copy.16
  22.4 0.0 copy-start.2
  22.4 0.2 prepare.3.refs_1_.refs_3_.refs_2_
  22.6 0.5 copy-done.2
  23.1 0.9 %cross_last.4 = bf16[528,256]{1,0:T(8,128)(2,1)S(1)} custom-call(s32[1,128]{1,0:T(1,128)S(1)} %copy-done.2, bf16[512,256]{1,0:T(8,128)(2,1)S(1)} %collective-permute-done.2.refs_0_, bf16[2,1664,128]{2,1,0:T(8,128)(2,1)S(1)} %prepare.3.refs_1_.refs_3_.refs_2_, f32[4,8,256]{2,1,0:T(8,128)S(1)} %get-tuple-element.25.refs_2_, ...), custom_call_target="tpu_custom_call" | custom-call | flops 2000000000 | bytes 1024 | tf_op jit(solution)/shard_map/cross_last/pallas_call | solution.py:267
  24.0 0.0 copy-start.4
  24.0 3.0 %collective-permute-start.6 = (bf16[528,256]{1,0:T(8,128)(2,1)S(1)}, bf16[528,256]{1,0:T(8,128)(2,1)S(1)}, u32[]{:S(2)}, u32[]{:S(2)}) collective-permute-start(bf16[528,256]{1,0:T(8,128)(2,1)S(1)} %cross_last.4), channel_id=1, source_target_pairs={{0,2},{1,3},{2,0},{3,1},{4,6},{5,7},{6,4},{7,5},{8,10},{9,11},{10,... | collective-permute-start | bytes 811016 | tf_op jit(solution)/shard_map/ppermute | solution.py:450
  27.0 0.0 collective-permute-done.4.refs_1_
  27.0 0.0 collective-permute-done.1.refs_0_
  27.0 3.0 %cross_last.5 = bf16[528,256]{1,0:T(8,128)(2,1)S(1)} custom-call(s32[1,128]{1,0:T(1,128)S(1)} %copy-done.2, bf16[512,256]{1,0:T(8,128)(2,1)S(1)} %collective-permute-done.1.refs_0_, bf16[512,256]{1,0:T(8,128)(2,1)S(1)} %collective-permute-done.4.refs_1_, bf16[2,1664,128]{2,1,0:T(8,128)(2,1)S(1)} %prepare.2.refs_1_.refs_2_, ...), custom_call_target="tpu_custom_call" | custom-call | flops 2000000000 | bytes 1024 | tf_op jit(solution)/shard_map/cross_last/pallas_call | solution.py:267
  30.0 3.0 %collective-permute-start.7 = (bf16[528,256]{1,0:T(8,128)(2,1)S(1)}, bf16[528,256]{1,0:T(8,128)(2,1)S(1)}, u32[]{:S(2)}, u32[]{:S(2)}) collective-permute-start(bf16[528,256]{1,0:T(8,128)(2,1)S(1)} %cross_last.5), channel_id=1, source_target_pairs={{0,3},{1,2},{2,1},{3,0},{4,7},{5,6},{6,5},{7,4},{8,11},{9,10},{10,... | collective-permute-start | bytes 811016 | tf_op jit(solution)/shard_map/ppermute | solution.py:450
  33.0 0.0 collective-permute-done.refs_0_
  33.0 0.0 copy-done.4
  33.0 3.9 %collective-permute-start.5 = (bf16[512,256]{1,0:T(8,128)(2,1)S(1)}, bf16[512,256]{1,0:T(8,128)(2,1)S(1)}, u32[]{:S(2)}, u32[]{:S(2)}) collective-permute-start(bf16[512,256]{1,0:T(8,128)(2,1)S(1)} %bitcast.15), channel_id=1, source_target_pairs={{0,16},{16,0},{1,17},{17,1},{2,18},{18,2},{3,19},{19,3},{4,20},{20... | collective-permute-start | bytes 786440 | tf_op jit(solution)/shard_map/ppermute | solution.py:446
  36.9 3.0 %cross_last.6 = bf16[528,256]{1,0:T(8,128)(2,1)S(1)} custom-call(s32[1,128]{1,0:T(1,128)S(1)} %copy-done.2, bf16[512,256]{1,0:T(8,128)(2,1)S(1)} %collective-permute-done.refs_0_, bf16[2,1664,128]{2,1,0:T(8,128)(2,1)S(1)} %prepare.2.refs_1_.refs_2_, bf16[2,1664,128]{2,1,0:T(8,128)(2,1)S(1)} %prepare.3.refs_1_.refs_3_.refs_2_), custom_call_target="tpu_custom_call" | custom-call | flops 2000000000 | bytes 1024 | tf_op jit(solution)/shard_map/cross_last/pallas_call | solution.py:267
  39.9 0.0 copy-start
  39.9 0.3 collective-permute-start.8
  40.2 1.0 %cross_last.7.refs_0_ = bf16[528,256]{1,0:T(8,128)(2,1)S(1)} custom-call(s32[1,128]{1,0:T(1,128)S(1)} %copy-done.2, bf16[512,256]{1,0:T(8,128)(2,1)S(1)} %copy-done.3, bf16[2,1664,128]{2,1,0:T(8,128)(2,1)S(1)} %prepare.3.refs_1_.refs_3_.refs_2_, f32[4,8,256]{2,1,0:T(8,128)S(1)} %get-tuple-element.22.refs_2_, f32[4,144,256]{2,1,0:T(8,128)S(1)} %get-tuple-element.23.refs_3_), custom_call_target="tpu_custom_call" | custom-call | flops 2000000000 | bytes 1024 | tf_op jit(solution)/shard_map/cross_last/pallas_call | solution.py:267
  41.3 0.0 copy-done
  41.3 1.1 %self_first.1 = (f32[2,8,512]{2,1,0:T(8,128)S(1)}, f32[2,144,512]{2,1,0:T(8,128)S(1)}) custom-call(bf16[512,256]{1,0:T(8,128)(2,1)S(1)} %copy-done, bf16[512,256]{1,0:T(8,128)(2,1)S(1)} %bitcast.16), custom_call_target="tpu_custom_call" | custom-call | bytes 1024 | tf_op jit(solution)/shard_map/self_first/pallas_call | solution.py:413
  42.4 0.0 collective-permute-done.5.refs_0_
  42.4 0.9 %self_last.1 = bf16[512,256]{1,0:T(8,128)(2,1)} custom-call(s32[1]{0:T(128)} %bitcast.position_ref, bf16[512,256]{1,0:T(8,128)(2,1)S(1)} %copy-done, f32[2,8,512]{2,1,0:T(8,128)S(1)} %get-tuple-element.34.high_ref, f32[2,144,512]{2,1,0:T(8,128)S(1)} %get-tuple-element.35.mixed_ref, bf16[512,256]{1,0:T(8,128)(2,1)S(1)} %collective-permute-done.5.refs_0_), custom_call_target="tpu_custom_call" | custom-call | bytes 1024 | tf_op jit(solution)/shard_map/self_last/pallas_call | solution.py:431
  43.3 2.2 %collective-permute-done.6.refs_1_ = bf16[528,256]{1,0:T(8,128)(2,1)S(1)} collective-permute-done((bf16[528,256]{1,0:T(8,128)(2,1)S(1)}, bf16[528,256]{1,0:T(8,128)(2,1)S(1)}, u32[]{:S(2)}, u32[]{:S(2)}) %collective-permute-start.6) | collective-permute-done | bytes 270368 | tf_op jit(solution)/shard_map/ppermute | solution.py:450
  45.5 0.1 combine.2
  45.6 0.0 collective-permute-done.7.refs_2_
  45.6 0.1 combine.3
  45.7 4.9 %collective-permute-done.8.refs_2_ = bf16[528,256]{1,0:T(8,128)(2,1)S(1)} collective-permute-done((bf16[528,256]{1,0:T(8,128)(2,1)S(1)}, bf16[528,256]{1,0:T(8,128)(2,1)S(1)}, u32[]{:S(2)}, u32[]{:S(2)}) %collective-permute-start.8) | collective-permute-done | bytes 270368 | tf_op jit(solution)/shard_map/ppermute | solution.py:450
  50.7 0.9 %combine_last.1 = bf16[512,256]{1,0:T(8,128)(2,1)} custom-call(f32[512,256]{1,0:T(8,128)S(1)} %get-tuple-element.40.refs_0_, f32[4,256]{1,0:T(4,128)S(1)} %get-tuple-element.41.refs_1_, bf16[528,256]{1,0:T(8,128)(2,1)S(1)} %collective-permute-done.8.refs_2_), custom_call_target="tpu_custom_call" | custom-call | flops 2000000000 | bytes 1024 | tf_op jit(solution)/shard_map/combine_last/pallas_call | solution.py:342
  (1 shorter events, 0.0 us)
Async XLA Ops:
  0.6 21.7 %collective-permute-start.3 = (bf16[1,2,1601,128]{3,1,2,0:T(2,128)(2,1)}, bf16[1,2,1601,128]{3,1,2,0:T(2,128)(2,1)S(1)}, u32[]{:S(2)}, u32[]{:S(2)}) collective-permute-start(bf16[1,2,1601,128]{3,1,2,0:T(2,128)(2,1)} %param.9), channel_id=1, source_target_pairs={{0,16},{16,0},{1,17},{17,1},{2,18},{18,2},{3,19},{19,3},{4,20},{20... | collective-permute-start | bytes 2459144 | tf_op jit(solution)/shard_map/ppermute | solution.py:446
  3.6 15.7 %collective-permute-start.2 = (bf16[512,256]{1,0:T(8,128)(2,1)}, bf16[512,256]{1,0:T(8,128)(2,1)S(1)}, u32[]{:S(2)}, u32[]{:S(2)}) collective-permute-start(bf16[512,256]{1,0:T(8,128)(2,1)} %refs_0_.2), channel_id=1, source_target_pairs={{0,2},{1,3},{2,0},{3,1},{4,6},{5,7},{6,4},{7,5},{8,10},{9,11},{10,... | collective-permute-start | bytes 786440 | tf_op jit(solution)/shard_map/ppermute | solution.py:450
  6.2 20.8 %collective-permute-start.1 = (bf16[512,256]{1,0:T(8,128)(2,1)}, bf16[512,256]{1,0:T(8,128)(2,1)S(1)}, u32[]{:S(2)}, u32[]{:S(2)}) collective-permute-start(bf16[512,256]{1,0:T(8,128)(2,1)} %refs_0_.2), channel_id=1, source_target_pairs={{0,0},{1,2},{2,1},{3,3},{4,4},{5,6},{6,5},{7,7},{8,8},{9,10},{10,9... | collective-permute-start | bytes 786440 | tf_op jit(solution)/shard_map/ppermute | solution.py:474
  7.8 25.1 %collective-permute-start = (bf16[512,256]{1,0:T(8,128)(2,1)}, bf16[512,256]{1,0:T(8,128)(2,1)S(1)}, u32[]{:S(2)}, u32[]{:S(2)}) collective-permute-start(bf16[512,256]{1,0:T(8,128)(2,1)} %refs_0_.2), channel_id=1, source_target_pairs={{0,1},{1,0},{2,3},{3,2},{4,5},{5,4},{6,7},{7,6},{8,9},{9,8},{10,11... | collective-permute-start | bytes 786440 | tf_op jit(solution)/shard_map/ppermute | solution.py:450
  11.0 1.6 %copy-start.3 = (bf16[512,256]{1,0:T(8,128)(2,1)S(1)}, bf16[512,256]{1,0:T(8,128)(2,1)}, u32[]{:S(2)}) copy-start(bf16[512,256]{1,0:T(8,128)(2,1)} %refs_0_.2) | copy-start | bytes 786436
  12.7 0.7 %copy-start.1 = (s32[1,128]{1,0:T(1,128)S(1)}, s32[1,128]{1,0:T(1,128)}, u32[]{:S(2)}) copy-start(s32[1,128]{1,0:T(1,128)} %seen_table.1.table_ref) | copy-start | bytes 1540
  19.3 7.7 %collective-permute-start.4 = (bf16[512,256]{1,0:T(8,128)(2,1)S(1)}, bf16[512,256]{1,0:T(8,128)(2,1)S(1)}, u32[]{:S(2)}, u32[]{:S(2)}) collective-permute-start(bf16[512,256]{1,0:T(8,128)(2,1)S(1)} %collective-permute-done.2.refs_0_), channel_id=1, source_target_pairs={{0,1},{1,0},{2,3},{3,2},{4,5},{5,4},{6,7},{7,6},{8,9},{9,8},{10,11... | collective-permute-start | bytes 786440 | tf_op jit(solution)/shard_map/ppermute | solution.py:450
  22.4 0.7 %copy-start.2 = (s32[1,128]{1,0:T(1,128)S(1)}, s32[1,128]{1,0:T(1,128)}, u32[]{:S(2)}) copy-start(s32[1,128]{1,0:T(1,128)} %seen_table.1.table_ref) | copy-start | bytes 1540
  24.0 9.0 %copy-start.4 = (bf16[512,2,128]{2,1,0:T(2,128)(2,1)S(1)}, bf16[512,2,128]{2,1,0:T(2,128)(2,1)}, u32[]{:S(2)}) copy-start(bf16[512,2,128]{2,1,0:T(2,128)(2,1)} %param.7) | copy-start | bytes 786436
  24.0 21.5 %collective-permute-start.6 = (bf16[528,256]{1,0:T(8,128)(2,1)S(1)}, bf16[528,256]{1,0:T(8,128)(2,1)S(1)}, u32[]{:S(2)}, u32[]{:S(2)}) collective-permute-start(bf16[528,256]{1,0:T(8,128)(2,1)S(1)} %cross_last.4), channel_id=1, source_target_pairs={{0,2},{1,3},{2,0},{3,1},{4,6},{5,7},{6,4},{7,5},{8,10},{9,11},{10,... | collective-permute-start | bytes 811016 | tf_op jit(solution)/shard_map/ppermute | solution.py:450
  30.0 15.6 %collective-permute-start.7 = (bf16[528,256]{1,0:T(8,128)(2,1)S(1)}, bf16[528,256]{1,0:T(8,128)(2,1)S(1)}, u32[]{:S(2)}, u32[]{:S(2)}) collective-permute-start(bf16[528,256]{1,0:T(8,128)(2,1)S(1)} %cross_last.5), channel_id=1, source_target_pairs={{0,3},{1,2},{2,1},{3,0},{4,7},{5,6},{6,5},{7,4},{8,11},{9,10},{10,... | collective-permute-start | bytes 811016 | tf_op jit(solution)/shard_map/ppermute | solution.py:450
  33.0 9.4 %collective-permute-start.5 = (bf16[512,256]{1,0:T(8,128)(2,1)S(1)}, bf16[512,256]{1,0:T(8,128)(2,1)S(1)}, u32[]{:S(2)}, u32[]{:S(2)}) collective-permute-start(bf16[512,256]{1,0:T(8,128)(2,1)S(1)} %bitcast.15), channel_id=1, source_target_pairs={{0,16},{16,0},{1,17},{17,1},{2,18},{18,2},{3,19},{19,3},{4,20},{20... | collective-permute-start | bytes 786440 | tf_op jit(solution)/shard_map/ppermute | solution.py:446
  39.9 1.4 %copy-start = (bf16[512,256]{1,0:T(8,128)(2,1)S(1)}, bf16[512,256]{1,0:T(8,128)(2,1)}, u32[]{:S(2)}) copy-start(bf16[512,256]{1,0:T(8,128)(2,1)} %q_ref.1) | copy-start | bytes 786436
  39.9 10.8 %collective-permute-start.8 = (bf16[528,256]{1,0:T(8,128)(2,1)S(1)}, bf16[528,256]{1,0:T(8,128)(2,1)S(1)}, u32[]{:S(2)}, u32[]{:S(2)}) collective-permute-start(bf16[528,256]{1,0:T(8,128)(2,1)S(1)} %cross_last.6), channel_id=1, source_target_pairs={{0,1},{1,0},{2,3},{3,2},{4,5},{5,4},{6,7},{7,6},{8,9},{9,8},{10,11... | collective-permute-start | bytes 811016 | tf_op jit(solution)/shard_map/ppermute | solution.py:450

commit v8 on v7

--- a/solution.py
+++ b/solution.py
@@ -131,6 +131,7 @@
         in_specs=[SMEM] * 4,
         out_specs=VMEM,
         scratch_shapes=[pltpu.SMEM((size,), jnp.int32)],
+        compiler_params=pltpu.CompilerParams(vmem_limit_bytes=VMEM_LIMIT),
         name="seen_table",
     )(position, inside, block_images.T, image_owner)
 

time: 51.8 us -> 51.9 us (level); the launches traced: 51.6 us -> 52.3 us
  waiting for transfers between devices: 10.2 us -> 15 us
  starting transfers between devices: 19.4 us -> 16.4 us
  Pallas kernels: 18.6 us -> 17.9 us
    ppermute x6, waiting for transfers between devices: 10.2 us -> 13.1 us  [swapped(): lax.ppermute(value, axis, [(source, source ^ bits) for source in range(la...]
    ppermute x2, waiting for transfers between devices: 0.01 us -> 1.9 us  [shifted(): lax.ppermute(value, axis, [(source, (source + steps) % count) for source...]
    ppermute x2, starting transfers between devices: 6.93 us -> 5.37 us  [shifted(): lax.ppermute(value, axis, [(source, (source + steps) % count) for source...]
    ppermute x6, starting transfers between devices: 10.9 us -> 9.44 us  [swapped(): lax.ppermute(value, axis, [(source, source ^ bits) for source in range(la...]
    pallas_call x1, Pallas kernels: 1.42 us -> 0.69 us  [seen_table(): pl.pallas_call(table_kernel, out_shape=jax.ShapeDtypeStruct((1, padded(si...]
  transfers between devices with their start and end apart: 9 -> 9, of which waited for: 3 -> 4; matrix products, arithmetic and copies ran while one was open for 3% -> 3% of each run, Pallas kernels for 34% -> 33%
where the time goes in v8:
time: 51.9 us; the launch traced here: 52.3 us
  Pallas kernels  17.9 us (34%)
  starting transfers between devices  16.4 us (32%)
  waiting for transfers between devices  15 us (29%)
  local copies, waits for them, and re-layouts  2.08 us (4%)
  between operations  0.82 us (2%)
    pallas_call x6, Pallas kernels, cross_part(): pl.pallas_call(functools.partial(cross_kernel, key_count, len(images), of...  13.8 us
    ppermute x6, waiting for transfers between devices, swapped(): lax.ppermute(value, axis, [(source, source ^ bits) for source in range(la...  13.1 us
    ppermute x6, starting transfers between devices, swapped(): lax.ppermute(value, axis, [(source, source ^ bits) for source in range(la...  9.44 us
    ppermute x2, starting transfers between devices, shifted(): lax.ppermute(value, axis, [(source, (source + steps) % count) for source...  5.37 us
    unnamed x12, local copies, waits for them, and re-layouts  1.98 us
    ppermute x2, waiting for transfers between devices, shifted(): lax.ppermute(value, axis, [(source, (source + steps) % count) for source...  1.9 us
    ppermute x1, starting transfers between devices, per_device(): lax.ppermute(cross_queries, 'enc', [(0, 0), (1, 2), (2, 1), (3, 3)])  1.6 us
    pallas_call x3, Pallas kernels, combined(): pl.pallas_call(functools.partial(combine_kernel, held, last), out_shape=o...  1.09 us
  transfers between devices with their start and end apart: 9, of which 4 were waited for; matrix products, arithmetic and copies ran while one was open for 3% of the time, Pallas kernels for 33%

profile of v8, /device:TPU:0, one launch (start us, length us, event | category | flops | bytes accessed | tf_op | source)
XLA Modules:
  0.0 52.3 jit_solution(9632721746944922921)
XLA Ops:
  0.6 3.0 %collective-permute-start.3 = (bf16[1,2,1601,128]{3,1,2,0:T(2,128)(2,1)}, bf16[1,2,1601,128]{3,1,2,0:T(2,128)(2,1)S(1)}, u32[]{:S(2)}, u32[]{:S(2)}) collective-permute-start(bf16[1,2,1601,128]{3,1,2,0:T(2,128)(2,1)} %param.9), channel_id=1, source_target_pairs={{0,16},{16,0},{1,17},{17,1},{2,18},{18,2},{3,19},{19,3},{4,20},{20... | collective-permute-start | bytes 2459144 | tf_op jit(solution)/shard_map/ppermute | solution.py:447
  3.6 2.6 %collective-permute-start.2 = (bf16[512,256]{1,0:T(8,128)(2,1)}, bf16[512,256]{1,0:T(8,128)(2,1)S(1)}, u32[]{:S(2)}, u32[]{:S(2)}) collective-permute-start(bf16[512,256]{1,0:T(8,128)(2,1)} %refs_0_.2), channel_id=1, source_target_pairs={{0,2},{1,3},{2,0},{3,1},{4,6},{5,7},{6,4},{7,5},{8,10},{9,11},{10,... | collective-permute-start | bytes 786440 | tf_op jit(solution)/shard_map/ppermute | solution.py:451
  6.2 1.6 %collective-permute-start.1 = (bf16[512,256]{1,0:T(8,128)(2,1)}, bf16[512,256]{1,0:T(8,128)(2,1)S(1)}, u32[]{:S(2)}, u32[]{:S(2)}) collective-permute-start(bf16[512,256]{1,0:T(8,128)(2,1)} %refs_0_.2), channel_id=1, source_target_pairs={{0,0},{1,2},{2,1},{3,3},{4,4},{5,6},{6,5},{7,7},{8,8},{9,10},{10,9... | collective-permute-start | bytes 786440 | tf_op jit(solution)/shard_map/ppermute | solution.py:475
  7.8 2.0 %collective-permute-start = (bf16[512,256]{1,0:T(8,128)(2,1)}, bf16[512,256]{1,0:T(8,128)(2,1)S(1)}, u32[]{:S(2)}, u32[]{:S(2)}) collective-permute-start(bf16[512,256]{1,0:T(8,128)(2,1)} %refs_0_.2), channel_id=1, source_target_pairs={{0,1},{1,0},{2,3},{3,2},{4,5},{5,4},{6,7},{7,6},{8,9},{9,8},{10,11... | collective-permute-start | bytes 786440 | tf_op jit(solution)/shard_map/ppermute | solution.py:451
  9.8 1.3 %copy.17 = bf16[1,2,1601,128]{3,2,1,0:T(8,128)(2,1)S(1)} copy(bf16[1,2,1601,128]{3,1,2,0:T(2,128)(2,1)} %param.9) | data formatting | bytes 1639424 | tf_op args[3]
  11.0 0.0 copy-start.3
  11.1 0.2 prepare.2.refs_1_.refs_2_
  11.3 0.0 copy-start.1
  11.3 0.0 copy-start.2
  11.3 0.7 %copy-done.1 = s32[4,2]{0,1:T(2,128)S(1)} copy-done((s32[4,2]{0,1:T(2,128)S(1)}, s32[4,2]{0,1:T(2,128)}, u32[]{:S(2)}) %copy-start.1) | copy-done | bytes 56
  11.9 0.0 copy-done.2
  11.9 0.7 %seen_table.1.table_ref = s32[1,128]{1,0:T(1,128)S(1)} custom-call(s32[1]{0:T(128)} %bitcast.position_ref, s32[1]{0:T(128)} %bitcast.1.inside_ref, s32[2,4]{1,0:T(2,128)S(1)} %bitcast.17, s32[2]{0:T(128)S(1)} %copy-done.2), custom_call_target="tpu_custom_call" | custom-call | tf_op jit(solution)/shard_map/seen_table/pallas_call | solution.py:128
  12.6 0.0 copy-done.3
  12.6 0.9 %cross_first.2 = (f32[4,8,256]{2,1,0:T(8,128)S(1)}, f32[4,144,256]{2,1,0:T(8,128)S(1)}) custom-call(s32[1,128]{1,0:T(1,128)S(1)} %seen_table.1.table_ref, bf16[512,256]{1,0:T(8,128)(2,1)S(1)} %copy-done.3, bf16[2,1664,128]{2,1,0:T(8,128)(2,1)S(1)} %prepare.2.refs_1_.refs_2_), custom_call_target="tpu_custom_call" | custom-call | flops 2000000000 | bytes 1024 | tf_op jit(solution)/shard_map/cross_first/pallas_call | solution.py:268
  13.5 5.8 %collective-permute-done.2.refs_0_ = bf16[512,256]{1,0:T(8,128)(2,1)S(1)} collective-permute-done((bf16[512,256]{1,0:T(8,128)(2,1)}, bf16[512,256]{1,0:T(8,128)(2,1)S(1)}, u32[]{:S(2)}, u32[]{:S(2)}) %collective-permute-start.2) | collective-permute-done | bytes 262176 | tf_op jit(solution)/shard_map/ppermute | solution.py:451
  19.3 0.0 collective-permute-start.4
  19.3 0.9 %cross_first.3 = (f32[4,8,256]{2,1,0:T(8,128)S(1)}, f32[4,144,256]{2,1,0:T(8,128)S(1)}) custom-call(s32[1,128]{1,0:T(1,128)S(1)} %seen_table.1.table_ref, bf16[512,256]{1,0:T(8,128)(2,1)S(1)} %collective-permute-done.2.refs_0_, bf16[2,1664,128]{2,1,0:T(8,128)(2,1)S(1)} %prepare.2.refs_1_.refs_2_), custom_call_target="tpu_custom_call" | custom-call | flops 2000000000 | bytes 1024 | tf_op jit(solution)/shard_map/cross_first/pallas_call | solution.py:268
  20.2 1.9 %collective-permute-done.3 = bf16[1,2,1601,128]{3,1,2,0:T(2,128)(2,1)S(1)} collective-permute-done((bf16[1,2,1601,128]{3,1,2,0:T(2,128)(2,1)}, bf16[1,2,1601,128]{3,1,2,0:T(2,128)(2,1)S(1)}, u32[]{:S(2)}, u32[]{:S(2)}) %collective-permute-start.3) | collective-permute-done | bytes 819744 | tf_op jit(solution)/shard_map/ppermute | solution.py:447
  22.1 0.1 copy.16
  22.2 0.2 prepare.3.refs_1_.refs_3_.refs_2_
  22.4 2.9 %cross_last.4 = bf16[528,256]{1,0:T(8,128)(2,1)S(1)} custom-call(s32[1,128]{1,0:T(1,128)S(1)} %seen_table.1.table_ref, bf16[512,256]{1,0:T(8,128)(2,1)S(1)} %collective-permute-done.2.refs_0_, bf16[2,1664,128]{2,1,0:T(8,128)(2,1)S(1)} %prepare.3.refs_1_.refs_3_.refs_2_, f32[4,8,256]{2,1,0:T(8,128)S(1)} %get-tuple-element.25.refs_2_, ...), custom_call_target="tpu_custom_call" | custom-call | flops 2000000000 | bytes 1024 | tf_op jit(solution)/shard_map/cross_last/pallas_call | solution.py:268
  25.4 0.0 copy-start.4
  25.4 2.9 %collective-permute-start.6 = (bf16[528,256]{1,0:T(8,128)(2,1)S(1)}, bf16[528,256]{1,0:T(8,128)(2,1)S(1)}, u32[]{:S(2)}, u32[]{:S(2)}) collective-permute-start(bf16[528,256]{1,0:T(8,128)(2,1)S(1)} %cross_last.4), channel_id=1, source_target_pairs={{0,2},{1,3},{2,0},{3,1},{4,6},{5,7},{6,4},{7,5},{8,10},{9,11},{10,... | collective-permute-start | bytes 811016 | tf_op jit(solution)/shard_map/ppermute | solution.py:451
  28.3 0.0 collective-permute-done.4.refs_1_
  28.3 0.0 collective-permute-done.1.refs_0_
  28.3 3.0 %cross_last.5 = bf16[528,256]{1,0:T(8,128)(2,1)S(1)} custom-call(s32[1,128]{1,0:T(1,128)S(1)} %seen_table.1.table_ref, bf16[512,256]{1,0:T(8,128)(2,1)S(1)} %collective-permute-done.1.refs_0_, bf16[512,256]{1,0:T(8,128)(2,1)S(1)} %collective-permute-done.4.refs_1_, bf16[2,1664,128]{2,1,0:T(8,128)(2,1)S(1)} %prepare.2.refs_1_.refs_2_, ...), custom_call_target="tpu_custom_call" | custom-call | flops 2000000000 | bytes 1024 | tf_op jit(solution)/shard_map/cross_last/pallas_call | solution.py:268
  31.3 1.7 %collective-permute-start.7 = (bf16[528,256]{1,0:T(8,128)(2,1)S(1)}, bf16[528,256]{1,0:T(8,128)(2,1)S(1)}, u32[]{:S(2)}, u32[]{:S(2)}) collective-permute-start(bf16[528,256]{1,0:T(8,128)(2,1)S(1)} %cross_last.5), channel_id=1, source_target_pairs={{0,3},{1,2},{2,1},{3,0},{4,7},{5,6},{6,5},{7,4},{8,11},{9,10},{10,... | collective-permute-start | bytes 811016 | tf_op jit(solution)/shard_map/ppermute | solution.py:451
  33.0 0.0 collective-permute-done.refs_0_
  33.0 0.0 copy-done.4
  33.0 2.4 %collective-permute-start.5 = (bf16[512,256]{1,0:T(8,128)(2,1)S(1)}, bf16[512,256]{1,0:T(8,128)(2,1)S(1)}, u32[]{:S(2)}, u32[]{:S(2)}) collective-permute-start(bf16[512,256]{1,0:T(8,128)(2,1)S(1)} %bitcast.15), channel_id=1, source_target_pairs={{0,16},{16,0},{1,17},{17,1},{2,18},{18,2},{3,19},{19,3},{4,20},{20... | collective-permute-start | bytes 786440 | tf_op jit(solution)/shard_map/ppermute | solution.py:447
  35.4 3.0 %cross_last.6 = bf16[528,256]{1,0:T(8,128)(2,1)S(1)} custom-call(s32[1,128]{1,0:T(1,128)S(1)} %seen_table.1.table_ref, bf16[512,256]{1,0:T(8,128)(2,1)S(1)} %collective-permute-done.refs_0_, bf16[2,1664,128]{2,1,0:T(8,128)(2,1)S(1)} %prepare.2.refs_1_.refs_2_, bf16[2,1664,128]{2,1,0:T(8,128)(2,1)S(1)} %prepare.3.refs_1_.refs_3_.refs_2_), custom_call_target="tpu_custom_call" | custom-call | flops 2000000000 | bytes 1024 | tf_op jit(solution)/shard_map/cross_last/pallas_call | solution.py:268
  38.4 0.0 copy-start
  38.4 0.3 collective-permute-start.8
  38.7 3.1 %cross_last.7.refs_0_ = bf16[528,256]{1,0:T(8,128)(2,1)S(1)} custom-call(s32[1,128]{1,0:T(1,128)S(1)} %seen_table.1.table_ref, bf16[512,256]{1,0:T(8,128)(2,1)S(1)} %copy-done.3, bf16[2,1664,128]{2,1,0:T(8,128)(2,1)S(1)} %prepare.3.refs_1_.refs_3_.refs_2_, f32[4,8,256]{2,1,0:T(8,128)S(1)} %get-tuple-element.22.refs_2_, ...), custom_call_target="tpu_custom_call" | custom-call | flops 2000000000 | bytes 1024 | tf_op jit(solution)/shard_map/cross_last/pallas_call | solution.py:268
  41.8 0.0 copy-done
  41.9 1.1 %self_first.1 = (f32[2,8,512]{2,1,0:T(8,128)S(1)}, f32[2,144,512]{2,1,0:T(8,128)S(1)}) custom-call(bf16[512,256]{1,0:T(8,128)(2,1)S(1)} %copy-done, bf16[512,256]{1,0:T(8,128)(2,1)S(1)} %bitcast.16), custom_call_target="tpu_custom_call" | custom-call | bytes 1024 | tf_op jit(solution)/shard_map/self_first/pallas_call | solution.py:414
  43.0 0.0 collective-permute-done.5.refs_0_
  43.0 0.9 %self_last.1 = bf16[512,256]{1,0:T(8,128)(2,1)} custom-call(s32[1]{0:T(128)} %bitcast.position_ref, bf16[512,256]{1,0:T(8,128)(2,1)S(1)} %copy-done, f32[2,8,512]{2,1,0:T(8,128)S(1)} %get-tuple-element.34.high_ref, f32[2,144,512]{2,1,0:T(8,128)S(1)} %get-tuple-element.35.mixed_ref, bf16[512,256]{1,0:T(8,128)(2,1)S(1)} %collective-permute-done.5.refs_0_), custom_call_target="tpu_custom_call" | custom-call | bytes 1024 | tf_op jit(solution)/shard_map/self_last/pallas_call | solution.py:432
  43.9 2.9 %collective-permute-done.6.refs_1_ = bf16[528,256]{1,0:T(8,128)(2,1)S(1)} collective-permute-done((bf16[528,256]{1,0:T(8,128)(2,1)S(1)}, bf16[528,256]{1,0:T(8,128)(2,1)S(1)}, u32[]{:S(2)}, u32[]{:S(2)}) %collective-permute-start.6) | collective-permute-done | bytes 270368 | tf_op jit(solution)/shard_map/ppermute | solution.py:451
  46.7 0.1 combine.2
  46.9 0.0 collective-permute-done.7.refs_2_
  46.9 0.1 combine.3
  47.0 4.4 %collective-permute-done.8.refs_2_ = bf16[528,256]{1,0:T(8,128)(2,1)S(1)} collective-permute-done((bf16[528,256]{1,0:T(8,128)(2,1)S(1)}, bf16[528,256]{1,0:T(8,128)(2,1)S(1)}, u32[]{:S(2)}, u32[]{:S(2)}) %collective-permute-start.8) | collective-permute-done | bytes 270368 | tf_op jit(solution)/shard_map/ppermute | solution.py:451
  51.4 0.9 %combine_last.1 = bf16[512,256]{1,0:T(8,128)(2,1)} custom-call(f32[512,256]{1,0:T(8,128)S(1)} %get-tuple-element.40.refs_0_, f32[4,256]{1,0:T(4,128)S(1)} %get-tuple-element.41.refs_1_, bf16[528,256]{1,0:T(8,128)(2,1)S(1)} %collective-permute-done.8.refs_2_), custom_call_target="tpu_custom_call" | custom-call | flops 2000000000 | bytes 1024 | tf_op jit(solution)/shard_map/combine_last/pallas_call | solution.py:343
  (1 shorter events, 0.0 us)
Async XLA Ops:
  0.6 21.5 %collective-permute-start.3 = (bf16[1,2,1601,128]{3,1,2,0:T(2,128)(2,1)}, bf16[1,2,1601,128]{3,1,2,0:T(2,128)(2,1)S(1)}, u32[]{:S(2)}, u32[]{:S(2)}) collective-permute-start(bf16[1,2,1601,128]{3,1,2,0:T(2,128)(2,1)} %param.9), channel_id=1, source_target_pairs={{0,16},{16,0},{1,17},{17,1},{2,18},{18,2},{3,19},{19,3},{4,20},{20... | collective-permute-start | bytes 2459144 | tf_op jit(solution)/shard_map/ppermute | solution.py:447
  3.6 15.7 %collective-permute-start.2 = (bf16[512,256]{1,0:T(8,128)(2,1)}, bf16[512,256]{1,0:T(8,128)(2,1)S(1)}, u32[]{:S(2)}, u32[]{:S(2)}) collective-permute-start(bf16[512,256]{1,0:T(8,128)(2,1)} %refs_0_.2), channel_id=1, source_target_pairs={{0,2},{1,3},{2,0},{3,1},{4,6},{5,7},{6,4},{7,5},{8,10},{9,11},{10,... | collective-permute-start | bytes 786440 | tf_op jit(solution)/shard_map/ppermute | solution.py:451
  6.2 22.1 %collective-permute-start.1 = (bf16[512,256]{1,0:T(8,128)(2,1)}, bf16[512,256]{1,0:T(8,128)(2,1)S(1)}, u32[]{:S(2)}, u32[]{:S(2)}) collective-permute-start(bf16[512,256]{1,0:T(8,128)(2,1)} %refs_0_.2), channel_id=1, source_target_pairs={{0,0},{1,2},{2,1},{3,3},{4,4},{5,6},{6,5},{7,7},{8,8},{9,10},{10,9... | collective-permute-start | bytes 786440 | tf_op jit(solution)/shard_map/ppermute | solution.py:475
  7.8 25.2 %collective-permute-start = (bf16[512,256]{1,0:T(8,128)(2,1)}, bf16[512,256]{1,0:T(8,128)(2,1)S(1)}, u32[]{:S(2)}, u32[]{:S(2)}) collective-permute-start(bf16[512,256]{1,0:T(8,128)(2,1)} %refs_0_.2), channel_id=1, source_target_pairs={{0,1},{1,0},{2,3},{3,2},{4,5},{5,4},{6,7},{7,6},{8,9},{9,8},{10,11... | collective-permute-start | bytes 786440 | tf_op jit(solution)/shard_map/ppermute | solution.py:451
  11.0 1.6 %copy-start.3 = (bf16[512,256]{1,0:T(8,128)(2,1)S(1)}, bf16[512,256]{1,0:T(8,128)(2,1)}, u32[]{:S(2)}) copy-start(bf16[512,256]{1,0:T(8,128)(2,1)} %refs_0_.2) | copy-start | bytes 786436
  11.3 0.7 %copy-start.1 = (s32[4,2]{0,1:T(2,128)S(1)}, s32[4,2]{0,1:T(2,128)}, u32[]{:S(2)}) copy-start(s32[4,2]{0,1:T(2,128)} %param.10) | copy-start | bytes 100
  11.3 0.7 %copy-start.2 = (s32[2]{0:T(128)S(1)}, s32[2]{0:T(128)}, u32[]{:S(2)}) copy-start(s32[2]{0:T(128)} %owner_ref.1) | copy-start | bytes 28
  19.3 8.9 %collective-permute-start.4 = (bf16[512,256]{1,0:T(8,128)(2,1)S(1)}, bf16[512,256]{1,0:T(8,128)(2,1)S(1)}, u32[]{:S(2)}, u32[]{:S(2)}) collective-permute-start(bf16[512,256]{1,0:T(8,128)(2,1)S(1)} %collective-permute-done.2.refs_0_), channel_id=1, source_target_pairs={{0,1},{1,0},{2,3},{3,2},{4,5},{5,4},{6,7},{7,6},{8,9},{9,8},{10,11... | collective-permute-start | bytes 786440 | tf_op jit(solution)/shard_map/ppermute | solution.py:451
  25.4 7.6 %copy-start.4 = (bf16[512,2,128]{2,1,0:T(2,128)(2,1)S(1)}, bf16[512,2,128]{2,1,0:T(2,128)(2,1)}, u32[]{:S(2)}) copy-start(bf16[512,2,128]{2,1,0:T(2,128)(2,1)} %param.7) | copy-start | bytes 786436
  25.4 21.4 %collective-permute-start.6 = (bf16[528,256]{1,0:T(8,128)(2,1)S(1)}, bf16[528,256]{1,0:T(8,128)(2,1)S(1)}, u32[]{:S(2)}, u32[]{:S(2)}) collective-permute-start(bf16[528,256]{1,0:T(8,128)(2,1)S(1)} %cross_last.4), channel_id=1, source_target_pairs={{0,2},{1,3},{2,0},{3,1},{4,6},{5,7},{6,4},{7,5},{8,10},{9,11},{10,... | collective-permute-start | bytes 811016 | tf_op jit(solution)/shard_map/ppermute | solution.py:451
  31.3 15.5 %collective-permute-start.7 = (bf16[528,256]{1,0:T(8,128)(2,1)S(1)}, bf16[528,256]{1,0:T(8,128)(2,1)S(1)}, u32[]{:S(2)}, u32[]{:S(2)}) collective-permute-start(bf16[528,256]{1,0:T(8,128)(2,1)S(1)} %cross_last.5), channel_id=1, source_target_pairs={{0,3},{1,2},{2,1},{3,0},{4,7},{5,6},{6,5},{7,4},{8,11},{9,10},{10,... | collective-permute-start | bytes 811016 | tf_op jit(solution)/shard_map/ppermute | solution.py:451
  33.0 9.9 %collective-permute-start.5 = (bf16[512,256]{1,0:T(8,128)(2,1)S(1)}, bf16[512,256]{1,0:T(8,128)(2,1)S(1)}, u32[]{:S(2)}, u32[]{:S(2)}) collective-permute-start(bf16[512,256]{1,0:T(8,128)(2,1)S(1)} %bitcast.15), channel_id=1, source_target_pairs={{0,16},{16,0},{1,17},{17,1},{2,18},{18,2},{3,19},{19,3},{4,20},{20... | collective-permute-start | bytes 786440 | tf_op jit(solution)/shard_map/ppermute | solution.py:447
  38.4 3.5 %copy-start = (bf16[512,256]{1,0:T(8,128)(2,1)S(1)}, bf16[512,256]{1,0:T(8,128)(2,1)}, u32[]{:S(2)}) copy-start(bf16[512,256]{1,0:T(8,128)(2,1)} %q_ref.1) | copy-start | bytes 786436
  38.4 13.0 %collective-permute-start.8 = (bf16[528,256]{1,0:T(8,128)(2,1)S(1)}, bf16[528,256]{1,0:T(8,128)(2,1)S(1)}, u32[]{:S(2)}, u32[]{:S(2)}) collective-permute-start(bf16[528,256]{1,0:T(8,128)(2,1)S(1)} %cross_last.6), channel_id=1, source_target_pairs={{0,1},{1,0},{2,3},{3,2},{4,5},{5,4},{6,7},{7,6},{8,9},{9,8},{10,11... | collective-permute-start | bytes 811016 | tf_op jit(solution)/shard_map/ppermute | solution.py:451

commit v9 on v8

--- a/solution.py
+++ b/solution.py
@@ -137,8 +137,9 @@
 
 
 def chunks_of(width):
-    half = width // LANES // 2 * LANES
-    return [(0, half), (half, width)] if half else [(0, width)]
+    tiles = width // LANES
+    cuts = sorted({tiles * index // 3 * LANES for index in range(3)} | {width})
+    return list(zip(cuts, cuts[1:]))
 
 
 def cross_kernel(key_count, pieces, offset, last, parts, table_ref, *refs):

time: 51.9 us -> 52.3 us (level)
  Pallas kernels: 17.9 us -> 21.7 us
  waiting for transfers between devices: 15 us -> 11.2 us
    pallas_call x6, Pallas kernels: 13.8 us -> 17.6 us  [cross_part(): pl.pallas_call(functools.partial(cross_kernel, key_count, len(images), of...]
    ppermute x6, waiting for transfers between devices: 13.1 us -> 10.3 us  [swapped(): lax.ppermute(value, axis, [(source, source ^ bits) for source in range(la...]
    ppermute x2, waiting for transfers between devices: 1.9 us -> 0.88 us  [shifted(): lax.ppermute(value, axis, [(source, (source + steps) % count) for source...]
  transfers between devices with their start and end apart: 9 -> 9, of which waited for: 4 -> 4; matrix products, arithmetic and copies ran while one was open for 3% -> 3% of each run, Pallas kernels for 33% -> 40%
where the time goes in v9:
time: 52.3 us; the launch traced here: 52.2 us
  Pallas kernels  21.7 us (41%)
  starting transfers between devices  16.4 us (31%)
  waiting for transfers between devices  11.2 us (21%)
  local copies, waits for them, and re-layouts  2.08 us (4%)
  between operations  0.82 us (2%)
    pallas_call x6, Pallas kernels, cross_part(): pl.pallas_call(functools.partial(cross_kernel, key_count, len(images), of...  17.6 us
    ppermute x6, waiting for transfers between devices, swapped(): lax.ppermute(value, axis, [(source, source ^ bits) for source in range(la...  10.3 us
    ppermute x6, starting transfers between devices, swapped(): lax.ppermute(value, axis, [(source, source ^ bits) for source in range(la...  9.52 us
    ppermute x2, starting transfers between devices, shifted(): lax.ppermute(value, axis, [(source, (source + steps) % count) for source...  5.26 us
    unnamed x12, local copies, waits for them, and re-layouts  1.98 us
    ppermute x1, starting transfers between devices, per_device(): lax.ppermute(cross_queries, 'enc', [(0, 0), (1, 2), (2, 1), (3, 3)])  1.6 us
    pallas_call x3, Pallas kernels, combined(): pl.pallas_call(functools.partial(combine_kernel, held, last), out_shape=o...  1.09 us
    pallas_call x1, Pallas kernels, self_first(): pl.pallas_call(functools.partial(self_first_kernel, group), out_shape=(ja...  1.09 us
  transfers between devices with their start and end apart: 9, of which 4 were waited for; matrix products, arithmetic and copies ran while one was open for 3% of the time, Pallas kernels for 40%

profile of v9, /device:TPU:0, one launch (start us, length us, event | category | flops | bytes accessed | tf_op | source)
XLA Modules:
  0.0 52.2 jit_solution(7662830238431885918)
XLA Ops:
  0.6 3.0 %collective-permute-start.3 = (bf16[1,2,1601,128]{3,1,2,0:T(2,128)(2,1)}, bf16[1,2,1601,128]{3,1,2,0:T(2,128)(2,1)S(1)}, u32[]{:S(2)}, u32[]{:S(2)}) collective-permute-start(bf16[1,2,1601,128]{3,1,2,0:T(2,128)(2,1)} %param.9), channel_id=1, source_target_pairs={{0,16},{16,0},{1,17},{17,1},{2,18},{18,2},{3,19},{19,3},{4,20},{20... | collective-permute-start | bytes 2459144 | tf_op jit(solution)/shard_map/ppermute | solution.py:448
  3.6 2.6 %collective-permute-start.2 = (bf16[512,256]{1,0:T(8,128)(2,1)}, bf16[512,256]{1,0:T(8,128)(2,1)S(1)}, u32[]{:S(2)}, u32[]{:S(2)}) collective-permute-start(bf16[512,256]{1,0:T(8,128)(2,1)} %refs_0_.2), channel_id=1, source_target_pairs={{0,2},{1,3},{2,0},{3,1},{4,6},{5,7},{6,4},{7,5},{8,10},{9,11},{10,... | collective-permute-start | bytes 786440 | tf_op jit(solution)/shard_map/ppermute | solution.py:452
  6.2 1.6 %collective-permute-start.1 = (bf16[512,256]{1,0:T(8,128)(2,1)}, bf16[512,256]{1,0:T(8,128)(2,1)S(1)}, u32[]{:S(2)}, u32[]{:S(2)}) collective-permute-start(bf16[512,256]{1,0:T(8,128)(2,1)} %refs_0_.2), channel_id=1, source_target_pairs={{0,0},{1,2},{2,1},{3,3},{4,4},{5,6},{6,5},{7,7},{8,8},{9,10},{10,9... | collective-permute-start | bytes 786440 | tf_op jit(solution)/shard_map/ppermute | solution.py:476
  7.8 2.0 %collective-permute-start = (bf16[512,256]{1,0:T(8,128)(2,1)}, bf16[512,256]{1,0:T(8,128)(2,1)S(1)}, u32[]{:S(2)}, u32[]{:S(2)}) collective-permute-start(bf16[512,256]{1,0:T(8,128)(2,1)} %refs_0_.2), channel_id=1, source_target_pairs={{0,1},{1,0},{2,3},{3,2},{4,5},{5,4},{6,7},{7,6},{8,9},{9,8},{10,11... | collective-permute-start | bytes 786440 | tf_op jit(solution)/shard_map/ppermute | solution.py:452
  9.8 1.3 %copy.17 = bf16[1,2,1601,128]{3,2,1,0:T(8,128)(2,1)S(1)} copy(bf16[1,2,1601,128]{3,1,2,0:T(2,128)(2,1)} %param.9) | data formatting | bytes 1639424 | tf_op args[3]
  11.0 0.0 copy-start.3
  11.1 0.2 prepare.2.refs_1_.refs_2_
  11.3 0.0 copy-start.1
  11.3 0.0 copy-start.2
  11.3 0.7 %copy-done.1 = s32[4,2]{0,1:T(2,128)S(1)} copy-done((s32[4,2]{0,1:T(2,128)S(1)}, s32[4,2]{0,1:T(2,128)}, u32[]{:S(2)}) %copy-start.1) | copy-done | bytes 56
  11.9 0.0 copy-done.2
  11.9 0.7 %seen_table.1.table_ref = s32[1,128]{1,0:T(1,128)S(1)} custom-call(s32[1]{0:T(128)} %bitcast.position_ref, s32[1]{0:T(128)} %bitcast.1.inside_ref, s32[2,4]{1,0:T(2,128)S(1)} %bitcast.17, s32[2]{0:T(128)S(1)} %copy-done.2), custom_call_target="tpu_custom_call" | custom-call | tf_op jit(solution)/shard_map/seen_table/pallas_call | solution.py:128
  12.6 0.0 copy-done.3
  12.6 1.9 %cross_first.2 = (f32[4,8,256]{2,1,0:T(8,128)S(1)}, f32[4,144,256]{2,1,0:T(8,128)S(1)}) custom-call(s32[1,128]{1,0:T(1,128)S(1)} %seen_table.1.table_ref, bf16[512,256]{1,0:T(8,128)(2,1)S(1)} %copy-done.3, bf16[2,1664,128]{2,1,0:T(8,128)(2,1)S(1)} %prepare.2.refs_1_.refs_2_), custom_call_target="tpu_custom_call" | custom-call | flops 2000000000 | bytes 1024 | tf_op jit(solution)/shard_map/cross_first/pallas_call | solution.py:269
  14.5 4.8 %collective-permute-done.2.refs_0_ = bf16[512,256]{1,0:T(8,128)(2,1)S(1)} collective-permute-done((bf16[512,256]{1,0:T(8,128)(2,1)}, bf16[512,256]{1,0:T(8,128)(2,1)S(1)}, u32[]{:S(2)}, u32[]{:S(2)}) %collective-permute-start.2) | collective-permute-done | bytes 262176 | tf_op jit(solution)/shard_map/ppermute | solution.py:452
  19.3 0.0 collective-permute-start.4
  19.3 1.9 %cross_first.3 = (f32[4,8,256]{2,1,0:T(8,128)S(1)}, f32[4,144,256]{2,1,0:T(8,128)S(1)}) custom-call(s32[1,128]{1,0:T(1,128)S(1)} %seen_table.1.table_ref, bf16[512,256]{1,0:T(8,128)(2,1)S(1)} %collective-permute-done.2.refs_0_, bf16[2,1664,128]{2,1,0:T(8,128)(2,1)S(1)} %prepare.2.refs_1_.refs_2_), custom_call_target="tpu_custom_call" | custom-call | flops 2000000000 | bytes 1024 | tf_op jit(solution)/shard_map/cross_first/pallas_call | solution.py:269
  21.2 0.9 %collective-permute-done.3 = bf16[1,2,1601,128]{3,1,2,0:T(2,128)(2,1)S(1)} collective-permute-done((bf16[1,2,1601,128]{3,1,2,0:T(2,128)(2,1)}, bf16[1,2,1601,128]{3,1,2,0:T(2,128)(2,1)S(1)}, u32[]{:S(2)}, u32[]{:S(2)}) %collective-permute-start.3) | collective-permute-done | bytes 819744 | tf_op jit(solution)/shard_map/ppermute | solution.py:448
  22.1 0.1 copy.16
  22.2 0.2 prepare.3.refs_1_.refs_3_.refs_2_
  22.4 2.9 %cross_last.4 = bf16[528,256]{1,0:T(8,128)(2,1)S(1)} custom-call(s32[1,128]{1,0:T(1,128)S(1)} %seen_table.1.table_ref, bf16[512,256]{1,0:T(8,128)(2,1)S(1)} %collective-permute-done.2.refs_0_, bf16[2,1664,128]{2,1,0:T(8,128)(2,1)S(1)} %prepare.3.refs_1_.refs_3_.refs_2_, f32[4,8,256]{2,1,0:T(8,128)S(1)} %get-tuple-element.25.refs_2_, ...), custom_call_target="tpu_custom_call" | custom-call | flops 2000000000 | bytes 1024 | tf_op jit(solution)/shard_map/cross_last/pallas_call | solution.py:269
  25.3 0.0 copy-start.4
  25.3 2.9 %collective-permute-start.6 = (bf16[528,256]{1,0:T(8,128)(2,1)S(1)}, bf16[528,256]{1,0:T(8,128)(2,1)S(1)}, u32[]{:S(2)}, u32[]{:S(2)}) collective-permute-start(bf16[528,256]{1,0:T(8,128)(2,1)S(1)} %cross_last.4), channel_id=1, source_target_pairs={{0,2},{1,3},{2,0},{3,1},{4,6},{5,7},{6,4},{7,5},{8,10},{9,11},{10,... | collective-permute-start | bytes 811016 | tf_op jit(solution)/shard_map/ppermute | solution.py:452
  28.2 0.0 collective-permute-done.4.refs_1_
  28.2 0.0 collective-permute-done.1.refs_0_
  28.2 4.0 %cross_last.5 = bf16[528,256]{1,0:T(8,128)(2,1)S(1)} custom-call(s32[1,128]{1,0:T(1,128)S(1)} %seen_table.1.table_ref, bf16[512,256]{1,0:T(8,128)(2,1)S(1)} %collective-permute-done.1.refs_0_, bf16[512,256]{1,0:T(8,128)(2,1)S(1)} %collective-permute-done.4.refs_1_, bf16[2,1664,128]{2,1,0:T(8,128)(2,1)S(1)} %prepare.2.refs_1_.refs_2_, ...), custom_call_target="tpu_custom_call" | custom-call | flops 2000000000 | bytes 1024 | tf_op jit(solution)/shard_map/cross_last/pallas_call | solution.py:269
  32.2 1.7 %collective-permute-start.7 = (bf16[528,256]{1,0:T(8,128)(2,1)S(1)}, bf16[528,256]{1,0:T(8,128)(2,1)S(1)}, u32[]{:S(2)}, u32[]{:S(2)}) collective-permute-start(bf16[528,256]{1,0:T(8,128)(2,1)S(1)} %cross_last.5), channel_id=1, source_target_pairs={{0,3},{1,2},{2,1},{3,0},{4,7},{5,6},{6,5},{7,4},{8,11},{9,10},{10,... | collective-permute-start | bytes 811016 | tf_op jit(solution)/shard_map/ppermute | solution.py:452
  33.9 0.0 collective-permute-done.refs_0_
  33.9 0.0 copy-done.4
  34.0 2.3 %collective-permute-start.5 = (bf16[512,256]{1,0:T(8,128)(2,1)S(1)}, bf16[512,256]{1,0:T(8,128)(2,1)S(1)}, u32[]{:S(2)}, u32[]{:S(2)}) collective-permute-start(bf16[512,256]{1,0:T(8,128)(2,1)S(1)} %bitcast.15), channel_id=1, source_target_pairs={{0,16},{16,0},{1,17},{17,1},{2,18},{18,2},{3,19},{19,3},{4,20},{20... | collective-permute-start | bytes 786440 | tf_op jit(solution)/shard_map/ppermute | solution.py:448
  36.2 3.9 %cross_last.6 = bf16[528,256]{1,0:T(8,128)(2,1)S(1)} custom-call(s32[1,128]{1,0:T(1,128)S(1)} %seen_table.1.table_ref, bf16[512,256]{1,0:T(8,128)(2,1)S(1)} %collective-permute-done.refs_0_, bf16[2,1664,128]{2,1,0:T(8,128)(2,1)S(1)} %prepare.2.refs_1_.refs_2_, bf16[2,1664,128]{2,1,0:T(8,128)(2,1)S(1)} %prepare.3.refs_1_.refs_3_.refs_2_), custom_call_target="tpu_custom_call" | custom-call | flops 2000000000 | bytes 1024 | tf_op jit(solution)/shard_map/cross_last/pallas_call | solution.py:269
  40.2 0.0 copy-start
  40.2 0.3 collective-permute-start.8
  40.5 3.1 %cross_last.7.refs_0_ = bf16[528,256]{1,0:T(8,128)(2,1)S(1)} custom-call(s32[1,128]{1,0:T(1,128)S(1)} %seen_table.1.table_ref, bf16[512,256]{1,0:T(8,128)(2,1)S(1)} %copy-done.3, bf16[2,1664,128]{2,1,0:T(8,128)(2,1)S(1)} %prepare.3.refs_1_.refs_3_.refs_2_, f32[4,8,256]{2,1,0:T(8,128)S(1)} %get-tuple-element.22.refs_2_, ...), custom_call_target="tpu_custom_call" | custom-call | flops 2000000000 | bytes 1024 | tf_op jit(solution)/shard_map/cross_last/pallas_call | solution.py:269
  43.6 0.0 copy-done
  43.6 1.1 %self_first.1 = (f32[2,8,512]{2,1,0:T(8,128)S(1)}, f32[2,144,512]{2,1,0:T(8,128)S(1)}) custom-call(bf16[512,256]{1,0:T(8,128)(2,1)S(1)} %copy-done, bf16[512,256]{1,0:T(8,128)(2,1)S(1)} %bitcast.16), custom_call_target="tpu_custom_call" | custom-call | bytes 1024 | tf_op jit(solution)/shard_map/self_first/pallas_call | solution.py:415
  44.7 0.0 collective-permute-done.5.refs_0_
  44.7 0.9 %self_last.1 = bf16[512,256]{1,0:T(8,128)(2,1)} custom-call(s32[1]{0:T(128)} %bitcast.position_ref, bf16[512,256]{1,0:T(8,128)(2,1)S(1)} %copy-done, f32[2,8,512]{2,1,0:T(8,128)S(1)} %get-tuple-element.34.high_ref, f32[2,144,512]{2,1,0:T(8,128)S(1)} %get-tuple-element.35.mixed_ref, bf16[512,256]{1,0:T(8,128)(2,1)S(1)} %collective-permute-done.5.refs_0_), custom_call_target="tpu_custom_call" | custom-call | bytes 1024 | tf_op jit(solution)/shard_map/self_last/pallas_call | solution.py:433
  45.6 1.1 %collective-permute-done.6.refs_1_ = bf16[528,256]{1,0:T(8,128)(2,1)S(1)} collective-permute-done((bf16[528,256]{1,0:T(8,128)(2,1)S(1)}, bf16[528,256]{1,0:T(8,128)(2,1)S(1)}, u32[]{:S(2)}, u32[]{:S(2)}) %collective-permute-start.6) | collective-permute-done | bytes 270368 | tf_op jit(solution)/shard_map/ppermute | solution.py:452
  46.7 0.1 combine.2
  46.8 0.0 collective-permute-done.7.refs_2_
  46.8 0.1 combine.3
  46.9 4.4 %collective-permute-done.8.refs_2_ = bf16[528,256]{1,0:T(8,128)(2,1)S(1)} collective-permute-done((bf16[528,256]{1,0:T(8,128)(2,1)S(1)}, bf16[528,256]{1,0:T(8,128)(2,1)S(1)}, u32[]{:S(2)}, u32[]{:S(2)}) %collective-permute-start.8) | collective-permute-done | bytes 270368 | tf_op jit(solution)/shard_map/ppermute | solution.py:452
  51.3 0.9 %combine_last.1 = bf16[512,256]{1,0:T(8,128)(2,1)} custom-call(f32[512,256]{1,0:T(8,128)S(1)} %get-tuple-element.40.refs_0_, f32[4,256]{1,0:T(4,128)S(1)} %get-tuple-element.41.refs_1_, bf16[528,256]{1,0:T(8,128)(2,1)S(1)} %collective-permute-done.8.refs_2_), custom_call_target="tpu_custom_call" | custom-call | flops 2000000000 | bytes 1024 | tf_op jit(solution)/shard_map/combine_last/pallas_call | solution.py:344
  (1 shorter events, 0.0 us)
Async XLA Ops:
  0.6 21.5 %collective-permute-start.3 = (bf16[1,2,1601,128]{3,1,2,0:T(2,128)(2,1)}, bf16[1,2,1601,128]{3,1,2,0:T(2,128)(2,1)S(1)}, u32[]{:S(2)}, u32[]{:S(2)}) collective-permute-start(bf16[1,2,1601,128]{3,1,2,0:T(2,128)(2,1)} %param.9), channel_id=1, source_target_pairs={{0,16},{16,0},{1,17},{17,1},{2,18},{18,2},{3,19},{19,3},{4,20},{20... | collective-permute-start | bytes 2459144 | tf_op jit(solution)/shard_map/ppermute | solution.py:448
  3.6 15.7 %collective-permute-start.2 = (bf16[512,256]{1,0:T(8,128)(2,1)}, bf16[512,256]{1,0:T(8,128)(2,1)S(1)}, u32[]{:S(2)}, u32[]{:S(2)}) collective-permute-start(bf16[512,256]{1,0:T(8,128)(2,1)} %refs_0_.2), channel_id=1, source_target_pairs={{0,2},{1,3},{2,0},{3,1},{4,6},{5,7},{6,4},{7,5},{8,10},{9,11},{10,... | collective-permute-start | bytes 786440 | tf_op jit(solution)/shard_map/ppermute | solution.py:452
  6.2 22.0 %collective-permute-start.1 = (bf16[512,256]{1,0:T(8,128)(2,1)}, bf16[512,256]{1,0:T(8,128)(2,1)S(1)}, u32[]{:S(2)}, u32[]{:S(2)}) collective-permute-start(bf16[512,256]{1,0:T(8,128)(2,1)} %refs_0_.2), channel_id=1, source_target_pairs={{0,0},{1,2},{2,1},{3,3},{4,4},{5,6},{6,5},{7,7},{8,8},{9,10},{10,9... | collective-permute-start | bytes 786440 | tf_op jit(solution)/shard_map/ppermute | solution.py:476
  7.8 26.1 %collective-permute-start = (bf16[512,256]{1,0:T(8,128)(2,1)}, bf16[512,256]{1,0:T(8,128)(2,1)S(1)}, u32[]{:S(2)}, u32[]{:S(2)}) collective-permute-start(bf16[512,256]{1,0:T(8,128)(2,1)} %refs_0_.2), channel_id=1, source_target_pairs={{0,1},{1,0},{2,3},{3,2},{4,5},{5,4},{6,7},{7,6},{8,9},{9,8},{10,11... | collective-permute-start | bytes 786440 | tf_op jit(solution)/shard_map/ppermute | solution.py:452
  11.0 1.6 %copy-start.3 = (bf16[512,256]{1,0:T(8,128)(2,1)S(1)}, bf16[512,256]{1,0:T(8,128)(2,1)}, u32[]{:S(2)}) copy-start(bf16[512,256]{1,0:T(8,128)(2,1)} %refs_0_.2) | copy-start | bytes 786436
  11.3 0.7 %copy-start.1 = (s32[4,2]{0,1:T(2,128)S(1)}, s32[4,2]{0,1:T(2,128)}, u32[]{:S(2)}) copy-start(s32[4,2]{0,1:T(2,128)} %param.10) | copy-start | bytes 100
  11.3 0.7 %copy-start.2 = (s32[2]{0:T(128)S(1)}, s32[2]{0:T(128)}, u32[]{:S(2)}) copy-start(s32[2]{0:T(128)} %owner_ref.1) | copy-start | bytes 28
  19.3 8.9 %collective-permute-start.4 = (bf16[512,256]{1,0:T(8,128)(2,1)S(1)}, bf16[512,256]{1,0:T(8,128)(2,1)S(1)}, u32[]{:S(2)}, u32[]{:S(2)}) collective-permute-start(bf16[512,256]{1,0:T(8,128)(2,1)S(1)} %collective-permute-done.2.refs_0_), channel_id=1, source_target_pairs={{0,1},{1,0},{2,3},{3,2},{4,5},{5,4},{6,7},{7,6},{8,9},{9,8},{10,11... | collective-permute-start | bytes 786440 | tf_op jit(solution)/shard_map/ppermute | solution.py:452
  25.3 8.6 %copy-start.4 = (bf16[512,2,128]{2,1,0:T(2,128)(2,1)S(1)}, bf16[512,2,128]{2,1,0:T(2,128)(2,1)}, u32[]{:S(2)}) copy-start(bf16[512,2,128]{2,1,0:T(2,128)(2,1)} %param.7) | copy-start | bytes 786436
  25.3 21.4 %collective-permute-start.6 = (bf16[528,256]{1,0:T(8,128)(2,1)S(1)}, bf16[528,256]{1,0:T(8,128)(2,1)S(1)}, u32[]{:S(2)}, u32[]{:S(2)}) collective-permute-start(bf16[528,256]{1,0:T(8,128)(2,1)S(1)} %cross_last.4), channel_id=1, source_target_pairs={{0,2},{1,3},{2,0},{3,1},{4,6},{5,7},{6,4},{7,5},{8,10},{9,11},{10,... | collective-permute-start | bytes 811016 | tf_op jit(solution)/shard_map/ppermute | solution.py:452
  32.2 14.6 %collective-permute-start.7 = (bf16[528,256]{1,0:T(8,128)(2,1)S(1)}, bf16[528,256]{1,0:T(8,128)(2,1)S(1)}, u32[]{:S(2)}, u32[]{:S(2)}) collective-permute-start(bf16[528,256]{1,0:T(8,128)(2,1)S(1)} %cross_last.5), channel_id=1, source_target_pairs={{0,3},{1,2},{2,1},{3,0},{4,7},{5,6},{6,5},{7,4},{8,11},{9,10},{10,... | collective-permute-start | bytes 811016 | tf_op jit(solution)/shard_map/ppermute | solution.py:452
  34.0 10.7 %collective-permute-start.5 = (bf16[512,256]{1,0:T(8,128)(2,1)S(1)}, bf16[512,256]{1,0:T(8,128)(2,1)S(1)}, u32[]{:S(2)}, u32[]{:S(2)}) collective-permute-start(bf16[512,256]{1,0:T(8,128)(2,1)S(1)} %bitcast.15), channel_id=1, source_target_pairs={{0,16},{16,0},{1,17},{17,1},{2,18},{18,2},{3,19},{19,3},{4,20},{20... | collective-permute-start | bytes 786440 | tf_op jit(solution)/shard_map/ppermute | solution.py:448
  40.2 3.4 %copy-start = (bf16[512,256]{1,0:T(8,128)(2,1)S(1)}, bf16[512,256]{1,0:T(8,128)(2,1)}, u32[]{:S(2)}) copy-start(bf16[512,256]{1,0:T(8,128)(2,1)} %q_ref.1) | copy-start | bytes 786436
  40.2 11.1 %collective-permute-start.8 = (bf16[528,256]{1,0:T(8,128)(2,1)S(1)}, bf16[528,256]{1,0:T(8,128)(2,1)S(1)}, u32[]{:S(2)}, u32[]{:S(2)}) collective-permute-start(bf16[528,256]{1,0:T(8,128)(2,1)S(1)} %cross_last.6), channel_id=1, source_target_pairs={{0,1},{1,0},{2,3},{3,2},{4,5},{5,4},{6,7},{7,6},{8,9},{9,8},{10,11... | collective-permute-start | bytes 811016 | tf_op jit(solution)/shard_map/ppermute | solution.py:452
